TPU v7x, 32 devices: a whole 2x2x4 slice. The times are simulated.
32 devices in a mesh: dp: 8 (over y, x, core), tensor: 4 (over z).
Axes of the slice: x: 2, y: 2, z: 4, core: 2. Of those that a mesh axis runs over, the one named last changes fastest.
Arguments:
- image_in: bfloat16 [2, 4, 1024, 1536], P(None, 'tensor', 'dp'), may hold values from -6 to 6
- text_in: bfloat16 [2, 4, 160, 1536], P(None, 'tensor', 'dp'), may hold values from -6 to 6
- cond_table: float32 [8, 1536], replicated, may hold values from -6 to 6
- cond_index: int32 [2, 4], replicated, may hold values from 0 to 7
- w_mod: bfloat16 [2, 2, 1536, 9216], P(None, None, 'dp', 'tensor'), may hold values from -0.21875 to 0.21875
- w_qkv: bfloat16 [2, 2, 3, 1536, 1536], P(None, None, None, 'dp', 'tensor'), may hold values from -0.15625 to 0.15625
- w_out: bfloat16 [2, 2, 1536, 1536], P(None, None, 'tensor', 'dp'), may hold values from -0.875 to 0.875
- w_up: bfloat16 [2, 2, 1536, 6144], P(None, None, 'dp', 'tensor'), may hold values from -0.15625 to 0.15625
- w_down: bfloat16 [2, 2, 6144, 1536], P(None, None, 'tensor', 'dp'), may hold values from -0.078125 to 0.078125
- cot_image: bfloat16 [2, 4, 1024, 1536], P(None, 'tensor', 'dp'), may hold values from -6 to 6
- cot_text: bfloat16 [2, 4, 160, 1536], P(None, 'tensor', 'dp'), may hold values from -6 to 6
Outputs:
- image_out: bfloat16 [2, 4, 1024, 1536], P(None, 'tensor', 'dp')
- text_out: bfloat16 [2, 4, 160, 1536], P(None, 'tensor', 'dp')
- grad_image: float32 [2, 4, 1024, 1536], P(None, 'tensor', 'dp')
- grad_text: float32 [2, 4, 160, 1536], P(None, 'tensor', 'dp')
- grad_cond: float32 [8, 1536], P(None, 'dp')
- grad_w_mod: float32 [2, 2, 1536, 9216], P(None, None, 'dp', 'tensor')
- grad_w_qkv: float32 [2, 2, 3, 1536, 1536], P(None, None, None, 'dp', 'tensor')
- grad_w_out: float32 [2, 2, 1536, 1536], P(None, None, 'tensor', 'dp')
- grad_w_up: float32 [2, 2, 1536, 6144], P(None, None, 'dp', 'tensor')
- grad_w_down: float32 [2, 2, 6144, 1536], P(None, None, 'tensor', 'dp')
All inputs are finite; a program needn't handle non-finite values.
Results may differ from a plain program's by a relative error of at most 0.029.
Values may be sent and summed in bfloat16 or wider, within the bound.
No kernel may reach another device: no remote copies, remote signals or barrier semaphores. Data moves between devices by JAX's collectives and lax.ppermute only.
A program may use at most 512 MiB of HBM per device.

v0:
```python
import jax
import jax.numpy as jnp
from jax import lax
from jax.sharding import PartitionSpec as P

HDIM = 64


EPS = 1e-06
HIGHEST = lax.Precision.HIGHEST


def shortened(array):
    return jax.tree.map(lambda a: a.astype(jnp.bfloat16) if a.dtype == jnp.float32 else a, array)


def modulate(values_in, shift_row, scale_row):
    centre = jnp.mean(values_in, axis=-1, keepdims=True)
    offsets = values_in - centre
    spread = jnp.mean(offsets * offsets, axis=-1, keepdims=True)
    return offsets * lax.rsqrt(spread + EPS) * (1.0 + scale_row) + shift_row


def gelu_tanh(values_in):
    return jax.nn.gelu(values_in, approximate=True)


def split_heads(values_in):
    return values_in.reshape(
        values_in.shape[0], values_in.shape[1], values_in.shape[2] // HDIM, HDIM
    )


def attend(queries, all_keys):
    scores = jnp.einsum(
        "sqhe,skhe->shqk",
        split_heads(queries),
        split_heads(all_keys),
        preferred_element_type=jnp.float32,
    )
    return scores * HDIM ** (-0.5)


def fetch_weights(w_qkv, w_out, w_up, w_down, layer_at):
    return (
        lax.all_gather(w_qkv[layer_at], "dp", axis=2, tiled=True),
        lax.all_gather(w_out[layer_at], "dp", axis=2, tiled=True),
        lax.all_gather(w_up[layer_at], "dp", axis=1, tiled=True),
        lax.all_gather(w_down[layer_at], "dp", axis=2, tiled=True),
    )


def reduce_grads(grad_terms):
    return (
        lax.psum_scatter(
            grad_terms[0].astype(jnp.bfloat16), "dp", scatter_dimension=2, tiled=True
        ).astype(jnp.float32),
        lax.psum_scatter(
            grad_terms[1].astype(jnp.bfloat16), "dp", scatter_dimension=2, tiled=True
        ).astype(jnp.float32),
        lax.psum_scatter(
            grad_terms[2].astype(jnp.bfloat16), "dp", scatter_dimension=1, tiled=True
        ).astype(jnp.float32),
        lax.psum_scatter(
            grad_terms[3].astype(jnp.bfloat16), "dp", scatter_dimension=2, tiled=True
        ).astype(jnp.float32),
    )


def gather_rows(stream_pair):
    return jax.tree.map(
        lambda part, own: part.astype(own.dtype),
        lax.all_gather(shortened(stream_pair), "tensor", axis=0, tiled=True),
        stream_pair,
    )


def gather_grads(stream_pair):
    return jax.tree.map(
        lambda part, own: part.astype(own.dtype),
        lax.all_gather(shortened(stream_pair), "tensor", axis=0, tiled=True),
        stream_pair,
    )


def sum_branch(term_fn, own_rows):
    return lax.psum_scatter(
        term_fn(jnp.int32(0), own_rows * lax.axis_size("tensor")),
        "tensor",
        scatter_dimension=0,
        tiled=True,
    )


def sum_normed(term_fn, own_rows):
    return lax.psum_scatter(
        term_fn(jnp.int32(0), lax.axis_size("tensor") * own_rows).astype(jnp.bfloat16),
        "tensor",
        scatter_dimension=0,
        tiled=True,
    ).astype(jnp.float32)


def stream_terms(inputs, weights, pattern):
    pieces = [
        jnp.einsum(pattern, inputs[stream], weights[stream], preferred_element_type=jnp.float32)
        for stream in range(2)
    ]
    return jnp.concatenate(pieces, axis=1)


def forward_layer(streams, mod_rows, weights):
    qkv_w, out_w, up_w, down_w = weights
    own_rows = streams[0].shape[0]
    rows_img = streams[0].shape[1]
    normed = tuple(
        (
            modulate(
                streams[stream], mod_rows[stream][:, None, 0], mod_rows[stream][:, None, 1]
            ).astype(jnp.bfloat16)
            for stream in range(2)
        )
    )
    normed_all = gather_rows(normed)
    projected = [
        jnp.einsum(
            "srd,jdc->jsrc", normed_all[stream], qkv_w[stream], preferred_element_type=jnp.float32
        ).astype(jnp.bfloat16)
        for stream in range(2)
    ]
    key_value = (
        lax.all_gather(projected[0][1:], "dp", axis=2, tiled=True),
        lax.all_gather(projected[1][1:], "dp", axis=2, tiled=True),
    )
    queries = jnp.concatenate([projected[0][0], projected[1][0]], axis=1)
    all_keys = jnp.concatenate([key_value[0][0], key_value[1][0]], axis=1)
    values = jnp.concatenate([key_value[0][1], key_value[1][1]], axis=1)
    scores = attend(queries, all_keys)
    peak_score = jnp.max(scores, axis=-1, keepdims=True)
    raised = jnp.exp(scores - peak_score)
    row_total = jnp.sum(raised, axis=-1, keepdims=True)
    soft_probs = (raised / row_total).astype(jnp.bfloat16)
    log_total = peak_score + jnp.log(row_total)
    mixed_heads = jnp.einsum(
        "shqk,skhe->sqhe", soft_probs, split_heads(values), preferred_element_type=jnp.float32
    )
    mixed_heads = mixed_heads.astype(jnp.bfloat16).reshape(queries.shape)
    mixed_pair = (mixed_heads[:, :rows_img], mixed_heads[:, rows_img:])
    attn_sum = sum_branch(
        lambda first_row, row_count: stream_terms(mixed_pair, out_w, "src,cd->srd"), own_rows
    )
    attn_pair = (attn_sum[:, :rows_img], attn_sum[:, rows_img:])
    middle = tuple(
        (streams[stream] + mod_rows[stream][:, None, 2] * attn_pair[stream] for stream in range(2))
    )
    normed_two = tuple(
        (
            modulate(
                middle[stream], mod_rows[stream][:, None, 3], mod_rows[stream][:, None, 4]
            ).astype(jnp.bfloat16)
            for stream in range(2)
        )
    )
    normed_next = gather_rows(normed_two)
    up_proj = [
        jnp.einsum(
            "srd,df->srf", normed_next[stream], up_w[stream], preferred_element_type=jnp.float32
        )
        for stream in range(2)
    ]
    active = [gelu_tanh(up_proj[stream]).astype(jnp.bfloat16) for stream in range(2)]
    mlp_sum = sum_branch(
        lambda first_row, row_count: stream_terms(active, down_w, "srf,fd->srd"), own_rows
    )
    mlp_pair = (mlp_sum[:, :rows_img], mlp_sum[:, rows_img:])
    result = tuple(
        (middle[stream] + mod_rows[stream][:, None, 5] * mlp_pair[stream] for stream in range(2))
    )
    saved_acts = (
        normed_all,
        queries,
        all_keys,
        values,
        log_total,
        mixed_pair,
        attn_pair,
        middle,
        normed_next,
        up_proj,
        active,
        mlp_pair,
    )
    return (result, saved_acts)


def backward_layer(streams, grads_out, mod_rows, weights, saved_acts):
    qkv_w, out_w, up_w, down_w = weights
    (
        normed_all,
        queries,
        all_keys,
        values,
        log_total,
        mixed_pair,
        attn_pair,
        middle,
        normed_next,
        up_proj,
        active,
        mlp_pair,
    ) = saved_acts
    own_rows = streams[0].shape[0]
    rows_img = streams[0].shape[1]
    keys_img = rows_img * lax.axis_size("dp")
    gated_two = tuple(
        (
            (mod_rows[stream][:, None, 5] * grads_out[stream]).astype(jnp.bfloat16)
            for stream in range(2)
        )
    )
    d_gate_two = [jnp.sum(grads_out[stream] * mlp_pair[stream], axis=1) for stream in range(2)]
    d_mlp = gather_grads(gated_two)
    grad_down = jnp.stack(
        [
            jnp.einsum(
                "srf,srd->fd", active[stream], d_mlp[stream], preferred_element_type=jnp.float32
            )
            for stream in range(2)
        ]
    )
    d_up = []
    for stream in range(2):
        d_active = jnp.einsum(
            "srd,fd->srf", d_mlp[stream], down_w[stream], preferred_element_type=jnp.float32
        )
        d_up.append(jax.vjp(gelu_tanh, up_proj[stream])[1](d_active)[0].astype(jnp.bfloat16))
    grad_up = jnp.stack(
        [
            jnp.einsum(
                "srd,srf->df", normed_next[stream], d_up[stream], preferred_element_type=jnp.float32
            )
            for stream in range(2)
        ]
    )
    d_normed_two = sum_normed(
        lambda first_row, row_count: stream_terms(d_up, up_w, "srf,df->srd"), own_rows
    )
    d_middle = []
    d_shift_two = []
    d_scale_two = []
    for stream in range(2):
        rows_here = d_normed_two[:, :rows_img] if stream == 0 else d_normed_two[:, rows_img:]
        pullback = jax.vjp(
            modulate, middle[stream], mod_rows[stream][:, None, 3], mod_rows[stream][:, None, 4]
        )[1]
        d_values, d_shift, d_scale = pullback(rows_here)
        d_middle.append(grads_out[stream] + d_values)
        d_shift_two.append(d_shift[:, 0])
        d_scale_two.append(d_scale[:, 0])
    gated_one = tuple(
        (
            (mod_rows[stream][:, None, 2] * d_middle[stream]).astype(jnp.bfloat16)
            for stream in range(2)
        )
    )
    d_gate_one = [jnp.sum(d_middle[stream] * attn_pair[stream], axis=1) for stream in range(2)]
    d_attn = gather_grads(gated_one)
    grad_proj_out = jnp.stack(
        [
            jnp.einsum(
                "src,srd->cd",
                mixed_pair[stream],
                d_attn[stream],
                preferred_element_type=jnp.float32,
            )
            for stream in range(2)
        ]
    )
    d_mixed = jnp.concatenate(
        [
            jnp.einsum(
                "srd,cd->src", d_attn[stream], out_w[stream], preferred_element_type=jnp.float32
            )
            for stream in range(2)
        ],
        axis=1,
    ).astype(jnp.bfloat16)
    scores = attend(queries, all_keys)
    soft_probs = jnp.exp(scores - log_total)
    d_soft = jnp.einsum(
        "sqhe,skhe->shqk",
        split_heads(d_mixed),
        split_heads(values),
        preferred_element_type=jnp.float32,
    )
    centre_term = jnp.sum(soft_probs * d_soft, axis=-1, keepdims=True)
    d_scores = (soft_probs * (d_soft - centre_term) * HDIM ** (-0.5)).astype(jnp.bfloat16)
    d_query = (
        jnp.einsum(
            "shqk,skhe->sqhe", d_scores, split_heads(all_keys), preferred_element_type=jnp.float32
        )
        .reshape(queries.shape)
        .astype(jnp.bfloat16)
    )
    d_key = jnp.einsum(
        "shqk,sqhe->skhe", d_scores, split_heads(queries), preferred_element_type=jnp.float32
    ).reshape(all_keys.shape)
    d_value = jnp.einsum(
        "shqk,sqhe->skhe",
        soft_probs.astype(jnp.bfloat16),
        split_heads(d_mixed),
        preferred_element_type=jnp.float32,
    ).reshape(all_keys.shape)
    key_terms = (
        lax.psum_scatter(
            jnp.stack([d_key[:, :keys_img], d_value[:, :keys_img]]).astype(jnp.bfloat16),
            "dp",
            scatter_dimension=2,
            tiled=True,
        ).astype(jnp.float32),
        lax.psum_scatter(
            jnp.stack([d_key[:, keys_img:], d_value[:, keys_img:]]).astype(jnp.bfloat16),
            "dp",
            scatter_dimension=2,
            tiled=True,
        ).astype(jnp.float32),
    )
    d_proj = (
        jnp.concatenate([d_query[None, :, :rows_img], key_terms[0].astype(jnp.bfloat16)], axis=0),
        jnp.concatenate([d_query[None, :, rows_img:], key_terms[1].astype(jnp.bfloat16)], axis=0),
    )
    grad_qkv = jnp.stack(
        [
            jnp.einsum(
                "srd,jsrc->jdc",
                normed_all[stream],
                d_proj[stream],
                preferred_element_type=jnp.float32,
            )
            for stream in range(2)
        ]
    )
    d_normed_one = sum_normed(
        lambda first_row, row_count: stream_terms(d_proj, qkv_w, "jsrc,jdc->srd"), own_rows
    )
    d_inputs = []
    dmod_list = []
    for stream in range(2):
        rows_here = d_normed_one[:, :rows_img] if stream == 0 else d_normed_one[:, rows_img:]
        pullback = jax.vjp(
            modulate, streams[stream], mod_rows[stream][:, None, 0], mod_rows[stream][:, None, 1]
        )[1]
        d_values, d_shift, d_scale = pullback(rows_here)
        d_inputs.append(d_middle[stream] + d_values)
        dmod_list.append(
            jnp.stack(
                [
                    d_shift[:, 0],
                    d_scale[:, 0],
                    d_gate_one[stream],
                    d_shift_two[stream],
                    d_scale_two[stream],
                    d_gate_two[stream],
                ],
                axis=1,
            )
        )
    return (tuple(d_inputs), jnp.stack(dmod_list), (grad_qkv, grad_proj_out, grad_up, grad_down))


def per_device(
    image_in,
    text_in,
    cond_table,
    cond_index,
    w_mod,
    w_qkv,
    w_out,
    w_up,
    w_down,
    cot_image,
    cot_text,
):
    n_tensor = lax.axis_size("tensor")
    tensor_at = lax.axis_index("tensor")
    dp_at = lax.axis_index("dp")
    micro_count = image_in.shape[0]
    own_rows = image_in.shape[1]
    model_width = image_in.shape[3]
    layer_count = w_qkv.shape[0]
    slab_rows = w_mod.shape[2]
    column_count = w_mod.shape[3]
    index_flat = cond_index.reshape(-1)
    onehot = (
        index_flat[:, None] == jnp.arange(cond_table.shape[0], dtype=jnp.int32)[None, :]
    ).astype(jnp.float32)
    cond_rows = jnp.dot(onehot, cond_table, precision=HIGHEST, preferred_element_type=jnp.float32)
    cond_slab = lax.dynamic_slice_in_dim(cond_rows, dp_at * slab_rows, slab_rows, 1)
    silu_slab = jax.nn.silu(cond_slab).astype(jnp.bfloat16)
    tensor_slot = (jnp.arange(n_tensor, dtype=jnp.int32) == tensor_at).astype(jnp.float32)
    partial_mod = jnp.einsum("sd,lmdc->lmsc", silu_slab, w_mod, preferred_element_type=jnp.float32)
    placed = partial_mod[:, :, :, None, :] * tensor_slot[None, None, None, :, None]
    mod_full = lax.psum(placed, ("dp", "tensor"))
    mod_full = mod_full.reshape(layer_count, 2, micro_count, n_tensor, own_rows, 6, model_width)
    mod_own = lax.dynamic_index_in_dim(mod_full, tensor_at, 3, keepdims=False)
    totals = [None] * layer_count
    dmod_store = [[None] * micro_count for layer_at in range(layer_count)]
    outputs_image = []
    outputs_text = []
    grads_image = []
    grads_text = []
    for micro_at in range(micro_count):
        streams = (image_in[micro_at].astype(jnp.float32), text_in[micro_at].astype(jnp.float32))
        layer_inputs = []
        layer_saved = []
        layer_weights = []
        for layer_at in range(layer_count):
            weights = fetch_weights(w_qkv, w_out, w_up, w_down, layer_at)
            layer_inputs.append(streams)
            streams, saved_acts = forward_layer(streams, mod_own[layer_at, :, micro_at], weights)
            layer_saved.append(saved_acts)
            layer_weights.append(weights)
        outputs_image.append(streams[0].astype(jnp.bfloat16))
        outputs_text.append(streams[1].astype(jnp.bfloat16))
        grads_now = (
            cot_image[micro_at].astype(jnp.float32),
            cot_text[micro_at].astype(jnp.float32),
        )
        for layer_at in reversed(range(layer_count)):
            weights = fetch_weights(w_qkv, w_out, w_up, w_down, layer_at)
            grads_now, dmod_rows, weight_terms = backward_layer(
                layer_inputs[layer_at],
                grads_now,
                mod_own[layer_at, :, micro_at],
                weights,
                layer_saved[layer_at],
            )
            dmod_store[layer_at][micro_at] = dmod_rows
            totals[layer_at] = (
                weight_terms
                if totals[layer_at] is None
                else jax.tree.map(jnp.add, totals[layer_at], weight_terms)
            )
        grads_image.append(grads_now[0])
        grads_text.append(grads_now[1])
    totals = [reduce_grads(totals[layer_at]) for layer_at in range(layer_count)]
    dmod_own = jnp.stack(
        [jnp.stack(dmod_store[layer_at], axis=1) for layer_at in range(layer_count)]
    )
    dmod_placed = dmod_own[:, :, :, None] * tensor_slot[None, None, None, :, None, None, None]
    dmod_full = lax.psum(dmod_placed, ("dp", "tensor"))
    dmod_full = dmod_full.reshape(
        layer_count, 2, micro_count * n_tensor * own_rows, n_tensor, column_count
    )
    dmod_cols = lax.dynamic_index_in_dim(dmod_full, tensor_at, 3, keepdims=False)
    grad_w_mod = jnp.einsum(
        "sd,lmsc->lmdc",
        silu_slab.astype(jnp.float32),
        dmod_cols,
        precision=HIGHEST,
        preferred_element_type=jnp.float32,
    )
    d_silu = jnp.einsum(
        "lmsc,lmdc->sd",
        dmod_cols,
        w_mod.astype(jnp.float32),
        precision=HIGHEST,
        preferred_element_type=jnp.float32,
    )
    d_cond = jax.vjp(jax.nn.silu, cond_slab)[1](d_silu)[0]
    grad_cond = lax.psum(
        jnp.dot(onehot.T, d_cond, precision=HIGHEST, preferred_element_type=jnp.float32), "tensor"
    )
    grad_w_qkv = jnp.stack([totals[layer_at][0] for layer_at in range(layer_count)])
    grad_w_out = jnp.stack([totals[layer_at][1] for layer_at in range(layer_count)])
    grad_w_up = jnp.stack([totals[layer_at][2] for layer_at in range(layer_count)])
    grad_w_down = jnp.stack([totals[layer_at][3] for layer_at in range(layer_count)])
    return (
        jnp.stack(outputs_image),
        jnp.stack(outputs_text),
        jnp.stack(grads_image),
        jnp.stack(grads_text),
        grad_cond,
        grad_w_mod,
        grad_w_qkv,
        grad_w_out,
        grad_w_up,
        grad_w_down,
    )


def solution(mesh):
    placed = (
        P(None, "tensor", "dp", None),
        P(None, "tensor", "dp", None),
        P(),
        P(),
        P(None, None, "dp", "tensor"),
        P(None, None, None, "dp", "tensor"),
        P(None, None, "tensor", "dp"),
        P(None, None, "dp", "tensor"),
        P(None, None, "tensor", "dp"),
        P(None, "tensor", "dp", None),
        P(None, "tensor", "dp", None),
    )
    return jax.shard_map(
        per_device,
        mesh=mesh,
        in_specs=placed,
        out_specs=(
            P(None, "tensor", "dp", None),
            P(None, "tensor", "dp", None),
            P(None, "tensor", "dp", None),
            P(None, "tensor", "dp", None),
            P(None, "dp"),
            P(None, None, "dp", "tensor"),
            P(None, None, None, "dp", "tensor"),
            P(None, None, "tensor", "dp"),
            P(None, None, "dp", "tensor"),
            P(None, None, "tensor", "dp"),
        ),
        check_vma=False,
    )
```

profile of v0, /device:TPU:0, one launch (start us, length us, event | category | flops | bytes accessed | tf_op | source)
XLA Modules:
  0.0 4282.2 jit_solution(11042560775754207691)
XLA Ops:
  19.1 131.1 %all-reduce.20.cloned.1.call-done = f32[2,2,2,4,1,6,1536]{6,5,3,2,1,0,4:T(8,128)} async-done(((f32[2,2,2,4,1,6,1536]{6,5,3,2,1,0,4:T(8,128)}), f32[2,2,2,4,1,6,1536]{6,5,3,2,1,0,4:T(8,128)}) %all-reduce.20.cloned.1.call-update) | async-done | bytes 1179664 | tf_op jit(solution)/shard_map/psum | solution.py:403
  162.0 30.2 all-gather.37.cloned.1.call-done
  192.2 50.2 %all-gather.77.cloned.1.call-done = bf16[1,2,3,1536,384]{4,3,2,1,0:T(8,128)(2,1)} async-done(((bf16[1,2,3,192,384]{4,3,2,1,0:T(8,128)(2,1)}), bf16[1,2,3,1536,384]{4,3,2,1,0:T(8,128)(2,1)}) %all-gather.77.cloned.1.call-update) | async-done | bytes 7077904 | tf_op jit(solution)/shard_map/all_gather | solution.py:46
  385.4 60.3 %reduce-scatter.23.cloned.1.call-done = f32[1,148,1536]{2,1,0:T(8,128)} async-done(((f32[4,148,1536]{2,1,0:T(8,128)}), f32[1,148,1536]{2,1,0:T(8,128)}) %reduce-scatter.23.cloned.1.call-update) | async-done | bytes 909328 | tf_op jit(solution)/shard_map/reduce_scatter | solution.py:87
  450.2 57.4 %all-gather.83.cloned.1.call-done = bf16[1,2,1536,1536]{2,1,0,3:T(2,128)(2,1)} async-done(((bf16[1,2,1536,192]{2,1,0,3:T(2,128)(2,1)}), bf16[1,2,1536,1536]{2,1,0,3:T(2,128)(2,1)}) %all-gather.83.cloned.1.call-update) | async-done | bytes 9437200 | tf_op jit(solution)/shard_map/all_gather | solution.py:49
  527.0 22.4 copy.517
  549.4 22.5 copy.516
  627.5 67.3 %reduce-scatter.25.cloned.1.call-done = f32[1,148,1536]{2,1,0:T(8,128)} async-done(((f32[4,148,1536]{2,1,0:T(8,128)}), f32[1,148,1536]{2,1,0:T(8,128)}) %reduce-scatter.25.cloned.1.call-update) | async-done | bytes 909328 | tf_op jit(solution)/shard_map/reduce_scatter | solution.py:87
  701.6 44.4 %all-gather.85.cloned.1.call-done = bf16[1,2,3,1536,384]{4,3,2,1,0:T(8,128)(2,1)} async-done(((bf16[1,2,3,192,384]{4,3,2,1,0:T(8,128)(2,1)}), bf16[1,2,3,1536,384]{4,3,2,1,0:T(8,128)(2,1)}) %all-gather.85.cloned.1.call-update) | async-done | bytes 7077904 | tf_op jit(solution)/shard_map/all_gather | solution.py:46
  746.0 39.1 all-gather.43.cloned.1.call-done
  793.7 21.8 all-gather.87.cloned.1.call-done
  934.1 65.4 %reduce-scatter.27.cloned.1.call-done = f32[1,148,1536]{2,1,0:T(8,128)} async-done(((f32[4,148,1536]{2,1,0:T(8,128)}), f32[1,148,1536]{2,1,0:T(8,128)}) %reduce-scatter.27.cloned.1.call-update) | async-done | bytes 909328 | tf_op jit(solution)/shard_map/reduce_scatter | solution.py:87
  1024.3 36.9 all-gather.91.cloned.1.call-done
  1061.2 19.4 fusion.555
  1080.7 22.3 copy.526
  1103.0 22.4 copy.508
  1171.0 31.9 all-gather.61.cloned.1.call-done
  1231.6 25.1 reduce-scatter.39.cloned.1.call-done
  1262.0 66.3 %reduce-scatter.29.cloned.1.call-done = f32[1,148,1536]{2,1,0:T(8,128)} async-done(((f32[4,148,1536]{2,1,0:T(8,128)}), f32[1,148,1536]{2,1,0:T(8,128)}) %reduce-scatter.29.cloned.1.call-update) | async-done | bytes 909328 | tf_op jit(solution)/shard_map/reduce_scatter | solution.py:87
  1401.1 40.2 convolution_convert_fusion.3
  1472.0 39.9 fusion.249
  1525.4 43.4 %reduce-scatter.41.cloned.1.call-done = bf16[2,4,128,384]{3,2,0,1:T(8,128)(2,1)} async-done(((bf16[2,4,1024,384]{3,2,0,1:T(8,128)(2,1)}), bf16[2,4,128,384]{3,2,0,1:T(8,128)(2,1)}) %reduce-scatter.41.cloned.1.call-update) | async-done | bytes 786448 | tf_op jit(solution)/shard_map/reduce_scatter | solution.py:315
  1575.0 40.0 reduce-scatter.43.cloned.1.call-done
  1679.8 38.9 reduce-scatter.45.cloned.1.call-done
  1793.7 40.6 convolution_convert_fusion.2
  1863.3 39.6 fusion.246
  1916.7 45.0 %reduce-scatter.47.cloned.1.call-done = bf16[2,4,128,384]{3,2,0,1:T(8,128)(2,1)} async-done(((bf16[2,4,1024,384]{3,2,0,1:T(8,128)(2,1)}), bf16[2,4,128,384]{3,2,0,1:T(8,128)(2,1)}) %reduce-scatter.47.cloned.1.call-update) | async-done | bytes 786448 | tf_op jit(solution)/shard_map/reduce_scatter | solution.py:315
  1970.2 37.6 reduce-scatter.49.cloned.1.call-done
  2015.2 36.4 all-gather.49.cloned.1.call-done
  2158.1 67.7 %reduce-scatter.31.cloned.1.call-done = f32[1,148,1536]{2,1,0:T(8,128)} async-done(((f32[4,148,1536]{2,1,0:T(8,128)}), f32[1,148,1536]{2,1,0:T(8,128)}) %reduce-scatter.31.cloned.1.call-update) | async-done | bytes 909328 | tf_op jit(solution)/shard_map/reduce_scatter | solution.py:87
  2284.2 69.6 %reduce-scatter.33.cloned.1.call-done = f32[1,148,1536]{2,1,0:T(8,128)} async-done(((f32[4,148,1536]{2,1,0:T(8,128)}), f32[1,148,1536]{2,1,0:T(8,128)}) %reduce-scatter.33.cloned.1.call-update) | async-done | bytes 909328 | tf_op jit(solution)/shard_map/reduce_scatter | solution.py:87
  2358.4 37.6 all-gather.55.cloned.1.call-done
  2502.8 67.3 %reduce-scatter.35.cloned.1.call-done = f32[1,148,1536]{2,1,0:T(8,128)} async-done(((f32[4,148,1536]{2,1,0:T(8,128)}), f32[1,148,1536]{2,1,0:T(8,128)}) %reduce-scatter.35.cloned.1.call-update) | async-done | bytes 909328 | tf_op jit(solution)/shard_map/reduce_scatter | solution.py:87
  2631.1 25.5 all-gather.69.cloned.1.call-done
  2671.6 38.9 reduce-scatter.51.cloned.1.call-done
  2783.8 40.4 convolution_convert_fusion.1
  2853.2 40.2 fusion.243
  2907.0 46.0 %reduce-scatter.53.cloned.1.call-done = bf16[2,4,128,384]{3,2,0,1:T(8,128)(2,1)} async-done(((bf16[2,4,1024,384]{3,2,0,1:T(8,128)(2,1)}), bf16[2,4,128,384]{3,2,0,1:T(8,128)(2,1)}) %reduce-scatter.53.cloned.1.call-update) | async-done | bytes 786448 | tf_op jit(solution)/shard_map/reduce_scatter | solution.py:315
  2971.1 28.0 reduce-scatter.55.cloned.1.call-done
  3005.7 64.8 %reduce-scatter.37.cloned.1.call-done = f32[1,148,1536]{2,1,0:T(8,128)} async-done(((f32[4,148,1536]{2,1,0:T(8,128)}), f32[1,148,1536]{2,1,0:T(8,128)}) %reduce-scatter.37.cloned.1.call-update) | async-done | bytes 909328 | tf_op jit(solution)/shard_map/reduce_scatter | solution.py:87
  3134.8 39.2 reduce-scatter.57.cloned.1.call-done
  3249.0 40.5 convolution_convert_fusion
  3318.6 39.4 fusion.240
  3371.6 45.4 %reduce-scatter.59.cloned.1.call-done = bf16[2,4,128,384]{3,2,0,1:T(8,128)(2,1)} async-done(((bf16[2,4,1024,384]{3,2,0,1:T(8,128)(2,1)}), bf16[2,4,128,384]{3,2,0,1:T(8,128)(2,1)}) %reduce-scatter.59.cloned.1.call-update) | async-done | bytes 786448 | tf_op jit(solution)/shard_map/reduce_scatter | solution.py:315
  3447.4 24.0 copy.441
  3601.2 24.4 copy.444
  3797.2 111.6 %all-reduce.22.cloned.1.call-done = f32[2,2,8,4,2304]{4,3,2,1,0:T(4,128)} async-done(((f32[2,2,8,4,2304]{4,3,2,1,0:T(4,128)}), f32[2,2,8,4,2304]{4,3,2,1,0:T(4,128)}) %all-reduce.22.cloned.1.call-update) | async-done | bytes 1179664 | tf_op jit(solution)/shard_map/psum | solution.py:451
  3933.1 323.7 %all-reduce.34.cloned.1.call-done = (bf16[2,3,1536,384]{3,0,1,2:T(2,128)(2,1)}, bf16[2,3,1536,384]{3,0,1,2:T(2,128)(2,1)}, bf16[2,384,1536]{1,0,2:T(2,128)(2,1)}...) async-done(((bf16[2,3,1536,384]{3,0,1,2:T(2,128)(2,1)}, bf16[2,3,1536,384]{3,0,1,2:T(2,128)(2,1)}, bf16[2,384,1536]{1,0,2:T(2,128)(2,1)}, ...) | async-done | bytes 28311568
  (1445 shorter events, 1849.7 us)
Async XLA Ops:
  7.2 143.0 %all-reduce.20.cloned.1.call-start = ((), (), s32[]{:S(2)}) async-start(), calls=%async_computation.22 | async-start | bytes 3145728 | tf_op jit(solution)/shard_map/psum | solution.py:403
  15.3 176.8 %all-gather.37.cloned.1.call-start = ((), (), s32[]{:S(2)}) async-start(), calls=%async_computation.23 | async-start | bytes 1966080 | tf_op jit(solution)/shard_map/all_gather | solution.py:73
  159.0 114.8 %all-gather.79.cloned.1.call-start = ((), (), s32[]{:S(2)}) async-start(), calls=%async_computation.67 | async-start | bytes 2654208 | tf_op jit(solution)/shard_map/all_gather | solution.py:47
  161.9 163.7 %all-gather.39.cloned.1.call-start = ((), (), s32[]{:S(2)}) async-start(), calls=%async_computation.24 | async-start | bytes 7077888 | tf_op jit(solution)/shard_map/all_gather | solution.py:132
  249.1 196.6 %reduce-scatter.23.cloned.1.call-start = ((), (), s32[]{:S(2)}) async-start(), calls=%async_computation.25 | async-start | bytes 4669440 | tf_op jit(solution)/shard_map/reduce_scatter | solution.py:87
  376.1 131.5 %all-gather.83.cloned.1.call-start = ((), (), s32[]{:S(2)}) async-start(), calls=%async_computation.69 | async-start | bytes 10616832 | tf_op jit(solution)/shard_map/all_gather | solution.py:49
  381.6 210.2 %all-gather.81.cloned.1.call-start = ((), (), s32[]{:S(2)}) async-start(), calls=%async_computation.68 | async-start | bytes 10616832 | tf_op jit(solution)/shard_map/all_gather | solution.py:48
  385.3 225.2 %all-gather.41.cloned.1.call-start = ((), (), s32[]{:S(2)}) async-start(), calls=%async_computation.26 | async-start | bytes 1966080 | tf_op jit(solution)/shard_map/all_gather | solution.py:73
  450.2 244.7 %reduce-scatter.25.cloned.1.call-start = ((), (), s32[]{:S(2)}) async-start(), calls=%async_computation.27 | async-start | bytes 4669440 | tf_op jit(solution)/shard_map/reduce_scatter | solution.py:87
  625.0 121.1 %all-gather.85.cloned.1.call-start = ((), (), s32[]{:S(2)}) async-start(), calls=%async_computation.70 | async-start | bytes 7962624 | tf_op jit(solution)/shard_map/all_gather | solution.py:46
  625.7 159.4 %all-gather.43.cloned.1.call-start = ((), (), s32[]{:S(2)}) async-start(), calls=%async_computation.28 | async-start | bytes 1966080 | tf_op jit(solution)/shard_map/all_gather | solution.py:73
  699.5 116.0 %all-gather.87.cloned.1.call-start = ((), (), s32[]{:S(2)}) async-start(), calls=%async_computation.71 | async-start | bytes 2654208 | tf_op jit(solution)/shard_map/all_gather | solution.py:47
  701.6 177.3 %all-gather.45.cloned.1.call-start = ((), (), s32[]{:S(2)}) async-start(), calls=%async_computation.29 | async-start | bytes 7077888 | tf_op jit(solution)/shard_map/all_gather | solution.py:132
  791.8 207.6 %reduce-scatter.27.cloned.1.call-start = ((), (), s32[]{:S(2)}) async-start(), calls=%async_computation.30 | async-start | bytes 4669440 | tf_op jit(solution)/shard_map/reduce_scatter | solution.py:87
  929.5 131.7 %all-gather.91.cloned.1.call-start = ((), (), s32[]{:S(2)}) async-start(), calls=%async_computation.73 | async-start | bytes 10616832 | tf_op jit(solution)/shard_map/all_gather | solution.py:49
  933.5 212.1 %all-gather.89.cloned.1.call-start = ((), (), s32[]{:S(2)}) async-start(), calls=%async_computation.72 | async-start | bytes 10616832 | tf_op jit(solution)/shard_map/all_gather | solution.py:48
  934.1 229.9 %all-gather.47.cloned.1.call-start = ((), (), s32[]{:S(2)}) async-start(), calls=%async_computation.31 | async-start | bytes 1966080 | tf_op jit(solution)/shard_map/all_gather | solution.py:73
  1004.1 198.8 %all-gather.61.cloned.1.call-start = ((), (), s32[]{:S(2)}) async-start(), calls=%async_computation.43 | async-start | bytes 1966080 | tf_op jit(solution)/shard_map/all_gather | solution.py:81
  1024.3 232.4 %reduce-scatter.39.cloned.1.call-start = ((), (), s32[]{:S(2)}) async-start(), calls=%async_computation.44 | async-start | bytes 2334720 | tf_op jit(solution)/shard_map/reduce_scatter | solution.py:96
  1217.8 110.6 %reduce-scatter.29.cloned.1.call-start = ((), (), s32[]{:S(2)}) async-start(), calls=%async_computation.32 | async-start | bytes 4669440 | tf_op jit(solution)/shard_map/reduce_scatter | solution.py:87
  1229.6 145.5 %all-gather.63.cloned.1.call-start = ((), (), s32[]{:S(2)}) async-start(), calls=%async_computation.45 | async-start | bytes 1966080 | tf_op jit(solution)/shard_map/all_gather | solution.py:81
  1333.1 186.4 %all-reduce.24.cloned.1.call-start = ((), (), s32[]{:S(2)}) async-start(), calls=%async_computation.74 | async-start | bytes 1966080
  1448.2 120.6 %reduce-scatter.41.cloned.1.call-start = ((), (), s32[]{:S(2)}) async-start(), calls=%async_computation.46 | async-start | bytes 7077888 | tf_op jit(solution)/shard_map/reduce_scatter | solution.py:315
  1470.2 144.8 %reduce-scatter.43.cloned.1.call-start = ((), (), s32[]{:S(2)}) async-start(), calls=%async_computation.47 | async-start | bytes 2334720 | tf_op jit(solution)/shard_map/reduce_scatter | solution.py:96
  1726.6 183.9 %all-reduce.26.cloned.1.call-start = ((), (), s32[]{:S(2)}) async-start(), calls=%async_computation.75 | async-start | bytes 1966080
  1841.2 120.5 %reduce-scatter.47.cloned.1.call-start = ((), (), s32[]{:S(2)}) async-start(), calls=%async_computation.51 | async-start | bytes 7077888 | tf_op jit(solution)/shard_map/reduce_scatter | solution.py:315
  1863.2 144.6 %reduce-scatter.49.cloned.1.call-start = ((), (), s32[]{:S(2)}) async-start(), calls=%async_computation.52 | async-start | bytes 2334720 | tf_op jit(solution)/shard_map/reduce_scatter | solution.py:96
  2058.2 167.5 %reduce-scatter.31.cloned.1.call-start = ((), (), s32[]{:S(2)}) async-start(), calls=%async_computation.35 | async-start | bytes 4669440 | tf_op jit(solution)/shard_map/reduce_scatter | solution.py:87
  2157.9 111.6 %all-gather.53.cloned.1.call-start = ((), (), s32[]{:S(2)}) async-start(), calls=%async_computation.36 | async-start | bytes 1966080 | tf_op jit(solution)/shard_map/all_gather | solution.py:73
  2230.2 123.6 %reduce-scatter.33.cloned.1.call-start = ((), (), s32[]{:S(2)}) async-start(), calls=%async_computation.37 | async-start | bytes 4669440 | tf_op jit(solution)/shard_map/reduce_scatter | solution.py:87
  2284.2 111.8 %all-gather.55.cloned.1.call-start = ((), (), s32[]{:S(2)}) async-start(), calls=%async_computation.38 | async-start | bytes 1966080 | tf_op jit(solution)/shard_map/all_gather | solution.py:73
  2402.7 167.4 %reduce-scatter.35.cloned.1.call-start = ((), (), s32[]{:S(2)}) async-start(), calls=%async_computation.40 | async-start | bytes 4669440 | tf_op jit(solution)/shard_map/reduce_scatter | solution.py:87
  2502.3 121.5 %all-gather.59.cloned.1.call-start = ((), (), s32[]{:S(2)}) async-start(), calls=%async_computation.41 | async-start | bytes 1966080 | tf_op jit(solution)/shard_map/all_gather | solution.py:73
  2592.7 117.8 %reduce-scatter.51.cloned.1.call-start = ((), (), s32[]{:S(2)}) async-start(), calls=%async_computation.54 | async-start | bytes 2334720 | tf_op jit(solution)/shard_map/reduce_scatter | solution.py:96
  2717.6 183.2 %all-reduce.28.cloned.1.call-start = ((), (), s32[]{:S(2)}) async-start(), calls=%async_computation.76 | async-start | bytes 1966080
  2831.0 122.0 %reduce-scatter.53.cloned.1.call-start = ((), (), s32[]{:S(2)}) async-start(), calls=%async_computation.56 | async-start | bytes 7077888 | tf_op jit(solution)/shard_map/reduce_scatter | solution.py:315
  2853.2 146.0 %reduce-scatter.55.cloned.1.call-start = ((), (), s32[]{:S(2)}) async-start(), calls=%async_computation.57 | async-start | bytes 2334720 | tf_op jit(solution)/shard_map/reduce_scatter | solution.py:96
  2959.1 111.4 %reduce-scatter.37.cloned.1.call-start = ((), (), s32[]{:S(2)}) async-start(), calls=%async_computation.42 | async-start | bytes 4669440 | tf_op jit(solution)/shard_map/reduce_scatter | solution.py:87
  2970.7 149.1 %all-gather.73.cloned.1.call-start = ((), (), s32[]{:S(2)}) async-start(), calls=%async_computation.58 | async-start | bytes 1966080 | tf_op jit(solution)/shard_map/all_gather | solution.py:81
  3077.8 96.2 %reduce-scatter.57.cloned.1.call-start = ((), (), s32[]{:S(2)}) async-start(), calls=%async_computation.59 | async-start | bytes 2334720 | tf_op jit(solution)/shard_map/reduce_scatter | solution.py:96
  3181.9 183.5 %all-reduce.30.cloned.1.call-start = ((), (), s32[]{:S(2)}) async-start(), calls=%async_computation.77 | async-start | bytes 1966080
  3296.5 120.6 %reduce-scatter.59.cloned.1.call-start = ((), (), s32[]{:S(2)}) async-start(), calls=%async_computation.61 | async-start | bytes 7077888 | tf_op jit(solution)/shard_map/reduce_scatter | solution.py:315
  3318.5 404.7 %reduce-scatter.61.cloned.1.call-start = ((), (), s32[]{:S(2)}) async-start(), calls=%async_computation.62 | async-start | bytes 2334720 | tf_op jit(solution)/shard_map/reduce_scatter | solution.py:96
  3423.2 363.0 %all-reduce.32.cloned.1.call-start = ((), (), s32[]{:S(2)}) async-start(), calls=%async_computation.78 | async-start | bytes 18874368
  3471.5 317.8 %reduce-scatter.65.cloned.1.call-start = ((), (), s32[]{:S(2)}) async-start(), calls=%async_computation.65 | async-start | bytes 10616832 | tf_op jit(solution)/shard_map/reduce_scatter | solution.py:61
  3495.4 294.0 %reduce-scatter.63.cloned.1.call-start = ((), (), s32[]{:S(2)}) async-start(), calls=%async_computation.64 | async-start | bytes 10616832 | tf_op jit(solution)/shard_map/reduce_scatter | solution.py:61
  3524.5 384.2 %all-reduce.22.cloned.1.call-start = ((), (), s32[]{:S(2)}) async-start(), calls=%async_computation.63 | async-start | bytes 2359296 | tf_op jit(solution)/shard_map/psum | solution.py:451
  3750.0 506.8 %all-reduce.34.cloned.1.call-start = ((), (), s32[]{:S(2)}) async-start(), calls=%async_computation.79 | async-start | bytes 56623104
  (369 other events, 4844.8 us)
Sparse Core Ops, SparseCore 0:
  15.5 134.6 all-reduce.19
  194.7 47.7 all-gather.76
  276.1 49.4 all-gather.38
  376.2 69.4 reduce-scatter.22
  448.3 59.2 all-gather.82
  510.2 58.8 all-gather.80
  571.3 39.1 all-gather.40
  625.1 69.7 reduce-scatter.24
  696.7 49.2 all-gather.84
  817.3 45.5 all-gather.44
  929.6 69.8 reduce-scatter.26
  1002.0 59.2 all-gather.90
  1063.7 58.8 all-gather.88
  1124.7 39.2 all-gather.46
  1259.7 68.5 reduce-scatter.28
  1333.2 41.8 all-gather.62
  1448.3 55.3 all-reduce.23
  1507.6 61.2 reduce-scatter.40
  1575.0 39.9 reduce-scatter.42
  1623.8 40.9 all-gather.64
  1679.8 38.7 reduce-scatter.44
  1726.7 40.9 all-gather.66
  1841.3 55.1 all-reduce.25
  1900.7 60.9 reduce-scatter.46
  1967.9 39.8 reduce-scatter.48
  2058.4 48.3 all-gather.50
  2158.0 67.7 reduce-scatter.30
  2230.3 39.1 all-gather.52
  2284.3 69.4 reduce-scatter.32
  2402.8 48.3 all-gather.56
  2502.4 67.5 reduce-scatter.34
  2574.8 43.7 all-gather.58
  2717.7 39.8 all-gather.70
  2831.2 56.6 all-reduce.27
  2892.0 60.9 reduce-scatter.52
  2959.2 39.8 reduce-scatter.54
  3001.9 68.5 reduce-scatter.36
  3077.9 41.8 all-gather.72
  3134.8 39.1 reduce-scatter.56
  3182.0 40.9 all-gather.74
  3296.6 55.2 all-reduce.29
  3356.2 60.8 reduce-scatter.58
  3423.3 39.8 reduce-scatter.60
  3471.6 138.2 all-reduce.31
  3613.8 76.5 reduce-scatter.64
  3694.3 76.4 reduce-scatter.62
  3777.7 130.9 all-reduce.21
  3913.8 342.9 all-reduce.33
  (10 shorter events, 354.3 us)
where the time goes:
time: 4300 us; the launch traced here: 4280 us
  waiting for transfers between devices  2040 us (47%)
  matrix products  856 us (20%)
  local copies, waits for them, and re-layouts  681 us (16%)
  other arithmetic  354 us (8%)
  blocking collectives  329 us (8%)
    reduce_scatter x8, waiting for transfers between devices, sum_branch(): lax.psum_scatter(term_fn(jnp.int32(0), own_rows * lax.axis_size('tensor')...  529 us
    unnamed x64, waiting for transfers between devices  326 us
    unnamed x772, local copies, waits for them, and re-layouts  283 us
    reduce_scatter x8, waiting for transfers between devices, sum_normed(): lax.psum_scatter(term_fn(jnp.int32(0), lax.axis_size('tensor') * own_rows...  248 us
    reduce_scatter x4, waiting for transfers between devices, backward_layer(): lax.psum_scatter(jnp.stack([d_key[:, :keys_img], d_value[:, :keys_img]])....  180 us
    all_gather x8, waiting for transfers between devices, gather_rows(): lax.all_gather(shortened(stream_pair), 'tensor', axis=0, tiled=True)  172 us
    dot_general x4, matrix products, backward_layer(): jnp.einsum('shqk,sqhe->skhe', d_scores, split_heads(queries), preferred_e...  162 us
    dot_general x4, matrix products, backward_layer(): jnp.einsum('shqk,skhe->sqhe', d_scores, split_heads(all_keys), preferred_...  159 us
  transfers between devices with their start and end apart: 58, of which 44 were waited for; matrix products, arithmetic and copies ran while one was open for 27% of the time, Pallas kernels for 0%

commit v1 on v0

v1 whole, which is shorter than its diff:
```python
import functools

import jax
import jax.numpy as jnp
from jax import lax
from jax.experimental import pallas as pl
from jax.experimental.layout import Layout, with_layout_constraint
from jax.experimental.pallas import tpu as pltpu
from jax.sharding import PartitionSpec as P

HDIM = 64
LANES = 128
EPS = 1e-06
HIGHEST = lax.Precision.HIGHEST
BF16 = jnp.bfloat16
F32 = jnp.float32


def dot32(pattern, left, right):
    return jnp.einsum(pattern, left, right, preferred_element_type=F32)


def tensor_swap(values, distance):
    count = lax.axis_size("tensor")
    return lax.ppermute(values, "tensor", [(i, i ^ distance) for i in range(count)])


def pair_swap(values):
    return tensor_swap(values, 1)


def hi_swap(values, block):
    return tensor_swap(values, 2 * block)


def pair_sum(own_part, other_part):
    return own_part + pair_swap(other_part.astype(BF16)).astype(F32)


def dp_sum(values):
    count = lax.axis_size("dp")
    step = 1
    while step < count:
        values = values + lax.ppermute(values, "dp", [(i, i ^ step) for i in range(count)])
        step *= 2
    return values


def rows_of_all(values):
    count = lax.axis_size("tensor")
    return jnp.stack([values] + [tensor_swap(values, at) for at in range(1, count)])


def sum_of_all(parts):
    total = parts[0]
    for at in range(1, lax.axis_size("tensor")):
        total = total + tensor_swap(parts[at].astype(BF16), at).astype(F32)
    return total


def to_sequences(parts, blocks):
    received = [parts[:2]] + [
        hi_swap(parts[2 * block : 2 * block + 2], block) for block in range(1, blocks)
    ]
    return [flat_pairs(part) for part in received]


def to_blocks(by_block, seqs):
    split = [part.reshape(2, seqs, *part.shape[1:]) for part in by_block]
    parts = [split[0]] + [hi_swap(split[block], block) for block in range(1, len(split))]
    return jnp.concatenate(parts, axis=0)


def flat_pairs(values):
    return values.reshape(-1, *values.shape[2:])


def head_mask(rows, which):
    lane = lax.broadcasted_iota(jnp.int32, (rows, LANES), 1)
    return (lane < HDIM) if which == 0 else (lane >= HDIM)


def nt_dot(left, right):
    return lax.dot_general(left, right, (((1,), (1,)), ((), ())), preferred_element_type=F32)


def attn_fwd_kernel(q_ref, k_ref, v_ref, o_ref, lse_ref):
    rows = q_ref.shape[0]
    queries = q_ref[...] * jnp.asarray(HDIM ** (-0.5), BF16)
    keys = k_ref[...]
    values_t = v_ref[...].astype(F32).T.astype(BF16)
    parts = []
    for which in range(2):
        masked = jnp.where(head_mask(rows, which), queries, jnp.zeros_like(queries))
        scores = nt_dot(keys, masked)
        peak = jnp.max(scores, axis=0, keepdims=True)
        raised = jnp.exp(scores - peak)
        total = jnp.sum(raised, axis=0, keepdims=True)
        out_t = jnp.dot(
            values_t[which * HDIM : (which + 1) * HDIM],
            raised.astype(BF16),
            preferred_element_type=F32,
        )
        parts.append(out_t * (1.0 / total))
        lse_ref[0, 0, which : which + 1, :] = peak + jnp.log(total)
    o_ref[...] = jnp.concatenate(parts, axis=0).T.astype(BF16)


def attn_bwd_kernel(q_ref, k_ref, v_ref, do_ref, lse_ref, dq_ref, dk_ref, dv_ref, dk_acc, dv_acc):
    tile = pl.program_id(1)
    rows = q_ref.shape[0]
    scale = HDIM ** (-0.5)

    @pl.when(tile == 0)
    def _():
        dk_acc[...] = jnp.zeros_like(dk_acc)
        dv_acc[...] = jnp.zeros_like(dv_acc)

    queries = q_ref[...] * jnp.asarray(scale, BF16)
    d_out = do_ref[...]
    keys = k_ref[...]
    values = v_ref[...]
    keys_t = keys.astype(F32).T.astype(BF16)
    parts = []
    for which in range(2):
        mask = head_mask(rows, which)
        q_masked = jnp.where(mask, queries, jnp.zeros_like(queries))
        do_masked = jnp.where(mask, d_out, jnp.zeros_like(d_out))
        scores = nt_dot(keys, q_masked)
        probs = jnp.exp(scores - lse_ref[0, 0, which : which + 1, :])
        d_probs = nt_dot(values, do_masked)
        centre = jnp.sum(probs * d_probs, axis=0, keepdims=True)
        d_scores = (probs * (d_probs - centre)).astype(BF16)
        dv_acc[...] += jnp.dot(probs.astype(BF16), do_masked, preferred_element_type=F32)
        dk_acc[...] += jnp.dot(d_scores, q_masked, preferred_element_type=F32)
        parts.append(
            jnp.dot(
                keys_t[which * HDIM : (which + 1) * HDIM], d_scores, preferred_element_type=F32
            )
        )
    dq_ref[...] = (jnp.concatenate(parts, axis=0).T * scale).astype(BF16)

    @pl.when(tile == pl.num_programs(1) - 1)
    def _():
        dk_ref[...] = dk_acc[...].astype(BF16)
        dv_ref[...] = dv_acc[...].astype(BF16)


def query_rows(length):
    return length // 2 if length % 32 == 0 else length


def padded_columns(columns):
    return -(-columns // LANES) * LANES


def pad_heads(packed, pieces):
    columns = packed.shape[1] // pieces
    wide = padded_columns(columns)
    if wide == columns:
        return packed
    split = packed.reshape(packed.shape[0], pieces, columns)
    return jnp.pad(split, ((0, 0), (0, 0), (0, wide - columns))).reshape(
        packed.shape[0], pieces * wide
    )


def attention_forward(packed):
    length = packed.shape[0]
    columns = packed.shape[1] // 3
    wide = padded_columns(columns)
    pairs = wide // LANES
    rows = query_rows(length)
    tiles = length // rows
    packed = pad_heads(packed, 3)
    mixed, lse = pl.pallas_call(
        attn_fwd_kernel,
        grid=(pairs, tiles),
        in_specs=[
            pl.BlockSpec((rows, LANES), lambda p, t: (t, p)),
            pl.BlockSpec((length, LANES), lambda p, t: (0, pairs + p)),
            pl.BlockSpec((length, LANES), lambda p, t: (0, 2 * pairs + p)),
        ],
        out_specs=[
            pl.BlockSpec((rows, LANES), lambda p, t: (t, p)),
            pl.BlockSpec((1, 1, 8, rows), lambda p, t: (p, t, 0, 0)),
        ],
        out_shape=[
            jax.ShapeDtypeStruct((length, wide), BF16),
            jax.ShapeDtypeStruct((pairs, tiles, 8, rows), F32),
        ],
        compiler_params=pltpu.CompilerParams(vmem_limit_bytes=40 * 1024 * 1024),
        cost_estimate=pl.CostEstimate(
            flops=8 * length * length * wide,
            bytes_accessed=8 * length * wide,
            transcendentals=length * length * wide // HDIM,
        ),
    )(packed, packed, packed)
    return mixed[:, :columns], lse


def attention_backward(packed, d_mixed, lse):
    length = packed.shape[0]
    columns = packed.shape[1] // 3
    wide = padded_columns(columns)
    pairs = wide // LANES
    rows = query_rows(length)
    tiles = length // rows
    packed = pad_heads(packed, 3)
    d_mixed = pad_heads(d_mixed, 1)
    grads = pl.pallas_call(
        attn_bwd_kernel,
        grid=(pairs, tiles),
        in_specs=[
            pl.BlockSpec((rows, LANES), lambda p, t: (t, p)),
            pl.BlockSpec((length, LANES), lambda p, t: (0, pairs + p)),
            pl.BlockSpec((length, LANES), lambda p, t: (0, 2 * pairs + p)),
            pl.BlockSpec((rows, LANES), lambda p, t: (t, p)),
            pl.BlockSpec((1, 1, 8, rows), lambda p, t: (p, t, 0, 0)),
        ],
        out_specs=[
            pl.BlockSpec((rows, LANES), lambda p, t: (t, p)),
            pl.BlockSpec((length, LANES), lambda p, t: (0, p)),
            pl.BlockSpec((length, LANES), lambda p, t: (0, p)),
        ],
        out_shape=[jax.ShapeDtypeStruct((length, wide), BF16)] * 3,
        scratch_shapes=[pltpu.VMEM((length, LANES), F32)] * 2,
        compiler_params=pltpu.CompilerParams(vmem_limit_bytes=48 * 1024 * 1024),
        cost_estimate=pl.CostEstimate(
            flops=20 * length * length * wide,
            bytes_accessed=14 * length * wide,
            transcendentals=length * length * wide // HDIM,
        ),
    )(packed, packed, packed, d_mixed, lse)
    return jnp.concatenate([part[:, :columns] for part in grads], axis=1)


def normalized(values_in):
    centre = jnp.mean(values_in, axis=-1, keepdims=True)
    offsets = values_in - centre
    spread = jnp.mean(offsets * offsets, axis=-1, keepdims=True)
    factor = lax.rsqrt(spread + EPS)
    return offsets * factor, factor


def modulate(values_in, mod_rows, first):
    normal, _ = normalized(values_in)
    shift = mod_rows[:, first][:, None]
    scale = mod_rows[:, first + 1][:, None]
    return (normal * (1.0 + scale) + shift).astype(BF16)


def modulate_backward(values_in, d_out, mod_rows, first):
    normal, factor = normalized(values_in)
    scale = mod_rows[:, first + 1][:, None]
    d_shift = jnp.sum(d_out, axis=1)
    d_scale = jnp.sum(d_out * normal, axis=1)
    d_normal = d_out * (1.0 + scale)
    mean_plain = jnp.mean(d_normal, axis=-1, keepdims=True)
    mean_along = jnp.mean(d_normal * normal, axis=-1, keepdims=True)
    return (d_normal - mean_plain - normal * mean_along) * factor, d_shift, d_scale


def gelu_tanh(values_in):
    return jax.nn.gelu(values_in, approximate=True)


def tied(values, *others):
    return lax.optimization_barrier((values, *others))


def both(own, other):
    return jnp.concatenate([own, other], axis=0)


def rows_dot(rows, page):
    return dot32("...d,df->...f", rows, page)


def back_dot(rows, page):
    return dot32("...f,df->...d", rows, page)


def back_sum(rows_list, pages):
    return sum(back_dot(rows, page) for rows, page in zip(rows_list, pages))


def flat(values):
    return values.reshape(-1, values.shape[-1])


def row_major(values):
    return with_layout_constraint(values, Layout(major_to_minor=tuple(range(values.ndim))))


def page_grad(left, right):
    grad = lax.dot_general(
        flat(left), flat(right), (((0,), (0,)), ((), ())), preferred_element_type=F32
    )
    return row_major(grad.astype(BF16))


def token_halves(values, seqs):
    return values[:seqs], values[seqs:]


def to_attention(image_parts, text_parts):
    packed = [
        jnp.concatenate([image, text], axis=1) for image, text in zip(image_parts, text_parts)
    ]
    packed = jnp.stack(packed, axis=1)
    return packed.reshape(-1, *packed.shape[2:])


def from_attention(values, blocks, image_rows):
    values = values.reshape(-1, blocks, *values.shape[1:])
    image = [values[:, block, :image_rows] for block in range(blocks)]
    text = [values[:, block, image_rows:] for block in range(blocks)]
    return image, text


def forward_layer(streams, mods, weights, fetch):
    seqs, image_rows = streams[0].shape[:2]
    qkv_w, out_w, up_w, down_w = weights
    blocks = len(qkv_w[0])
    with jax.named_scope("attention"):
        normed = [modulate(streams[u], mods[u], 0) for u in range(2)]
        text_one = rows_of_all(normed[1])
        image_one = (normed[0], pair_swap(normed[0]))
        text_heads = rows_dot(text_one, qkv_w[1][0]).astype(BF16)
        text_heads = to_sequences(text_heads, blocks)
        image_heads = [
            both(*[rows_dot(part, page).astype(BF16) for part in image_one]) for page in qkv_w[0]
        ]
        packed = to_attention(image_heads, text_heads)
        tokens, columns = packed.shape[1:]
        next_attn = next_mlp = None
        if fetch:
            next_attn, packed = fetch[0](packed)
        packed = lax.all_to_all(packed, "dp", 0, 0, tiled=True)
        if fetch:
            next_attn, packed = attention_weights(next_attn, False, packed)
            next_mlp, packed = fetch[1](packed)
        packed = packed.reshape(-1, columns)
        mixed, lse = attention_forward(packed)
        mixed = mixed.reshape(-1, tokens, columns // 3)
        mixed = lax.all_to_all(mixed, "dp", 0, 0, tiled=True)
        if fetch:
            next_mlp, mixed = mlp_weights(next_mlp, mixed)
        image_mixed, text_mixed = from_attention(mixed, blocks, image_rows)
        text_mixed = to_blocks(text_mixed, seqs)
        other = back_sum([part[seqs:] for part in image_mixed], out_w[0])
        text_terms = back_dot(text_mixed, out_w[1][0])
        own = back_sum([part[:seqs] for part in image_mixed], out_w[0])
        attn = [pair_sum(own, other), sum_of_all(text_terms)]
    with jax.named_scope("mlp"):
        middle = [streams[u] + mods[u][:, 2][:, None] * attn[u] for u in range(2)]
        normed_two = [modulate(middle[u], mods[u], 3) for u in range(2)]
        text_two = rows_of_all(normed_two[1])
        image_two = (normed_two[0], pair_swap(normed_two[0]))
        image_up = [[rows_dot(part, page) for page in up_w[0]] for part in image_two]
        image_act = [[gelu_tanh(up).astype(BF16) for up in part] for part in image_up]
        other = back_sum(image_act[1], down_w[0])
        text_up = rows_dot(text_two, up_w[1][0])
        text_act = gelu_tanh(text_up).astype(BF16)
        text_terms = back_dot(text_act, down_w[1][0])
        own = back_sum(image_act[0], down_w[0])
        mlp = [pair_sum(own, other), sum_of_all(text_terms)]
        result = [middle[u] + mods[u][:, 5][:, None] * mlp[u] for u in range(2)]
    saved = dict(
        streams=streams,
        image_one=both(*image_one),
        text_one=text_one,
        packed=packed,
        lse=lse,
        image_mixed=image_mixed,
        text_mixed=text_mixed,
        attn=attn,
        middle=middle,
        image_two=both(*image_two),
        text_two=text_two,
        image_up=image_up,
        image_act=[both(*parts) for parts in zip(*image_act)],
        text_up=text_up,
        text_act=text_act,
        mlp=mlp,
    )
    return result, saved, (next_attn, next_mlp)


def gelu_pull(up_values, d_active):
    return jax.vjp(gelu_tanh, up_values)[1](d_active)[0].astype(BF16)


def scatter_pages(grads, after):
    wide, after = tied(jnp.concatenate(grads, axis=1), after)
    return lax.psum_scatter(wide, "dp", scatter_dimension=0, tiled=True), after


def shard_rows(slab, width, blocks):
    image = slab[:, :width].astype(F32)
    for block in range(1, blocks):
        part = slab[:, (block + 1) * width : (block + 2) * width]
        image = image + hi_swap(part, block).astype(F32)
    return image, slab[:, width : 2 * width].astype(F32)


def page_list(image_first, image_second, text_first, text_second):
    pages = [image_first[0], image_second[0], text_first, text_second]
    for pair in zip(image_first[1:], image_second[1:]):
        pages += pair
    return pages


def mlp_shard(slab, blocks):
    width = slab.shape[1] // (blocks + 1)
    rows = shard_rows(slab, width, blocks)
    half = width // 2
    return (
        jnp.stack([part[:, half:] for part in rows]),
        jnp.stack([part[:, :half].T for part in rows]),
    )


def attention_shard(slab, blocks):
    width = slab.shape[1] // (blocks + 1)
    rows = shard_rows(slab, width, blocks)
    columns = width // 4
    return (
        jnp.stack(
            [
                part[:, : 3 * columns].reshape(-1, 3, columns).transpose(1, 0, 2)
                for part in rows
            ]
        ),
        jnp.stack([part[:, 3 * columns :].T for part in rows]),
    )


def backward_layer(grads_out, mods, weights, saved, pending):
    seqs, image_rows = grads_out[0].shape[:2]
    qkv_w, out_w, up_w, down_w = weights
    blocks = len(qkv_w[0])
    middle, attn, mlp = saved["middle"], saved["attn"], saved["mlp"]
    with jax.named_scope("mlp_grad"):
        gated = [(mods[u][:, 5][:, None] * grads_out[u]).astype(BF16) for u in range(2)]
        text_dmlp = rows_of_all(gated[1])
        image_dmlp = (gated[0], pair_swap(gated[0]))
        d_gate_two = [jnp.sum(grads_out[u] * mlp[u], axis=1) for u in range(2)]
        image_dup = [
            [
                gelu_pull(saved["image_up"][at][block], rows_dot(image_dmlp[at], down_w[0][block]))
                for block in range(blocks)
            ]
            for at in range(2)
        ]
        other = back_sum(image_dup[1], up_w[0])
        text_dup = gelu_pull(saved["text_up"], rows_dot(text_dmlp, down_w[1][0]))
        text_terms = back_dot(text_dup, up_w[1][0])
        own = back_sum(image_dup[0], up_w[0])
        dmlp_rows = both(*image_dmlp)
        received = pair_swap(other.astype(BF16))
        grads = page_list(
            [page_grad(dmlp_rows, act) for act in saved["image_act"]],
            [page_grad(saved["image_two"], both(*parts)) for parts in zip(*image_dup)],
            page_grad(text_dmlp, saved["text_act"]),
            page_grad(saved["text_two"], text_dup),
        )
        mlp_slab, received = scatter_pages(grads, received)
        d_two = [own + received.astype(F32), sum_of_all(text_terms)]
        d_middle, d_shift_two, d_scale_two = [], [], []
        for u in range(2):
            d_values, d_shift, d_scale = modulate_backward(middle[u], d_two[u], mods[u], 3)
            d_middle.append(grads_out[u] + d_values)
            d_shift_two.append(d_shift)
            d_scale_two.append(d_scale)
    with jax.named_scope("attention_grad"):
        gated = [(mods[u][:, 2][:, None] * d_middle[u]).astype(BF16) for u in range(2)]
        text_dattn = rows_of_all(gated[1])
        image_dattn = (gated[0], pair_swap(gated[0]))
        d_gate_one = [jnp.sum(d_middle[u] * attn[u], axis=1) for u in range(2)]
        text_dmixed = to_sequences(rows_dot(text_dattn, out_w[1][0]).astype(BF16), blocks)
        image_dmixed = [
            both(*[rows_dot(part, page).astype(BF16) for part in image_dattn]) for page in out_w[0]
        ]
        d_mixed = to_attention(image_dmixed, text_dmixed)
        tokens, columns = d_mixed.shape[1:]
        d_mixed = lax.all_to_all(d_mixed, "dp", 0, 0, tiled=True)
        done = []
        if pending:
            mlp_before, d_mixed = tied(pending[0], d_mixed)
            done.append(mlp_shard(mlp_before, blocks))
        d_mixed = d_mixed.reshape(-1, columns)
        d_packed = attention_backward(saved["packed"], d_mixed, saved["lse"])
        d_packed = d_packed.reshape(-1, tokens, 3 * columns)
        d_packed = lax.all_to_all(d_packed, "dp", 0, 0, tiled=True)
        if pending:
            done[0], attn_before, d_packed = tied(done[0], pending[1], d_packed)
            done.append(attention_shard(attn_before, blocks))
        image_dproj, text_dproj = from_attention(d_packed, blocks, image_rows)
        text_dproj = to_blocks(text_dproj, seqs)
        other = back_sum([part[seqs:] for part in image_dproj], qkv_w[0])
        received = pair_swap(other.astype(BF16))
        text_terms = back_dot(text_dproj, qkv_w[1][0])
        own = back_sum([part[:seqs] for part in image_dproj], qkv_w[0])
        dattn_rows = both(*image_dattn)
        grads = page_list(
            [page_grad(saved["image_one"], part) for part in image_dproj],
            [page_grad(dattn_rows, part) for part in saved["image_mixed"]],
            page_grad(saved["text_one"], text_dproj),
            page_grad(text_dattn, saved["text_mixed"]),
        )
        attn_slab, (mlp_slab, done) = scatter_pages(grads, (mlp_slab, done))
        d_one = [own + received.astype(F32), sum_of_all(text_terms)]
        d_inputs, d_mods = [], []
        for u in range(2):
            d_values, d_shift, d_scale = modulate_backward(
                saved["streams"][u], d_one[u], mods[u], 0
            )
            d_inputs.append(d_middle[u] + d_values)
            d_mods.append(
                jnp.stack(
                    [d_shift, d_scale, d_gate_one[u], d_shift_two[u], d_scale_two[u], d_gate_two[u]],
                    axis=1,
                )
            )
    return d_inputs, jnp.stack(d_mods), (mlp_slab, attn_slab), done


def with_blocks(pages):
    hi_count = lax.axis_size("tensor") // 2
    return [pages] + [hi_swap(pages, block) for block in range(1, hi_count)]


def gather_pages(pages):
    return lax.all_gather(pages, "dp", axis=1, tiled=True)


def attn_page(w_qkv, w_out, layer_at, u):
    qkv = w_qkv[layer_at, u].transpose(1, 0, 2)
    qkv = qkv.reshape(qkv.shape[0], -1)
    return jnp.concatenate([qkv, w_out[layer_at, u].T], axis=1)


def attention_shards(w_qkv, w_out, layer_at, after):
    own = [attn_page(w_qkv, w_out, layer_at, u)[None] for u in range(2)]
    own, after = tied(own, after)
    lists = with_blocks(own[0])
    return [lists[0], own[1], *lists[1:]], after


def attention_weights(lists, split, after):
    lists, after = tied(lists, after)
    if split:
        first = gather_pages(jnp.concatenate(lists[:2], axis=0))
        rest, first = tied(lists[2:], first)
        rest = gather_pages(jnp.concatenate(rest, axis=0))
        pages = [first[0], first[1]] + [rest[at] for at in range(len(lists) - 2)]
    else:
        whole = gather_pages(jnp.concatenate(lists, axis=0))
        pages = [whole[at] for at in range(len(lists))]
    qkv_columns = lists[0].shape[2] * 3 // 4
    by_stream = [[pages[0], *pages[2:]], [pages[1]]]
    qkv_w = [[page[:, :qkv_columns] for page in group] for group in by_stream]
    out_w = [[page[:, qkv_columns:] for page in group] for group in by_stream]
    return (qkv_w, out_w), after


def mlp_shards(w_up, w_down, layer_at, after):
    own = [jnp.stack([w_up[layer_at, u], w_down[layer_at, u].T]) for u in range(2)]
    own, after = tied(own, after)
    return with_blocks(own[0]) + [own[1]], after


def mlp_weights(lists, after):
    lists, after = tied(lists, after)
    blocks = len(lists) - 1
    whole = gather_pages(jnp.concatenate(lists, axis=0))
    up_w = [[whole[2 * at] for at in range(blocks)], [whole[2 * blocks]]]
    down_w = [[whole[2 * at + 1] for at in range(blocks)], [whole[2 * blocks + 1]]]
    return (up_w, down_w), after


def per_device(
    image_in,
    text_in,
    cond_table,
    cond_index,
    w_mod,
    w_qkv,
    w_out,
    w_up,
    w_down,
    cot_image,
    cot_text,
):
    n_tensor = lax.axis_size("tensor")
    dp_at = lax.axis_index("dp")
    micro_count, own_rows = image_in.shape[:2]
    seqs = micro_count * own_rows
    model_width = image_in.shape[3]
    layer_count = w_qkv.shape[0]
    slab_rows = w_mod.shape[2]
    column_count = w_mod.shape[3]
    index_flat = cond_index.reshape(-1)
    attn_w, _ = attention_weights(attention_shards(w_qkv, w_out, 0, ())[0], True, ())
    mlp_lists, _ = mlp_shards(w_up, w_down, 0, ())
    with jax.named_scope("modulation"):
        onehot = (
            index_flat[:, None] == jnp.arange(cond_table.shape[0], dtype=jnp.int32)[None, :]
        ).astype(F32)
        cond_slab = lax.dynamic_slice_in_dim(cond_table, dp_at * slab_rows, slab_rows, 1)
        cond_slab = jnp.dot(onehot, cond_slab, precision=HIGHEST, preferred_element_type=F32)
        silu_slab = jax.nn.silu(cond_slab).astype(BF16)
        partial_mod = dot32("sd,lmdc->lmsc", silu_slab, w_mod)
        partial_mod = partial_mod.reshape(
            layer_count * 2, micro_count, n_tensor, own_rows * column_count
        )
        partial_mod = partial_mod.transpose(2, 0, 1, 3).reshape(n_tensor, -1, column_count)
        partial_mod = dp_sum(lax.all_to_all(partial_mod, "tensor", 0, 0, tiled=True))
        mod_own = partial_mod.transpose(1, 0, 2)
        mod_own = mod_own.reshape(layer_count, 2, seqs, 6, model_width)
    mlp_w, mod_own = mlp_weights(mlp_lists, mod_own)
    mods = [[mod_own[layer_at, u] for u in range(2)] for layer_at in range(layer_count)]

    def rows_in(values):
        return values.reshape(seqs, values.shape[2], model_width).astype(F32)

    def rows_out(values):
        return values.reshape(micro_count, own_rows, values.shape[1], model_width)

    streams = [rows_in(image_in), rows_in(text_in)]
    saved, weights = [], []
    for layer_at in range(layer_count):
        weights.append((*attn_w, *mlp_w))
        fetch = None
        if layer_at + 1 < layer_count:
            fetch = (
                functools.partial(attention_shards, w_qkv, w_out, layer_at + 1),
                functools.partial(mlp_shards, w_up, w_down, layer_at + 1),
            )
        streams, kept, (attn_w, mlp_w) = forward_layer(
            streams, mods[layer_at], weights[layer_at], fetch
        )
        saved.append(kept)
    grads_now = [rows_in(cot_image), rows_in(cot_text)]
    shards = [None] * layer_count
    d_cond_terms = []
    grad_w_mod = [None] * layer_count
    pending = None
    for layer_at in reversed(range(layer_count)):
        grads_now, d_mods, slabs, done = backward_layer(
            grads_now, mods[layer_at], weights[layer_at], saved[layer_at], pending
        )
        if pending:
            shards[layer_at + 1] = done
        pending = slabs
        with jax.named_scope("modulation_grad"):
            d_mods = d_mods.reshape(2 * seqs, n_tensor, column_count).transpose(1, 0, 2)
            d_mods = dp_sum(lax.all_to_all(d_mods, "tensor", 0, 0, tiled=True))
            d_mods = d_mods.reshape(n_tensor, 2, micro_count, own_rows, column_count)
            d_mods = d_mods.transpose(1, 2, 0, 3, 4)
            d_columns = d_mods.reshape(2, micro_count * n_tensor * own_rows, column_count)
            grad_w_mod[layer_at] = jnp.einsum(
                "sd,msc->mdc",
                silu_slab.astype(F32),
                d_columns,
                precision=HIGHEST,
                preferred_element_type=F32,
            )
            d_cond_terms.append(
                jnp.einsum(
                    "msc,mdc->sd",
                    d_columns,
                    w_mod[layer_at].astype(F32),
                    precision=HIGHEST,
                    preferred_element_type=F32,
                )
            )
    with jax.named_scope("conditioning_grad"):
        d_silu = sum(d_cond_terms)
        d_cond = jax.vjp(jax.nn.silu, cond_slab)[1](d_silu)[0]
        grad_cond = lax.psum(
            jnp.dot(onehot.T, d_cond, precision=HIGHEST, preferred_element_type=F32), "tensor"
        )
    with jax.named_scope("weight_grads"):
        blocks = n_tensor // 2
        shards[0] = (mlp_shard(pending[0], blocks), attention_shard(pending[1], blocks))
        stacked = [
            jnp.stack([layer[part][at] for layer in shards])
            for part, at in ((1, 0), (1, 1), (0, 0), (0, 1))
        ]
    return (
        rows_out(streams[0].astype(BF16)),
        rows_out(streams[1].astype(BF16)),
        rows_out(grads_now[0]),
        rows_out(grads_now[1]),
        grad_cond,
        jnp.stack(grad_w_mod),
        *stacked,
    )


def solution(mesh):
    rows = P(None, "tensor", "dp", None)
    up_like = P(None, None, "dp", "tensor")
    down_like = P(None, None, "tensor", "dp")
    qkv_like = P(None, None, None, "dp", "tensor")
    return jax.shard_map(
        per_device,
        mesh=mesh,
        in_specs=(
            rows,
            rows,
            P(),
            P(),
            up_like,
            qkv_like,
            down_like,
            up_like,
            down_like,
            rows,
            rows,
        ),
        out_specs=(
            rows,
            rows,
            rows,
            rows,
            P(None, "dp"),
            up_like,
            qkv_like,
            down_like,
            up_like,
            down_like,
        ),
        check_vma=False,
    )
```

time: 4300 us -> 1620 us (0.38)
  waiting for transfers between devices: 2040 us -> 698 us
  local copies, waits for them, and re-layouts: 681 us -> 102 us
  matrix products: 856 us -> 355 us
  other arithmetic: 354 us -> 103 us
  blocking collectives: 329 us -> 86.7 us
  starting transfers between devices: 6.33 us -> 156 us
  Pallas kernels: 0 us -> 90.6 us
    reduce_scatter x22 -> x4, waiting for transfers between devices: 956 us -> 0.03 us  [scatter_pages(): lax.psum_scatter(wide, 'dp', scatter_dimension=0, tiled=True)]
    dot_general x125 -> x111, matrix products: 856 us -> 355 us  [the longest x81 246 us: dot32(): return jnp.einsum(pattern, left, right, preferred_element_type=F32)]
    all_gather x28 -> x5, waiting for transfers between devices: 511 us -> 60.2 us  [gather_pages(): return lax.all_gather(pages, 'dp', axis=1, tiled=True)]
    ppermute x0 -> x89, waiting for transfers between devices: none -> 391 us  [the longest x80 354 us: tensor_swap(): lax.ppermute(values, 'tensor', [(i, i ^ distance) for i in range(count)])]
    unnamed x64 -> x9, waiting for transfers between devices: 326 us -> 0.15 us
    all_gather x20 -> x0, blocking collectives: 317 us -> none  [the longest x8 132 us: gather_grads(): lax.all_gather(shortened(stream_pair), 'tensor', axis=0, tiled=True)]
    unnamed x772 -> x640, local copies, waits for them, and re-layouts: 283 us -> 33.1 us
    all_to_all x0 -> x8, waiting for transfers between devices: none -> 246 us  [the longest x2 92.9 us: forward_layer(): packed = lax.all_to_all(packed, 'dp', 0, 0, tiled=True)]
  transfers between devices with their start and end apart: 58 -> 106, of which waited for: 44 -> 54; matrix products, arithmetic and copies ran while one was open for 27% -> 32% of each run, Pallas kernels for 0% -> 6%
where the time goes in v1:
time: 1620 us; the launch traced here: 1610 us
  waiting for transfers between devices  698 us (43%)
  matrix products  355 us (22%)
  starting transfers between devices  156 us (10%)
  other arithmetic  103 us (6%)
  local copies, waits for them, and re-layouts  102 us (6%)
  Pallas kernels  90.6 us (6%)
  blocking collectives  86.7 us (5%)
  between operations  19 us (1%)
    ppermute x80, waiting for transfers between devices, tensor_swap(): lax.ppermute(values, 'tensor', [(i, i ^ distance) for i in range(count)])  354 us
    dot_general x81, matrix products, dot32(): return jnp.einsum(pattern, left, right, preferred_element_type=F32)  246 us
    ppermute x80, starting transfers between devices, tensor_swap(): lax.ppermute(values, 'tensor', [(i, i ^ distance) for i in range(count)])  109 us
    dot_general x24, matrix products, page_grad(): lax.dot_general(flat(left), flat(right), (((0,), (0,)), ((), ())), prefer...  98.8 us
    all_to_all x2, waiting for transfers between devices, forward_layer(): packed = lax.all_to_all(packed, 'dp', 0, 0, tiled=True)  92.9 us
    all_to_all x2, waiting for transfers between devices, backward_layer(): d_packed = lax.all_to_all(d_packed, 'dp', 0, 0, tiled=True)  86.3 us
    all_gather x5, waiting for transfers between devices, gather_pages(): return lax.all_gather(pages, 'dp', axis=1, tiled=True)  60.2 us
    pallas_call x2, Pallas kernels, attention_backward(): pl.pallas_call(attn_bwd_kernel, grid=(pairs, tiles), in_specs=[pl.BlockSp...  58.3 us
  transfers between devices with their start and end apart: 106, of which 54 were waited for; matrix products, arithmetic and copies ran while one was open for 32% of the time, Pallas kernels for 6%

profile of v1, /device:TPU:0, one launch (start us, length us, event | category | flops | bytes accessed | tf_op | source)
XLA Modules:
  0.0 1609.8 jit_solution(6230913640246206902)
XLA Ops:
  15.8 26.0 %collective-permute-done.4 = bf16[1,192,1536]{2,1,0:T(8,128)(2,1)S(1)} collective-permute-done((bf16[1,192,1536]{2,1,0:T(8,128)(2,1)S(1)}, bf16[1,192,1536]{2,1,0:T(8,128)(2,1)S(1)}, u32[]{:S(2)}, u32[]{:S(2)}) %collective-permute-start.4) | collective-permute-done | bytes 589856 | tf_op jit(solution)/shard_map/ppermute | solution.py:25
  43.0 60.1 %all-gather.6.cloned.1.call-done = bf16[2,1536,1536]{2,1,0:T(8,128)(2,1)} async-done(((bf16[2,192,1536]{2,1,0:T(8,128)(2,1)}), bf16[2,1536,1536]{2,1,0:T(8,128)(2,1)}) %all-gather.6.cloned.1.call-update) | async-done | bytes 9437200 | tf_op jit(solution)/shard_map/all_gather | solution.py:536
  112.9 8.7 all-to-all-done
  126.4 12.1 collective-permute-done.2
  139.0 10.1 collective-permute-done.3
  149.4 30.6 %collective-permute-done = bf16[2,192,1536]{2,1,0:T(8,128)(2,1)} collective-permute-done((bf16[2,192,1536]{2,1,0:T(8,128)(2,1)S(1)}, bf16[2,192,1536]{2,1,0:T(8,128)(2,1)}, u32[]{:S(2)}, u32[]{:S(2)}) %collective-permute-start) | collective-permute-done | bytes 1179680 | tf_op jit(solution)/shard_map/ppermute | solution.py:25
  211.3 11.2 collective-permute-done.5
  237.9 28.6 %collective-permute-done.10 = bf16[1,192,1536]{2,1,0:T(8,128)(2,1)} collective-permute-done((bf16[1,192,1536]{2,1,0:T(8,128)(2,1)}, bf16[1,192,1536]{2,1,0:T(8,128)(2,1)}, u32[]{:S(2)}, u32[]{:S(2)}) %collective-permute-start.10) | collective-permute-done | bytes 589856 | tf_op jit(solution)/shard_map/attention/ppermute | solution.py:25
  266.5 35.4 %all-to-all-done.1 = bf16[8,148,1152]{2,1,0:T(8,128)(2,1)S(1)} async-done(((bf16[8,148,1152]{2,1,0:T(8,128)(2,1)}), bf16[8,148,1152]{2,1,0:T(8,128)(2,1)S(1)}, u32[]{:S(2)}, u32[]{:S(2)}) %all-to-all-start.1) | async-done | bytes 2727968 | tf_op jit(solution)/shard_map/attention/all_to_all | solution.py:340
  312.8 16.2 %attention.2 = (bf16[1184,384]{1,0:T(8,128)(2,1)S(1)}, f32[3,2,8,592]{3,2,1,0:T(8,128)S(1)}) custom-call(bf16[1184,1152]{1,0:T(8,128)(2,1)S(1)} %reshape.471.q_ref.k_ref.v_ref, bf16[1184,1152]{1,0:T(8,128)(2,1)S(1)} %reshape.471.q_ref.k_ref.v_ref, bf16[1184,1152]{1,0:T(8,128)(2,1)S(1)} %reshape.471.q_ref.k_ref.v_ref), custom_call_target="tpu_custom_call" | custom-call | flops 4306501632 | bytes 3637248 | tf_op jit(solution)/shard_map/attention/pallas_call | solution.py:176
  331.3 26.4 %all_to_all.55 = bf16[8,148,384]{2,1,0:T(8,128)(2,1)S(1)} all-to-all(bf16[8,148,384]{2,1,0:T(8,128)(2,1)S(1)} %reshape.472), channel_id=1, replica_groups=mesh['dp'=8,'tensor'=4] {'dp'}, dimensions={0} | all-to-all | bytes 1818624 | tf_op jit(solution)/shard_map/attention/all_to_all | solution.py:347
  381.2 7.3 collective-permute-done.18
  388.9 14.0 collective-permute-done.12
  412.2 18.0 %collective-permute-done.13 = bf16[2,128,1536]{2,1,0:T(8,128)(2,1)} collective-permute-done((bf16[2,128,1536]{2,1,0:T(8,128)(2,1)S(1)}, bf16[2,128,1536]{2,1,0:T(8,128)(2,1)}, u32[]{:S(2)}, u32[]{:S(2)}) %collective-permute-start.13) | collective-permute-done | bytes 786464 | tf_op jit(solution)/shard_map/mlp/ppermute | solution.py:25
  490.5 5.9 slice_bitcast_fusion.6
  503.6 6.9 collective-permute-done.15
  527.2 57.5 %all-to-all-done.3 = bf16[8,148,1152]{2,1,0:T(8,128)(2,1)} async-done(((bf16[8,148,1152]{2,1,0:T(8,128)(2,1)}), bf16[8,148,1152]{2,1,0:T(8,128)(2,1)}, u32[]{:S(2)}, u32[]{:S(2)}) %all-to-all-start.3) | async-done | bytes 2727968 | tf_op jit(solution)/shard_map/attention/all_to_all | solution.py:340
  587.4 16.2 %attention.3 = (bf16[1184,384]{1,0:T(8,128)(2,1)S(1)}, f32[3,2,8,592]{3,2,1,0:T(8,128)S(1)}) custom-call(bf16[1184,1152]{1,0:T(8,128)(2,1)S(1)} %reshape.477.q_ref.k_ref.v_ref, bf16[1184,1152]{1,0:T(8,128)(2,1)S(1)} %reshape.477.q_ref.k_ref.v_ref, bf16[1184,1152]{1,0:T(8,128)(2,1)S(1)} %reshape.477.q_ref.k_ref.v_ref), custom_call_target="tpu_custom_call" | custom-call | flops 4306501632 | bytes 3637248 | tf_op jit(solution)/shard_map/attention/pallas_call | solution.py:176
  612.1 12.3 all-to-all-done.4
  646.4 30.4 %collective-permute-done.30 = bf16[2,128,1536]{2,1,0:T(8,128)(2,1)S(1)} collective-permute-done((bf16[2,128,1536]{2,1,0:T(8,128)(2,1)S(1)}, bf16[2,128,1536]{2,1,0:T(8,128)(2,1)S(1)}, u32[]{:S(2)}, u32[]{:S(2)}) %collective-permute-start.30) | collective-permute-done | bytes 786464 | tf_op jit(solution)/shard_map/attention/ppermute | solution.py:25
  684.4 15.8 collective-permute-done.31
  732.9 6.7 fusion.4
  744.1 5.9 fusion.5
  767.6 5.9 fusion.6
  822.3 9.1 collective-permute-done.41
  840.8 6.1 collective-permute-done.53
  849.0 5.6 multiply_reduce_fusion.3
  863.1 9.4 collective-permute-done.48
  874.1 38.4 %all_to_all.56 = bf16[8,148,384]{2,1,0:T(8,128)(2,1)} all-to-all(bf16[8,148,384]{2,1,0:T(8,128)(2,1)S(1)} %bitcast.1205), channel_id=1, replica_groups=mesh['dp'=8,'tensor'=4] {'dp'}, dimensions={0} | all-to-all | bytes 1818624 | tf_op jit(solution)/shard_map/attention_grad/all_to_all | solution.py:488
  913.9 29.2 %attention_grad.2 = (bf16[1184,384]{1,0:T(8,128)(2,1)S(1)}, bf16[1184,384]{1,0:T(8,128)(2,1)S(1)}, bf16[1184,384]{1,0:T(8,128)(2,1)S(1)}) custom-call(bf16[1184,1152]{1,0:T(8,128)(2,1)} %copy-done.3, bf16[1184,1152]{1,0:T(8,128)(2,1)} %copy-done.3, bf16[1184,1152]{1,0:T(8,128)(2,1)} %copy-done.3, bf16[1184,384]{1,0:T(8,128)(2,1)S(1)} %reshape.485.do_ref, ...), custom_call_target="tpu_custom_call" | custom-call | flops 10766254080 | bytes 6365184 | tf_op jit(solution)/shard_map/attention_grad/pallas_call | solution.py:211
  958.3 36.1 %all-to-all-done.6 = bf16[8,148,1152]{2,1,0:T(8,128)(2,1)} async-done(((bf16[8,148,1152]{2,1,0:T(8,128)(2,1)}), bf16[8,148,1152]{2,1,0:T(8,128)(2,1)}, u32[]{:S(2)}, u32[]{:S(2)}) %all-to-all-start.6) | async-done | bytes 2727968 | tf_op jit(solution)/shard_map/attention_grad/all_to_all | solution.py:496
  1050.2 14.0 collective-permute-done.62
  1087.1 6.8 collective-permute-done.57
  1102.8 5.9 fusion.8
  1127.3 5.6 fusion.11
  1158.8 8.5 collective-permute-done.71
  1187.4 15.9 collective-permute-done.66
  1205.7 9.0 all-to-all-start.7
  1220.2 19.0 %all-to-all-done.7 = bf16[8,148,384]{2,1,0:T(8,128)(2,1)} async-done(((bf16[8,148,384]{2,1,0:T(8,128)(2,1)}), bf16[8,148,384]{2,1,0:T(8,128)(2,1)}, u32[]{:S(2)}, u32[]{:S(2)}) %all-to-all-start.7) | async-done | bytes 909344 | tf_op jit(solution)/shard_map/attention_grad/all_to_all | solution.py:488
  1247.2 29.1 %attention_grad.3 = (bf16[1184,384]{1,0:T(8,128)(2,1)S(1)}, bf16[1184,384]{1,0:T(8,128)(2,1)S(1)}, bf16[1184,384]{1,0:T(8,128)(2,1)S(1)}) custom-call(bf16[1184,1152]{1,0:T(8,128)(2,1)} %copy-done.2, bf16[1184,1152]{1,0:T(8,128)(2,1)} %copy-done.2, bf16[1184,1152]{1,0:T(8,128)(2,1)} %copy-done.2, bf16[1184,384]{1,0:T(8,128)(2,1)S(1)} %reshape.493.do_ref, ...), custom_call_target="tpu_custom_call" | custom-call | flops 10766254080 | bytes 6365184 | tf_op jit(solution)/shard_map/attention_grad/pallas_call | solution.py:211
  1288.9 6.5 collective-permute-done.74
  1300.6 50.2 %all-to-all-done.8 = bf16[8,148,1152]{2,1,0:T(8,128)(2,1)} async-done(((bf16[8,148,1152]{2,1,0:T(8,128)(2,1)}), bf16[8,148,1152]{2,1,0:T(8,128)(2,1)}, u32[]{:S(2)}, u32[]{:S(2)}) %all-to-all-start.8) | async-done | bytes 2727968 | tf_op jit(solution)/shard_map/attention_grad/all_to_all | solution.py:496
  1368.9 19.5 %collective-permute-done.76 = bf16[2,2,20,1152]{3,2,1,0:T(8,128)(2,1)S(1)} collective-permute-done((bf16[2,2,20,1152]{3,2,1,0:T(8,128)(2,1)S(1)}, bf16[2,2,20,1152]{3,2,1,0:T(8,128)(2,1)S(1)}, u32[]{:S(2)}, u32[]{:S(2)}) %collective-permute-start.76) | collective-permute-done | bytes 184352 | tf_op jit(solution)/shard_map/attention_grad/ppermute | solution.py:25
  1411.5 9.4 all_to_all.57
  1470.0 14.1 collective-permute-done.75
  1496.8 26.7 %all-to-all-done.10 = f32[4,4,2304]{2,1,0:T(4,128)S(1)} async-done(((f32[4,4,2304]{2,1,0:T(4,128)}), f32[4,4,2304]{2,1,0:T(4,128)S(1)}, u32[]{:S(2)}, u32[]{:S(2)}) %all-to-all-start.10) | async-done | bytes 147488 | tf_op jit(solution)/shard_map/modulation_grad/all_to_all | solution.py:660
  1539.7 12.5 psum.7
  1576.7 16.9 %collective-permute-done.87 = bf16[192,1536]{1,0:T(8,128)(2,1)S(1)} collective-permute-done((bf16[192,1536]{1,0:T(8,128)(2,1)}, bf16[192,1536]{1,0:T(8,128)(2,1)S(1)}, u32[]{:S(2)}, u32[]{:S(2)}) %collective-permute-start.87) | collective-permute-done | bytes 589856 | tf_op jit(solution)/shard_map/weight_grads/ppermute | solution.py:25
  (1185 shorter events, 719.1 us)
Async XLA Ops:
  7.2 96.0 %all-gather.6.cloned.1.call-start = ((), (), s32[]{:S(2)}) async-start(), calls=%async_computation.15 | async-start | bytes 10616832 | tf_op jit(solution)/shard_map/all_gather | solution.py:536
  11.7 30.1 %collective-permute-start.4 = (bf16[1,192,1536]{2,1,0:T(8,128)(2,1)S(1)}, bf16[1,192,1536]{2,1,0:T(8,128)(2,1)S(1)}, u32[]{:S(2)}, u32[]{:S(2)}) collective-permute-start(bf16[1,192,1536]{2,1,0:T(8,128)(2,1)S(1)} %get-tuple-element.71), channel_id=1, source_target_pairs={{0,2},{1,3},{2,0},{3,1},{4,6},{5,7},{6,4},{7,5},{8,10},{9,11},{10,... | collective-permute-start | bytes 1769480 | tf_op jit(solution)/shard_map/ppermute | solution.py:25
  43.0 182.0 %all-gather.8.cloned.1.call-start = ((), (), s32[]{:S(2)}) async-start(), calls=%async_computation.16 | async-start | bytes 5308416 | tf_op jit(solution)/shard_map/all_gather | solution.py:536
  111.7 318.5 %all-gather.10.cloned.1.call-start = ((), (), s32[]{:S(2)}) async-start(), calls=%async_computation.17 | async-start | bytes 31850496 | tf_op jit(solution)/shard_map/all_gather | solution.py:536
  126.3 53.7 %collective-permute-start = (bf16[2,192,1536]{2,1,0:T(8,128)(2,1)S(1)}, bf16[2,192,1536]{2,1,0:T(8,128)(2,1)}, u32[]{:S(2)}, u32[]{:S(2)}) collective-permute-start(bf16[2,192,1536]{2,1,0:T(8,128)(2,1)S(1)} %get-tuple-element.84), channel_id=1, source_target_pairs={{0,2},{1,3},{2,0},{3,1},{4,6},{5,7},{6,4},{7,5},{8,10},{9,11},{10,... | collective-permute-start | bytes 3538952 | tf_op jit(solution)/shard_map/ppermute | solution.py:25
  194.3 28.2 %collective-permute-start.5 = (bf16[2,128,1536]{2,1,0:T(8,128)(2,1)}, bf16[2,128,1536]{2,1,0:T(8,128)(2,1)}, u32[]{:S(2)}, u32[]{:S(2)}) collective-permute-start(bf16[2,128,1536]{2,1,0:T(8,128)(2,1)} %fusion.108), channel_id=1, source_target_pairs={{0,1},{1,0},{2,3},{3,2},{4,5},{5,4},{6,7},{7,6},{8,9},{9,8},{10,11... | collective-permute-start | bytes 2359304 | tf_op jit(solution)/shard_map/attention/ppermute | solution.py:25
  205.8 25.2 %collective-permute-start.9 = (bf16[2,2,20,1152]{3,2,1,0:T(8,128)(2,1)}, bf16[2,2,20,1152]{3,2,1,0:T(8,128)(2,1)}, u32[]{:S(2)}, u32[]{:S(2)}) collective-permute-start(bf16[2,2,20,1152]{3,2,1,0:T(8,128)(2,1)} %get-tuple-element.296), channel_id=1, source_target_pairs={{0,2},{1,3},{2,0},{3,1},{4,6},{5,7},{6,4},{7,5},{8,10},{9,11},{10,... | collective-permute-start | bytes 552968 | tf_op jit(solution)/shard_map/attention/ppermute | solution.py:25
  234.1 67.8 %all-to-all-start.1 = ((bf16[8,148,1152]{2,1,0:T(8,128)(2,1)}), bf16[8,148,1152]{2,1,0:T(8,128)(2,1)S(1)}, u32[]{:S(2)}, u32[]{:S(2)}) async-start(bf16[8,148,1152]{2,1,0:T(8,128)(2,1)} %bitcast.1171), calls=%async_computation.1 | async-start | bytes 5603328 | tf_op jit(solution)/shard_map/attention/all_to_all | solution.py:340
  237.8 252.7 %all-gather.12.cloned.1.call-start = ((), (), s32[]{:S(2)}) async-start(), calls=%async_computation.18 | async-start | bytes 15925248 | tf_op jit(solution)/shard_map/attention/all_gather | solution.py:536
  237.8 28.7 %collective-permute-start.10 = (bf16[1,192,1536]{2,1,0:T(8,128)(2,1)}, bf16[1,192,1536]{2,1,0:T(8,128)(2,1)}, u32[]{:S(2)}, u32[]{:S(2)}) collective-permute-start(bf16[1,192,1536]{2,1,0:T(8,128)(2,1)} %get-tuple-element.87), channel_id=1, source_target_pairs={{0,2},{1,3},{2,0},{3,1},{4,6},{5,7},{6,4},{7,5},{8,10},{9,11},{10,... | collective-permute-start | bytes 1769480 | tf_op jit(solution)/shard_map/attention/ppermute | solution.py:25
  305.8 395.4 %all-gather.14.cloned.1.call-start = ((), (), s32[]{:S(2)}) async-start(), calls=%async_computation.19 | async-start | bytes 31850496 | tf_op jit(solution)/shard_map/attention/all_gather | solution.py:536
  312.7 48.6 %collective-permute-start.11 = (bf16[2,192,1536]{2,1,0:T(8,128)(2,1)}, bf16[2,192,1536]{2,1,0:T(8,128)(2,1)}, u32[]{:S(2)}, u32[]{:S(2)}) collective-permute-start(bf16[2,192,1536]{2,1,0:T(8,128)(2,1)} %get-tuple-element.91), channel_id=1, source_target_pairs={{0,2},{1,3},{2,0},{3,1},{4,6},{5,7},{6,4},{7,5},{8,10},{9,11},{10,... | collective-permute-start | bytes 3538952 | tf_op jit(solution)/shard_map/attention/ppermute | solution.py:25
  380.5 22.4 %collective-permute-start.12 = (bf16[2,128,1536]{2,1,0:T(8,128)(2,1)S(1)}, bf16[2,128,1536]{2,1,0:T(8,128)(2,1)S(1)}, u32[]{:S(2)}, u32[]{:S(2)}) collective-permute-start(bf16[2,128,1536]{2,1,0:T(8,128)(2,1)S(1)} %fusion.80), channel_id=1, source_target_pairs={{0,1},{1,0},{2,3},{3,2},{4,5},{5,4},{6,7},{7,6},{8,9},{9,8},{10,11... | collective-permute-start | bytes 2359304 | tf_op jit(solution)/shard_map/attention/ppermute | solution.py:25
  407.4 22.8 %collective-permute-start.13 = (bf16[2,128,1536]{2,1,0:T(8,128)(2,1)S(1)}, bf16[2,128,1536]{2,1,0:T(8,128)(2,1)}, u32[]{:S(2)}, u32[]{:S(2)}) collective-permute-start(bf16[2,128,1536]{2,1,0:T(8,128)(2,1)S(1)} %add_convert_fusion.3), channel_id=1, source_target_pairs={{0,1},{1,0},{2,3},{3,2},{4,5},{5,4},{6,7},{7,6},{8,9},{9,8},{10,11... | collective-permute-start | bytes 2359304 | tf_op jit(solution)/shard_map/mlp/ppermute | solution.py:25
  407.5 41.2 %collective-permute-start.20 = (bf16[2,20,1536]{2,1,0:T(8,128)(2,1)S(1)}, bf16[2,20,1536]{2,1,0:T(8,128)(2,1)S(1)}, u32[]{:S(2)}, u32[]{:S(2)}) collective-permute-start(bf16[2,20,1536]{2,1,0:T(8,128)(2,1)S(1)} %add_convert_fusion.7), channel_id=1, source_target_pairs={{0,1},{1,0},{2,3},{3,2},{4,5},{5,4},{6,7},{7,6},{8,9},{9,8},{10,11... | collective-permute-start | bytes 368648 | tf_op jit(solution)/shard_map/mlp/ppermute | solution.py:25
  409.6 39.2 %collective-permute-start.21 = (bf16[2,20,1536]{2,1,0:T(8,128)(2,1)S(1)}, bf16[2,20,1536]{2,1,0:T(8,128)(2,1)}, u32[]{:S(2)}, u32[]{:S(2)}) collective-permute-start(bf16[2,20,1536]{2,1,0:T(8,128)(2,1)S(1)} %add_convert_fusion.7), channel_id=1, source_target_pairs={{0,2},{1,3},{2,0},{3,1},{4,6},{5,7},{6,4},{7,5},{8,10},{9,11},{10,... | collective-permute-start | bytes 368648 | tf_op jit(solution)/shard_map/mlp/ppermute | solution.py:25
  411.1 37.7 %collective-permute-start.22 = (bf16[2,20,1536]{2,1,0:T(8,128)(2,1)S(1)}, bf16[2,20,1536]{2,1,0:T(8,128)(2,1)}, u32[]{:S(2)}, u32[]{:S(2)}) collective-permute-start(bf16[2,20,1536]{2,1,0:T(8,128)(2,1)S(1)} %add_convert_fusion.7), channel_id=1, source_target_pairs={{0,3},{1,2},{2,1},{3,0},{4,7},{5,6},{6,5},{7,4},{8,11},{9,10},{10,... | collective-permute-start | bytes 368648 | tf_op jit(solution)/shard_map/mlp/ppermute | solution.py:25
  448.7 34.8 %collective-permute-start.14 = (bf16[2,128,1536]{2,1,0:T(8,128)(2,1)S(1)}, bf16[2,128,1536]{2,1,0:T(8,128)(2,1)S(1)}, u32[]{:S(2)}, u32[]{:S(2)}) collective-permute-start(bf16[2,128,1536]{2,1,0:T(8,128)(2,1)S(1)} %fusion.83), channel_id=1, source_target_pairs={{0,1},{1,0},{2,3},{3,2},{4,5},{5,4},{6,7},{7,6},{8,9},{9,8},{10,11... | collective-permute-start | bytes 2359304 | tf_op jit(solution)/shard_map/mlp/ppermute | solution.py:25
  515.3 69.3 %all-to-all-start.3 = ((bf16[8,148,1152]{2,1,0:T(8,128)(2,1)}), bf16[8,148,1152]{2,1,0:T(8,128)(2,1)}, u32[]{:S(2)}, u32[]{:S(2)}) async-start(bf16[8,148,1152]{2,1,0:T(8,128)(2,1)} %bitcast.117), calls=%async_computation.3 | async-start | bytes 5603328 | tf_op jit(solution)/shard_map/attention/all_to_all | solution.py:340
  520.8 229.2 %collective-permute-start.44 = (bf16[2,20,1536]{2,1,0:T(8,128)(2,1)}, bf16[2,20,1536]{2,1,0:T(8,128)(2,1)}, u32[]{:S(2)}, u32[]{:S(2)}) collective-permute-start(bf16[2,20,1536]{2,1,0:T(8,128)(2,1)} %fusion.256), channel_id=1, source_target_pairs={{0,1},{1,0},{2,3},{3,2},{4,5},{5,4},{6,7},{7,6},{8,9},{9,8},{10,11... | collective-permute-start | bytes 368648 | tf_op jit(solution)/shard_map/mlp_grad/ppermute | solution.py:25
  520.8 229.2 %collective-permute-start.45 = (bf16[2,20,1536]{2,1,0:T(8,128)(2,1)}, bf16[2,20,1536]{2,1,0:T(8,128)(2,1)}, u32[]{:S(2)}, u32[]{:S(2)}) collective-permute-start(bf16[2,20,1536]{2,1,0:T(8,128)(2,1)} %fusion.256), channel_id=1, source_target_pairs={{0,2},{1,3},{2,0},{3,1},{4,6},{5,7},{6,4},{7,5},{8,10},{9,11},{10,... | collective-permute-start | bytes 368648 | tf_op jit(solution)/shard_map/mlp_grad/ppermute | solution.py:25
  610.4 406.7 %reduce-scatter.5.cloned.1.call-start = ((), (), s32[]{:S(2)}) async-start(), calls=%async_computation.20 | async-start | bytes 31850496 | tf_op jit(solution)/shard_map/mlp_grad/reduce_scatter | solution.py:397
  643.2 73.1 %collective-permute-start.43 = (bf16[2,128,1536]{2,1,0:T(8,128)(2,1)}, bf16[2,128,1536]{2,1,0:T(8,128)(2,1)}, u32[]{:S(2)}, u32[]{:S(2)}) collective-permute-start(bf16[2,128,1536]{2,1,0:T(8,128)(2,1)} %fusion.116), channel_id=1, source_target_pairs={{0,1},{1,0},{2,3},{3,2},{4,5},{5,4},{6,7},{7,6},{8,9},{9,8},{10,11... | collective-permute-start | bytes 2359304 | tf_op jit(solution)/shard_map/mlp_grad/ppermute | solution.py:25
  643.2 33.6 %collective-permute-start.30 = (bf16[2,128,1536]{2,1,0:T(8,128)(2,1)S(1)}, bf16[2,128,1536]{2,1,0:T(8,128)(2,1)S(1)}, u32[]{:S(2)}, u32[]{:S(2)}) collective-permute-start(bf16[2,128,1536]{2,1,0:T(8,128)(2,1)S(1)} %fusion.81), channel_id=1, source_target_pairs={{0,1},{1,0},{2,3},{3,2},{4,5},{5,4},{6,7},{7,6},{8,9},{9,8},{10,11... | collective-permute-start | bytes 2359304 | tf_op jit(solution)/shard_map/attention/ppermute | solution.py:25
  682.3 57.3 %collective-permute-start.37 = (bf16[2,20,1536]{2,1,0:T(8,128)(2,1)}, bf16[2,20,1536]{2,1,0:T(8,128)(2,1)}, u32[]{:S(2)}, u32[]{:S(2)}) collective-permute-start(bf16[2,20,1536]{2,1,0:T(8,128)(2,1)} %add_convert_fusion.5), channel_id=1, source_target_pairs={{0,1},{1,0},{2,3},{3,2},{4,5},{5,4},{6,7},{7,6},{8,9},{9,8},{10,11... | collective-permute-start | bytes 368648 | tf_op jit(solution)/shard_map/mlp/ppermute | solution.py:25
  701.2 39.6 %collective-permute-start.38 = (bf16[2,20,1536]{2,1,0:T(8,128)(2,1)}, bf16[2,20,1536]{2,1,0:T(8,128)(2,1)}, u32[]{:S(2)}, u32[]{:S(2)}) collective-permute-start(bf16[2,20,1536]{2,1,0:T(8,128)(2,1)} %add_convert_fusion.5), channel_id=1, source_target_pairs={{0,2},{1,3},{2,0},{3,1},{4,6},{5,7},{6,4},{7,5},{8,10},{9,11},{10,... | collective-permute-start | bytes 368648 | tf_op jit(solution)/shard_map/mlp/ppermute | solution.py:25
  716.3 24.5 %collective-permute-start.39 = (bf16[2,20,1536]{2,1,0:T(8,128)(2,1)}, bf16[2,20,1536]{2,1,0:T(8,128)(2,1)S(1)}, u32[]{:S(2)}, u32[]{:S(2)}) collective-permute-start(bf16[2,20,1536]{2,1,0:T(8,128)(2,1)} %add_convert_fusion.5), channel_id=1, source_target_pairs={{0,3},{1,2},{2,1},{3,0},{4,7},{5,6},{6,5},{7,4},{8,11},{9,10},{10,... | collective-permute-start | bytes 368648 | tf_op jit(solution)/shard_map/mlp/ppermute | solution.py:25
  740.8 37.3 %collective-permute-start.47 = (bf16[2,128,1536]{2,1,0:T(8,128)(2,1)}, bf16[2,128,1536]{2,1,0:T(8,128)(2,1)}, u32[]{:S(2)}, u32[]{:S(2)}) collective-permute-start(bf16[2,128,1536]{2,1,0:T(8,128)(2,1)} %fusion.84), channel_id=1, source_target_pairs={{0,1},{1,0},{2,3},{3,2},{4,5},{5,4},{6,7},{7,6},{8,9},{9,8},{10,11... | collective-permute-start | bytes 2359304 | tf_op jit(solution)/shard_map/mlp_grad/ppermute | solution.py:25
  786.0 68.5 %collective-permute-start.32 = (bf16[2,128,1536]{2,1,0:T(8,128)(2,1)S(1)}, bf16[2,128,1536]{2,1,0:T(8,128)(2,1)S(1)}, u32[]{:S(2)}, u32[]{:S(2)}) collective-permute-start(bf16[2,128,1536]{2,1,0:T(8,128)(2,1)S(1)} %fusion.85), channel_id=1, source_target_pairs={{0,1},{1,0},{2,3},{3,2},{4,5},{5,4},{6,7},{7,6},{8,9},{9,8},{10,11... | collective-permute-start | bytes 2359304 | tf_op jit(solution)/shard_map/mlp/ppermute | solution.py:25
  792.4 24.8 %collective-permute-start.49 = (bf16[2,20,1536]{2,1,0:T(8,128)(2,1)S(1)}, bf16[2,20,1536]{2,1,0:T(8,128)(2,1)S(1)}, u32[]{:S(2)}, u32[]{:S(2)}) collective-permute-start(bf16[2,20,1536]{2,1,0:T(8,128)(2,1)S(1)} %get-tuple-element.274), channel_id=1, source_target_pairs={{0,1},{1,0},{2,3},{3,2},{4,5},{5,4},{6,7},{7,6},{8,9},{9,8},{10,11... | collective-permute-start | bytes 368648 | tf_op jit(solution)/shard_map/mlp_grad/ppermute | solution.py:25
  793.5 27.4 %collective-permute-start.50 = (bf16[2,20,1536]{2,1,0:T(8,128)(2,1)S(1)}, bf16[2,20,1536]{2,1,0:T(8,128)(2,1)S(1)}, u32[]{:S(2)}, u32[]{:S(2)}) collective-permute-start(bf16[2,20,1536]{2,1,0:T(8,128)(2,1)S(1)} %get-tuple-element.276), channel_id=1, source_target_pairs={{0,2},{1,3},{2,0},{3,1},{4,6},{5,7},{6,4},{7,5},{8,10},{9,11},{10,... | collective-permute-start | bytes 368648 | tf_op jit(solution)/shard_map/mlp_grad/ppermute | solution.py:25
  796.0 25.5 %collective-permute-start.51 = (bf16[2,20,1536]{2,1,0:T(8,128)(2,1)S(1)}, bf16[2,20,1536]{2,1,0:T(8,128)(2,1)S(1)}, u32[]{:S(2)}, u32[]{:S(2)}) collective-permute-start(bf16[2,20,1536]{2,1,0:T(8,128)(2,1)S(1)} %get-tuple-element.275), channel_id=1, source_target_pairs={{0,3},{1,2},{2,1},{3,0},{4,7},{5,6},{6,5},{7,4},{8,11},{9,10},{10,... | collective-permute-start | bytes 368648 | tf_op jit(solution)/shard_map/mlp_grad/ppermute | solution.py:25
  949.0 45.3 %all-to-all-start.6 = ((bf16[8,148,1152]{2,1,0:T(8,128)(2,1)}), bf16[8,148,1152]{2,1,0:T(8,128)(2,1)}, u32[]{:S(2)}, u32[]{:S(2)}) async-start(bf16[8,148,1152]{2,1,0:T(8,128)(2,1)} %reshape.486), calls=%async_computation.6 | async-start | bytes 5603328 | tf_op jit(solution)/shard_map/attention_grad/all_to_all | solution.py:496
  953.5 397.3 %reduce-scatter.7.cloned.1.call-start = ((), (), s32[]{:S(2)}) async-start(), calls=%async_computation.21 | async-start | bytes 15925248 | tf_op jit(solution)/shard_map/attention_grad/reduce_scatter | solution.py:397
  1017.1 393.1 %reduce-scatter.9.cloned.1.call-start = ((), (), s32[]{:S(2)}) async-start(), calls=%async_computation.22 | async-start | bytes 31850496 | tf_op jit(solution)/shard_map/mlp_grad/reduce_scatter | solution.py:397
  1035.3 35.9 %collective-permute-start.56 = (bf16[2,128,1536]{2,1,0:T(8,128)(2,1)S(1)}, bf16[2,128,1536]{2,1,0:T(8,128)(2,1)S(1)}, u32[]{:S(2)}, u32[]{:S(2)}) collective-permute-start(bf16[2,128,1536]{2,1,0:T(8,128)(2,1)S(1)} %fusion.86), channel_id=1, source_target_pairs={{0,1},{1,0},{2,3},{3,2},{4,5},{5,4},{6,7},{7,6},{8,9},{9,8},{10,11... | collective-permute-start | bytes 2359304 | tf_op jit(solution)/shard_map/attention_grad/ppermute | solution.py:25
  1102.7 30.2 %collective-permute-start.65 = (bf16[2,128,1536]{2,1,0:T(8,128)(2,1)S(1)}, bf16[2,128,1536]{2,1,0:T(8,128)(2,1)S(1)}, u32[]{:S(2)}, u32[]{:S(2)}) collective-permute-start(bf16[2,128,1536]{2,1,0:T(8,128)(2,1)S(1)} %fusion.82), channel_id=1, source_target_pairs={{0,1},{1,0},{2,3},{3,2},{4,5},{5,4},{6,7},{7,6},{8,9},{9,8},{10,11... | collective-permute-start | bytes 2359304 | tf_op jit(solution)/shard_map/mlp_grad/ppermute | solution.py:25
  1182.7 20.6 %collective-permute-start.66 = (bf16[2,128,1536]{2,1,0:T(8,128)(2,1)S(1)}, bf16[2,128,1536]{2,1,0:T(8,128)(2,1)S(1)}, u32[]{:S(2)}, u32[]{:S(2)}) collective-permute-start(bf16[2,128,1536]{2,1,0:T(8,128)(2,1)S(1)} %multiply_convert_fusion), channel_id=1, source_target_pairs={{0,1},{1,0},{2,3},{3,2},{4,5},{5,4},{6,7},{7,6},{8,9},{9,8},{10,11... | collective-permute-start | bytes 2359304 | tf_op jit(solution)/shard_map/attention_grad/ppermute | solution.py:25
  1205.7 33.5 %all-to-all-start.7 = ((bf16[8,148,384]{2,1,0:T(8,128)(2,1)}), bf16[8,148,384]{2,1,0:T(8,128)(2,1)}, u32[]{:S(2)}, u32[]{:S(2)}) async-start(bf16[8,148,384]{2,1,0:T(8,128)(2,1)} %bitcast.243), calls=%async_computation.8 | async-start | bytes 1867776 | tf_op jit(solution)/shard_map/attention_grad/all_to_all | solution.py:488
  1244.7 50.7 %collective-permute-start.74 = (bf16[192,3072]{1,0:T(8,128)(2,1)}, bf16[192,3072]{1,0:T(8,128)(2,1)}, u32[]{:S(2)}, u32[]{:S(2)}) collective-permute-start(bf16[192,3072]{1,0:T(8,128)(2,1)} %get-tuple-element.217), channel_id=1, source_target_pairs={{0,2},{1,3},{2,0},{3,1},{4,6},{5,7},{6,4},{7,5},{8,10},{9,11},{10,... | collective-permute-start | bytes 3538952 | tf_op jit(solution)/shard_map/attention_grad/ppermute | solution.py:25
  1282.6 68.2 %all-to-all-start.8 = ((bf16[8,148,1152]{2,1,0:T(8,128)(2,1)}), bf16[8,148,1152]{2,1,0:T(8,128)(2,1)}, u32[]{:S(2)}, u32[]{:S(2)}) async-start(bf16[8,148,1152]{2,1,0:T(8,128)(2,1)} %reshape.494), calls=%async_computation.10 | async-start | bytes 5603328 | tf_op jit(solution)/shard_map/attention_grad/all_to_all | solution.py:496
  1287.0 280.1 %reduce-scatter.11.cloned.1.call-start = ((), (), s32[]{:S(2)}) async-start(), calls=%async_computation.23 | async-start | bytes 15925248 | tf_op jit(solution)/shard_map/attention_grad/reduce_scatter | solution.py:397
  1353.1 47.6 %collective-permute-start.86 = (bf16[192,1536]{1,0:T(8,128)(2,1)}, bf16[192,1536]{1,0:T(8,128)(2,1)}, u32[]{:S(2)}, u32[]{:S(2)}) collective-permute-start(bf16[192,1536]{1,0:T(8,128)(2,1)} %get-tuple-element.249), channel_id=1, source_target_pairs={{0,2},{1,3},{2,0},{3,1},{4,6},{5,7},{6,4},{7,5},{8,10},{9,11},{10,... | collective-permute-start | bytes 1769480 | tf_op jit(solution)/shard_map/attention_grad/ppermute | solution.py:25
  1358.8 29.7 %collective-permute-start.76 = (bf16[2,2,20,1152]{3,2,1,0:T(8,128)(2,1)S(1)}, bf16[2,2,20,1152]{3,2,1,0:T(8,128)(2,1)S(1)}, u32[]{:S(2)}, u32[]{:S(2)}) collective-permute-start(bf16[2,2,20,1152]{3,2,1,0:T(8,128)(2,1)S(1)} %bitcast.1276), channel_id=1, source_target_pairs={{0,2},{1,3},{2,0},{3,1},{4,6},{5,7},{6,4},{7,5},{8,10},{9,11},{10,... | collective-permute-start | bytes 552968 | tf_op jit(solution)/shard_map/attention_grad/ppermute | solution.py:25
  1457.6 26.6 %collective-permute-start.75 = (bf16[2,128,1536]{2,1,0:T(8,128)(2,1)}, bf16[2,128,1536]{2,1,0:T(8,128)(2,1)}, u32[]{:S(2)}, u32[]{:S(2)}) collective-permute-start(bf16[2,128,1536]{2,1,0:T(8,128)(2,1)} %fusion.87), channel_id=1, source_target_pairs={{0,1},{1,0},{2,3},{3,2},{4,5},{5,4},{6,7},{7,6},{8,9},{9,8},{10,11... | collective-permute-start | bytes 2359304 | tf_op jit(solution)/shard_map/attention_grad/ppermute | solution.py:25
  1467.7 89.9 %collective-permute-start.88 = (bf16[192,3072]{1,0:T(8,128)(2,1)}, bf16[192,3072]{1,0:T(8,128)(2,1)}, u32[]{:S(2)}, u32[]{:S(2)}) collective-permute-start(bf16[192,3072]{1,0:T(8,128)(2,1)} %get-tuple-element.215), channel_id=1, source_target_pairs={{0,2},{1,3},{2,0},{3,1},{4,6},{5,7},{6,4},{7,5},{8,10},{9,11},{10,... | collective-permute-start | bytes 3538952 | tf_op jit(solution)/shard_map/weight_grads/ppermute | solution.py:25
  1490.3 33.2 %all-to-all-start.10 = ((f32[4,4,2304]{2,1,0:T(4,128)}), f32[4,4,2304]{2,1,0:T(4,128)S(1)}, u32[]{:S(2)}, u32[]{:S(2)}) async-start(f32[4,4,2304]{2,1,0:T(4,128)} %copy.126), calls=%async_computation.12 | async-start | bytes 294912 | tf_op jit(solution)/shard_map/modulation_grad/all_to_all | solution.py:660
  1569.5 24.1 %collective-permute-start.87 = (bf16[192,1536]{1,0:T(8,128)(2,1)}, bf16[192,1536]{1,0:T(8,128)(2,1)S(1)}, u32[]{:S(2)}, u32[]{:S(2)}) collective-permute-start(bf16[192,1536]{1,0:T(8,128)(2,1)} %get-tuple-element.247), channel_id=1, source_target_pairs={{0,2},{1,3},{2,0},{3,1},{4,6},{5,7},{6,4},{7,5},{8,10},{9,11},{10,... | collective-permute-start | bytes 1769480 | tf_op jit(solution)/shard_map/weight_grads/ppermute | solution.py:25
  (364 other events, 4421.6 us)
Sparse Core Ops, SparseCore 0:
  43.1 60.0 all-gather.5
  105.6 42.5 all-gather.7
  183.2 176.2 all-gather.9
  361.3 77.9 all-gather.11
  441.0 168.6 all-gather.13
  778.2 193.7 reduce-scatter.4
  1017.2 102.2 reduce-scatter.6
  1133.1 218.2 reduce-scatter.8
  1410.3 100.0 reduce-scatter.10

commit v2 on v1

--- a/solution.py
+++ b/solution.py
@@ -33,29 +33,35 @@
     return tensor_swap(values, 2 * block)
 
 
-def pair_sum(own_part, other_part):
-    return own_part + pair_swap(other_part.astype(BF16)).astype(F32)
-
-
-def dp_sum(values):
-    count = lax.axis_size("dp")
+def axis_sum(values, axis):
+    count = lax.axis_size(axis)
     step = 1
     while step < count:
-        values = values + lax.ppermute(values, "dp", [(i, i ^ step) for i in range(count)])
+        values = values + lax.ppermute(values, axis, [(i, i ^ step) for i in range(count)])
         step *= 2
     return values
 
 
-def rows_of_all(values):
-    count = lax.axis_size("tensor")
-    return jnp.stack([values] + [tensor_swap(values, at) for at in range(1, count)])
-
-
-def sum_of_all(parts):
-    total = parts[0]
-    for at in range(1, lax.axis_size("tensor")):
-        total = total + tensor_swap(parts[at].astype(BF16), at).astype(F32)
-    return total
+def rows_of_others(image, text):
+    image_rows = image.shape[1]
+    received = pair_swap(jnp.concatenate([image, text], axis=1))
+    far = [tensor_swap(text, at) for at in range(2, lax.axis_size("tensor"))]
+    return (image, received[:, :image_rows]), jnp.stack([text, received[:, image_rows:], *far])
+
+
+def sum_over_others(image_own, image_other, text_terms, *meanwhile):
+    image_rows = image_own.shape[1]
+    sent = jnp.concatenate([image_other.astype(BF16), text_terms[1].astype(BF16)], axis=1)
+    received = pair_swap(sent)
+    far = [
+        tensor_swap(text_terms[at].astype(BF16), at) for at in range(2, text_terms.shape[0])
+    ]
+    received, far, *meanwhile = tied(received, far, *meanwhile)
+    image = image_own + received[:, :image_rows].astype(F32)
+    text = text_terms[0] + received[:, image_rows:].astype(F32)
+    for part in far:
+        text = text + part.astype(F32)
+    return [image, text], *meanwhile
 
 
 def to_sequences(parts, blocks):
@@ -319,14 +325,19 @@
     return image, text
 
 
-def forward_layer(streams, mods, weights, fetch):
+def forward_layer(streams, mods, attn_w, mlp_shards, next_shards):
     seqs, image_rows = streams[0].shape[:2]
-    qkv_w, out_w, up_w, down_w = weights
-    blocks = len(qkv_w[0])
     with jax.named_scope("attention"):
         normed = [modulate(streams[u], mods[u], 0) for u in range(2)]
-        text_one = rows_of_all(normed[1])
-        image_one = (normed[0], pair_swap(normed[0]))
+        image_one, text_one = rows_of_others(*normed)
+        text_one, attn_w, mlp_shards, next_shards = tied(
+            text_one, attn_w, mlp_shards, next_shards
+        )
+        mlp_w = [gather_pages(jnp.concatenate(mlp_shards, axis=0))]
+        mlp_others = with_blocks(mlp_shards[0])[1:]
+        next_others = with_blocks(next_shards[0])[1:] if next_shards else []
+        qkv_w, out_w = attention_pages(attn_w)
+        blocks = len(qkv_w[0])
         text_heads = rows_dot(text_one, qkv_w[1][0]).astype(BF16)
         text_heads = to_sequences(text_heads, blocks)
         image_heads = [
@@ -334,38 +345,39 @@
         ]
         packed = to_attention(image_heads, text_heads)
         tokens, columns = packed.shape[1:]
-        next_attn = next_mlp = None
-        if fetch:
-            next_attn, packed = fetch[0](packed)
         packed = lax.all_to_all(packed, "dp", 0, 0, tiled=True)
-        if fetch:
-            next_attn, packed = attention_weights(next_attn, False, packed)
-            next_mlp, packed = fetch[1](packed)
         packed = packed.reshape(-1, columns)
         mixed, lse = attention_forward(packed)
         mixed = mixed.reshape(-1, tokens, columns // 3)
         mixed = lax.all_to_all(mixed, "dp", 0, 0, tiled=True)
-        if fetch:
-            next_mlp, mixed = mlp_weights(next_mlp, mixed)
+        mixed, mlp_others, next_others = tied(mixed, mlp_others, next_others)
+        mlp_others, mlp_w[0] = tied(mlp_others, mlp_w[0])
+        mlp_w.append(gather_pages(jnp.concatenate(mlp_others, axis=0)))
         image_mixed, text_mixed = from_attention(mixed, blocks, image_rows)
         text_mixed = to_blocks(text_mixed, seqs)
         other = back_sum([part[seqs:] for part in image_mixed], out_w[0])
         text_terms = back_dot(text_mixed, out_w[1][0])
         own = back_sum([part[:seqs] for part in image_mixed], out_w[0])
-        attn = [pair_sum(own, other), sum_of_all(text_terms)]
+        (attn,) = sum_over_others(own, other, text_terms)
     with jax.named_scope("mlp"):
         middle = [streams[u] + mods[u][:, 2][:, None] * attn[u] for u in range(2)]
         normed_two = [modulate(middle[u], mods[u], 3) for u in range(2)]
-        text_two = rows_of_all(normed_two[1])
-        image_two = (normed_two[0], pair_swap(normed_two[0]))
+        image_two, text_two = rows_of_others(*normed_two)
+        text_two, mlp_w, next_shards, next_others = tied(
+            text_two, mlp_w, next_shards, next_others
+        )
+        next_attn = None
+        if next_shards:
+            next_attn = (gather_pages(jnp.concatenate([*next_shards, *next_others], axis=0)),)
+        up_w, down_w = mlp_pages(mlp_w)
         image_up = [[rows_dot(part, page) for page in up_w[0]] for part in image_two]
         image_act = [[gelu_tanh(up).astype(BF16) for up in part] for part in image_up]
-        other = back_sum(image_act[1], down_w[0])
+        other = back_sum(image_act[1], down_w[0]).astype(BF16)
         text_up = rows_dot(text_two, up_w[1][0])
         text_act = gelu_tanh(text_up).astype(BF16)
         text_terms = back_dot(text_act, down_w[1][0])
         own = back_sum(image_act[0], down_w[0])
-        mlp = [pair_sum(own, other), sum_of_all(text_terms)]
+        (mlp,) = sum_over_others(own, other, text_terms)
         result = [middle[u] + mods[u][:, 5][:, None] * mlp[u] for u in range(2)]
     saved = dict(
         streams=streams,
@@ -385,16 +397,15 @@
         text_act=text_act,
         mlp=mlp,
     )
-    return result, saved, (next_attn, next_mlp)
+    return result, saved, (attn_w, mlp_w), next_attn
 
 
 def gelu_pull(up_values, d_active):
     return jax.vjp(gelu_tanh, up_values)[1](d_active)[0].astype(BF16)
 
 
-def scatter_pages(grads, after):
-    wide, after = tied(jnp.concatenate(grads, axis=1), after)
-    return lax.psum_scatter(wide, "dp", scatter_dimension=0, tiled=True), after
+def scatter_pages(wide):
+    return lax.psum_scatter(wide, "dp", scatter_dimension=0, tiled=True)
 
 
 def shard_rows(slab, width, blocks):
@@ -429,7 +440,7 @@
     return (
         jnp.stack(
             [
-                part[:, : 3 * columns].reshape(-1, 3, columns).transpose(1, 0, 2)
+                jnp.stack([part[:, at * columns : (at + 1) * columns] for at in range(3)])
                 for part in rows
             ]
         ),
@@ -437,15 +448,15 @@
     )
 
 
-def backward_layer(grads_out, mods, weights, saved, pending):
+def backward_layer(grads_out, mods, weights, saved, pending, final):
     seqs, image_rows = grads_out[0].shape[:2]
-    qkv_w, out_w, up_w, down_w = weights
+    qkv_w, out_w = attention_pages(weights[0])
+    up_w, down_w = mlp_pages(weights[1])
     blocks = len(qkv_w[0])
     middle, attn, mlp = saved["middle"], saved["attn"], saved["mlp"]
     with jax.named_scope("mlp_grad"):
         gated = [(mods[u][:, 5][:, None] * grads_out[u]).astype(BF16) for u in range(2)]
-        text_dmlp = rows_of_all(gated[1])
-        image_dmlp = (gated[0], pair_swap(gated[0]))
+        image_dmlp, text_dmlp = rows_of_others(*gated)
         d_gate_two = [jnp.sum(grads_out[u] * mlp[u], axis=1) for u in range(2)]
         image_dup = [
             [
@@ -459,15 +470,15 @@
         text_terms = back_dot(text_dup, up_w[1][0])
         own = back_sum(image_dup[0], up_w[0])
         dmlp_rows = both(*image_dmlp)
-        received = pair_swap(other.astype(BF16))
         grads = page_list(
             [page_grad(dmlp_rows, act) for act in saved["image_act"]],
             [page_grad(saved["image_two"], both(*parts)) for parts in zip(*image_dup)],
             page_grad(text_dmlp, saved["text_act"]),
             page_grad(saved["text_two"], text_dup),
         )
-        mlp_slab, received = scatter_pages(grads, received)
-        d_two = [own + received.astype(F32), sum_of_all(text_terms)]
+        wide = jnp.concatenate(grads, axis=1)
+        d_two, wide = sum_over_others(own, other, text_terms, wide)
+        mlp_slab = scatter_pages(wide)
         d_middle, d_shift_two, d_scale_two = [], [], []
         for u in range(2):
             d_values, d_shift, d_scale = modulate_backward(middle[u], d_two[u], mods[u], 3)
@@ -476,8 +487,7 @@
             d_scale_two.append(d_scale)
     with jax.named_scope("attention_grad"):
         gated = [(mods[u][:, 2][:, None] * d_middle[u]).astype(BF16) for u in range(2)]
-        text_dattn = rows_of_all(gated[1])
-        image_dattn = (gated[0], pair_swap(gated[0]))
+        image_dattn, text_dattn = rows_of_others(*gated)
         d_gate_one = [jnp.sum(d_middle[u] * attn[u], axis=1) for u in range(2)]
         text_dmixed = to_sequences(rows_dot(text_dattn, out_w[1][0]).astype(BF16), blocks)
         image_dmixed = [
@@ -499,19 +509,26 @@
             done.append(attention_shard(attn_before, blocks))
         image_dproj, text_dproj = from_attention(d_packed, blocks, image_rows)
         text_dproj = to_blocks(text_dproj, seqs)
-        other = back_sum([part[seqs:] for part in image_dproj], qkv_w[0])
-        received = pair_swap(other.astype(BF16))
-        text_terms = back_dot(text_dproj, qkv_w[1][0])
-        own = back_sum([part[:seqs] for part in image_dproj], qkv_w[0])
+        grad_rows = image_dproj
+        if not final:
+            other = back_sum([part[seqs:] for part in image_dproj], qkv_w[0]).astype(BF16)
+            grad_rows, other = tied(image_dproj, other)
         dattn_rows = both(*image_dattn)
         grads = page_list(
-            [page_grad(saved["image_one"], part) for part in image_dproj],
+            [page_grad(saved["image_one"], part) for part in grad_rows],
             [page_grad(dattn_rows, part) for part in saved["image_mixed"]],
             page_grad(saved["text_one"], text_dproj),
             page_grad(text_dattn, saved["text_mixed"]),
         )
-        attn_slab, (mlp_slab, done) = scatter_pages(grads, (mlp_slab, done))
-        d_one = [own + received.astype(F32), sum_of_all(text_terms)]
+        wide = jnp.concatenate(grads, axis=1)
+        if final:
+            wide, image_dproj = tied(wide, image_dproj)
+            other = back_sum([part[seqs:] for part in image_dproj], qkv_w[0]).astype(BF16)
+        text_terms = back_dot(text_dproj, qkv_w[1][0])
+        own = back_sum([part[:seqs] for part in image_dproj], qkv_w[0])
+        (d_one,) = sum_over_others(own, other, text_terms)
+        wide, mlp_slab = tied(wide, mlp_slab)
+        attn_slab = scatter_pages(wide)
         d_inputs, d_mods = [], []
         for u in range(2):
             d_values, d_shift, d_scale = modulate_backward(
@@ -519,12 +536,12 @@
             )
             d_inputs.append(d_middle[u] + d_values)
             d_mods.append(
-                jnp.stack(
+                jnp.concatenate(
                     [d_shift, d_scale, d_gate_one[u], d_shift_two[u], d_scale_two[u], d_gate_two[u]],
                     axis=1,
                 )
             )
-    return d_inputs, jnp.stack(d_mods), (mlp_slab, attn_slab), done
+    return d_inputs, jnp.concatenate(d_mods), (mlp_slab, attn_slab), done
 
 
 def with_blocks(pages):
@@ -542,43 +559,27 @@
     return jnp.concatenate([qkv, w_out[layer_at, u].T], axis=1)
 
 
-def attention_shards(w_qkv, w_out, layer_at, after):
-    own = [attn_page(w_qkv, w_out, layer_at, u)[None] for u in range(2)]
-    own, after = tied(own, after)
-    lists = with_blocks(own[0])
-    return [lists[0], own[1], *lists[1:]], after
-
-
-def attention_weights(lists, split, after):
-    lists, after = tied(lists, after)
-    if split:
-        first = gather_pages(jnp.concatenate(lists[:2], axis=0))
-        rest, first = tied(lists[2:], first)
-        rest = gather_pages(jnp.concatenate(rest, axis=0))
-        pages = [first[0], first[1]] + [rest[at] for at in range(len(lists) - 2)]
-    else:
-        whole = gather_pages(jnp.concatenate(lists, axis=0))
-        pages = [whole[at] for at in range(len(lists))]
-    qkv_columns = lists[0].shape[2] * 3 // 4
+def attention_shards(w_qkv, w_out, layer_at):
+    return [attn_page(w_qkv, w_out, layer_at, u)[None] for u in range(2)]
+
+
+def mlp_shards(w_up, w_down, layer_at):
+    return [jnp.stack([w_up[layer_at, u], w_down[layer_at, u].T]) for u in range(2)]
+
+
+def attention_pages(gathered):
+    pages = [pages[at] for pages in gathered for at in range(pages.shape[0])]
+    qkv_columns = pages[0].shape[1] * 3 // 4
     by_stream = [[pages[0], *pages[2:]], [pages[1]]]
     qkv_w = [[page[:, :qkv_columns] for page in group] for group in by_stream]
     out_w = [[page[:, qkv_columns:] for page in group] for group in by_stream]
-    return (qkv_w, out_w), after
-
-
-def mlp_shards(w_up, w_down, layer_at, after):
-    own = [jnp.stack([w_up[layer_at, u], w_down[layer_at, u].T]) for u in range(2)]
-    own, after = tied(own, after)
-    return with_blocks(own[0]) + [own[1]], after
-
-
-def mlp_weights(lists, after):
-    lists, after = tied(lists, after)
-    blocks = len(lists) - 1
-    whole = gather_pages(jnp.concatenate(lists, axis=0))
-    up_w = [[whole[2 * at] for at in range(blocks)], [whole[2 * blocks]]]
-    down_w = [[whole[2 * at + 1] for at in range(blocks)], [whole[2 * blocks + 1]]]
-    return (up_w, down_w), after
+    return qkv_w, out_w
+
+
+def mlp_pages(gathered):
+    pages = [pages[at] for pages in gathered for at in range(pages.shape[0])]
+    by_stream = [[*pages[:2], *pages[4:]], pages[2:4]]
+    return [group[0::2] for group in by_stream], [group[1::2] for group in by_stream]
 
 
 def per_device(
@@ -603,8 +604,9 @@
     slab_rows = w_mod.shape[2]
     column_count = w_mod.shape[3]
     index_flat = cond_index.reshape(-1)
-    attn_w, _ = attention_weights(attention_shards(w_qkv, w_out, 0, ())[0], True, ())
-    mlp_lists, _ = mlp_shards(w_up, w_down, 0, ())
+    attn_shards = [attention_shards(w_qkv, w_out, at) for at in range(layer_count)]
+    all_mlp_shards = [mlp_shards(w_up, w_down, at) for at in range(layer_count)]
+    first_attn = gather_pages(jnp.concatenate(attn_shards[0], axis=0))
     with jax.named_scope("modulation"):
         onehot = (
             index_flat[:, None] == jnp.arange(cond_table.shape[0], dtype=jnp.int32)[None, :]
@@ -617,10 +619,14 @@
             layer_count * 2, micro_count, n_tensor, own_rows * column_count
         )
         partial_mod = partial_mod.transpose(2, 0, 1, 3).reshape(n_tensor, -1, column_count)
-        partial_mod = dp_sum(lax.all_to_all(partial_mod, "tensor", 0, 0, tiled=True))
+        partial_mod = lax.all_to_all(partial_mod, "tensor", 0, 0, tiled=True)
+        attn_own, partial_mod = tied(attn_shards[0], partial_mod)
+        attn_others = with_blocks(attn_own[0])[1:]
+        partial_mod = axis_sum(partial_mod, "dp")
         mod_own = partial_mod.transpose(1, 0, 2)
         mod_own = mod_own.reshape(layer_count, 2, seqs, 6, model_width)
-    mlp_w, mod_own = mlp_weights(mlp_lists, mod_own)
+    rest, first_attn, mod_own = tied(attn_others, first_attn, mod_own)
+    attn_w = (first_attn, gather_pages(jnp.concatenate(rest, axis=0)))
     mods = [[mod_own[layer_at, u] for u in range(2)] for layer_at in range(layer_count)]
 
     def rows_in(values):
@@ -632,60 +638,58 @@
     streams = [rows_in(image_in), rows_in(text_in)]
     saved, weights = [], []
     for layer_at in range(layer_count):
-        weights.append((*attn_w, *mlp_w))
-        fetch = None
-        if layer_at + 1 < layer_count:
-            fetch = (
-                functools.partial(attention_shards, w_qkv, w_out, layer_at + 1),
-                functools.partial(mlp_shards, w_up, w_down, layer_at + 1),
-            )
-        streams, kept, (attn_w, mlp_w) = forward_layer(
-            streams, mods[layer_at], weights[layer_at], fetch
-        )
+        streams, kept, gathered, attn_w = forward_layer(
+            streams,
+            mods[layer_at],
+            attn_w,
+            all_mlp_shards[layer_at],
+            attn_shards[layer_at + 1] if layer_at + 1 < layer_count else [],
+        )
+        weights.append(gathered)
         saved.append(kept)
     grads_now = [rows_in(cot_image), rows_in(cot_text)]
     shards = [None] * layer_count
-    d_cond_terms = []
-    grad_w_mod = [None] * layer_count
+    d_mods = [None] * layer_count
     pending = None
     for layer_at in reversed(range(layer_count)):
-        grads_now, d_mods, slabs, done = backward_layer(
-            grads_now, mods[layer_at], weights[layer_at], saved[layer_at], pending
+        grads_now, d_mods[layer_at], slabs, done = backward_layer(
+            grads_now, mods[layer_at], weights[layer_at], saved[layer_at], pending, layer_at == 0
         )
         if pending:
             shards[layer_at + 1] = done
         pending = slabs
-        with jax.named_scope("modulation_grad"):
-            d_mods = d_mods.reshape(2 * seqs, n_tensor, column_count).transpose(1, 0, 2)
-            d_mods = dp_sum(lax.all_to_all(d_mods, "tensor", 0, 0, tiled=True))
-            d_mods = d_mods.reshape(n_tensor, 2, micro_count, own_rows, column_count)
-            d_mods = d_mods.transpose(1, 2, 0, 3, 4)
-            d_columns = d_mods.reshape(2, micro_count * n_tensor * own_rows, column_count)
-            grad_w_mod[layer_at] = jnp.einsum(
-                "sd,msc->mdc",
-                silu_slab.astype(F32),
-                d_columns,
-                precision=HIGHEST,
-                preferred_element_type=F32,
-            )
-            d_cond_terms.append(
-                jnp.einsum(
-                    "msc,mdc->sd",
-                    d_columns,
-                    w_mod[layer_at].astype(F32),
-                    precision=HIGHEST,
-                    preferred_element_type=F32,
-                )
-            )
+    with jax.named_scope("modulation_grad"):
+        d_mods = jnp.concatenate(d_mods).reshape(layer_count * 2 * seqs, n_tensor, column_count)
+        d_mods = lax.all_to_all(d_mods.transpose(1, 0, 2), "tensor", 0, 0, tiled=True)
+        attn_slab, d_mods = tied(pending[1], d_mods)
+        shards[0] = (
+            mlp_shard(pending[0], n_tensor // 2),
+            attention_shard(attn_slab, n_tensor // 2),
+        )
+        d_mods = axis_sum(d_mods, "dp")
+        d_mods = d_mods.reshape(n_tensor, layer_count, 2, micro_count, own_rows, column_count)
+        d_columns = d_mods.transpose(1, 2, 3, 0, 4, 5)
+        d_columns = d_columns.reshape(layer_count, 2, -1, column_count)
+        grad_w_mod = jnp.einsum(
+            "sd,lmsc->lmdc",
+            silu_slab.astype(F32),
+            d_columns,
+            precision=HIGHEST,
+            preferred_element_type=F32,
+        )
+        d_silu = jnp.einsum(
+            "lmsc,lmdc->sd",
+            d_columns,
+            w_mod.astype(F32),
+            precision=HIGHEST,
+            preferred_element_type=F32,
+        )
     with jax.named_scope("conditioning_grad"):
-        d_silu = sum(d_cond_terms)
         d_cond = jax.vjp(jax.nn.silu, cond_slab)[1](d_silu)[0]
-        grad_cond = lax.psum(
+        grad_cond = axis_sum(
             jnp.dot(onehot.T, d_cond, precision=HIGHEST, preferred_element_type=F32), "tensor"
         )
     with jax.named_scope("weight_grads"):
-        blocks = n_tensor // 2
-        shards[0] = (mlp_shard(pending[0], blocks), attention_shard(pending[1], blocks))
         stacked = [
             jnp.stack([layer[part][at] for layer in shards])
             for part, at in ((1, 0), (1, 1), (0, 0), (0, 1))
@@ -696,7 +700,7 @@
         rows_out(grads_now[0]),
         rows_out(grads_now[1]),
         grad_cond,
-        jnp.stack(grad_w_mod),
+        grad_w_mod,
         *stacked,
     )
 

time: 1620 us -> 1490 us (0.920)
  waiting for transfers between devices: 698 us -> 614 us
  local copies, waits for them, and re-layouts: 102 us -> 167 us
  blocking collectives: 86.7 us -> 43.3 us
  matrix products: 355 us -> 320 us
  starting transfers between devices: 156 us -> 129 us
    all_gather x5 -> x7, waiting for transfers between devices: 60.2 us -> 17.6 us  [gather_pages(): return lax.all_gather(pages, 'dp', axis=1, tiled=True)]
    all_to_all x2 -> x1, waiting for transfers between devices: 35.5 us -> 0.01 us  [per_device(): lax.all_to_all(d_mods.transpose(1, 0, 2), 'tensor', 0, 0, tiled=True)]
    unnamed x640 -> x717, local copies, waits for them, and re-layouts: 33.1 us -> 58 us
    ppermute x80 -> x64, starting transfers between devices: 109 us -> 84.1 us  [tensor_swap(): lax.ppermute(values, 'tensor', [(i, i ^ distance) for i in range(count)])]
    dot_general x81, matrix products: 246 us -> 224 us  [dot32(): return jnp.einsum(pattern, left, right, preferred_element_type=F32)]
    all_to_all x2 -> x1, blocking collectives: 35.8 us -> 15.7 us  [per_device(): partial_mod = lax.all_to_all(partial_mod, 'tensor', 0, 0, tiled=True)]
    ppermute x9 -> x8, waiting for transfers between devices: 37.2 us -> 30.3 us  [axis_sum(): lax.ppermute(values, axis, [(i, i ^ step) for i in range(count)])]
    ppermute x80 -> x64, waiting for transfers between devices: 354 us -> 353 us  [tensor_swap(): lax.ppermute(values, 'tensor', [(i, i ^ distance) for i in range(count)])]
  transfers between devices with their start and end apart: 106 -> 91, of which waited for: 54 -> 49; matrix products, arithmetic and copies ran while one was open for 32% -> 35% of each run, Pallas kernels for 6% -> 6%
where the time goes in v2:
time: 1490 us
  waiting for transfers between devices  614 us (41%)
  matrix products  320 us (21%)
  local copies, waits for them, and re-layouts  167 us (11%)
  starting transfers between devices  129 us (9%)
  other arithmetic  103 us (7%)
  Pallas kernels  90.5 us (6%)
  blocking collectives  43.3 us (3%)
  between operations  19.2 us (1%)
    ppermute x64, waiting for transfers between devices, tensor_swap(): lax.ppermute(values, 'tensor', [(i, i ^ distance) for i in range(count)])  353 us
    dot_general x81, matrix products, dot32(): return jnp.einsum(pattern, left, right, preferred_element_type=F32)  224 us
    all_to_all x2, waiting for transfers between devices, forward_layer(): packed = lax.all_to_all(packed, 'dp', 0, 0, tiled=True)  89.4 us
    dot_general x24, matrix products, page_grad(): lax.dot_general(flat(left), flat(right), (((0,), (0,)), ((), ())), prefer...  86 us
    ppermute x64, starting transfers between devices, tensor_swap(): lax.ppermute(values, 'tensor', [(i, i ^ distance) for i in range(count)])  84.1 us
    all_to_all x2, waiting for transfers between devices, backward_layer(): d_packed = lax.all_to_all(d_packed, 'dp', 0, 0, tiled=True)  75.3 us
    pallas_call x2, Pallas kernels, attention_backward(): pl.pallas_call(attn_bwd_kernel, grid=(pairs, tiles), in_specs=[pl.BlockSp...  58.3 us
    unnamed x717, local copies, waits for them, and re-layouts  58 us
  transfers between devices with their start and end apart: 91, of which 49 were waited for; matrix products, arithmetic and copies ran while one was open for 35% of the time, Pallas kernels for 6%

profile of v2, /device:TPU:0, one launch (start us, length us, event | category | flops | bytes accessed | tf_op | source)
XLA Modules:
  0.0 1486.3 jit_solution(9706300308247779774)
XLA Ops:
  20.7 15.7 %all_to_all.50 = f32[4,8,2304]{2,1,0:T(8,128)S(1)} all-to-all(f32[4,8,2304]{2,1,0:T(8,128)S(1)} %copy.202), channel_id=1, replica_groups=mesh['dp'=8,'tensor'=4] {'tensor'}, dimensions={0} | all-to-all | bytes 589824 | tf_op jit(solution)/shard_map/modulation/all_to_all | solution.py:622
  39.6 7.9 collective-permute-done.2
  51.4 10.9 collective-permute-done.3
  65.1 12.3 collective-permute-done
  77.4 6.0 all-gather.8.cloned.1.call-done
  102.2 21.7 %collective-permute-done.4 = bf16[2,148,1536]{2,0,1:T(2,128)(2,1)S(1)} collective-permute-done((bf16[2,148,1536]{2,0,1:T(2,128)(2,1)S(1)}, bf16[2,148,1536]{2,0,1:T(2,128)(2,1)S(1)}, u32[]{:S(2)}, u32[]{:S(2)}) %collective-permute-start.4) | collective-permute-done | bytes 909344 | tf_op jit(solution)/shard_map/attention/ppermute | solution.py:25
  130.8 7.2 slice_bitcast_fusion.3
  138.1 5.1 fusion.211
  162.2 45.9 %all-to-all-done.1 = bf16[8,148,1152]{2,1,0:T(8,128)(2,1)} async-done(((bf16[8,148,1152]{2,1,0:T(8,128)(2,1)}), bf16[8,148,1152]{2,1,0:T(8,128)(2,1)}, u32[]{:S(2)}, u32[]{:S(2)}) %all-to-all-start.1) | async-done | bytes 2727968 | tf_op jit(solution)/shard_map/attention/all_to_all | solution.py:348
  214.3 16.1 %attention.2 = (bf16[1184,384]{1,0:T(8,128)(2,1)S(1)}, f32[3,2,8,592]{3,2,1,0:T(8,128)S(1)}) custom-call(bf16[1184,1152]{1,0:T(8,128)(2,1)S(1)} %copy-done.1, bf16[1184,1152]{1,0:T(8,128)(2,1)S(1)} %copy-done.1, bf16[1184,1152]{1,0:T(8,128)(2,1)S(1)} %copy-done.1), custom_call_target="tpu_custom_call" | custom-call | flops 4306501632 | bytes 3637248 | tf_op jit(solution)/shard_map/attention/pallas_call | solution.py:182
  241.0 26.9 %collective-permute-done.9 = bf16[1,192,1536]{2,1,0:T(8,128)(2,1)} collective-permute-done((bf16[1,192,1536]{2,1,0:T(8,128)(2,1)}, bf16[1,192,1536]{2,1,0:T(8,128)(2,1)}, u32[]{:S(2)}, u32[]{:S(2)}) %collective-permute-start.9) | collective-permute-done | bytes 589856 | tf_op jit(solution)/shard_map/attention/ppermute | solution.py:25
  284.5 20.2 %collective-permute-done.13 = bf16[2,20,1536]{2,1,0:T(8,128)(2,1)S(1)} collective-permute-done((bf16[2,20,1536]{2,1,0:T(8,128)(2,1)S(1)}, bf16[2,20,1536]{2,1,0:T(8,128)(2,1)S(1)}, u32[]{:S(2)}, u32[]{:S(2)}) %collective-permute-start.13) | collective-permute-done | bytes 122912 | tf_op jit(solution)/shard_map/attention/ppermute | solution.py:25
  317.7 19.2 %collective-permute-done.14 = bf16[2,148,1536]{2,0,1:T(2,128)(2,1)S(1)} collective-permute-done((bf16[2,148,1536]{2,0,1:T(2,128)(2,1)S(1)}, bf16[2,148,1536]{2,0,1:T(2,128)(2,1)S(1)}, u32[]{:S(2)}, u32[]{:S(2)}) %collective-permute-start.14) | collective-permute-done | bytes 909344 | tf_op jit(solution)/shard_map/mlp/ppermute | solution.py:25
  364.0 5.2 multiply_convert_fusion.7
  381.5 6.4 multiply_convert_fusion.9
  412.3 18.6 %collective-permute-done.20 = bf16[2,148,1536]{2,0,1:T(2,128)(2,1)S(1)} collective-permute-done((bf16[2,148,1536]{2,0,1:T(2,128)(2,1)S(1)}, bf16[2,148,1536]{2,0,1:T(2,128)(2,1)S(1)}, u32[]{:S(2)}, u32[]{:S(2)}) %collective-permute-start.20) | collective-permute-done | bytes 909344 | tf_op jit(solution)/shard_map/attention/ppermute | solution.py:25
  438.0 6.0 slice_bitcast_fusion
  461.9 43.5 %all-to-all-done.3 = bf16[8,148,1152]{2,1,0:T(8,128)(2,1)} async-done(((bf16[8,148,1152]{2,1,0:T(8,128)(2,1)}), bf16[8,148,1152]{2,1,0:T(8,128)(2,1)}, u32[]{:S(2)}, u32[]{:S(2)}) %all-to-all-start.3) | async-done | bytes 2727968 | tf_op jit(solution)/shard_map/attention/all_to_all | solution.py:348
  512.4 16.1 %attention.3 = (bf16[1184,384]{1,0:T(8,128)(2,1)S(1)}, f32[3,2,8,592]{3,2,1,0:T(8,128)S(1)}) custom-call(bf16[1184,1152]{1,0:T(8,128)(2,1)S(1)} %copy-done.2, bf16[1184,1152]{1,0:T(8,128)(2,1)S(1)} %copy-done.2, bf16[1184,1152]{1,0:T(8,128)(2,1)S(1)} %copy-done.2), custom_call_target="tpu_custom_call" | custom-call | flops 4306501632 | bytes 3637248 | tf_op jit(solution)/shard_map/attention/pallas_call | solution.py:182
  536.7 24.4 %all-to-all-done.4 = bf16[8,148,384]{2,1,0:T(8,128)(2,1)} async-done(((bf16[8,148,384]{2,1,0:T(8,128)(2,1)}), bf16[8,148,384]{2,1,0:T(8,128)(2,1)}, u32[]{:S(2)}, u32[]{:S(2)}) %all-to-all-start.4) | async-done | bytes 909344 | tf_op jit(solution)/shard_map/attention/all_to_all | solution.py:352
  561.2 11.6 all-gather.18.cloned.1.call-done
  606.8 17.9 %collective-permute-done.28 = bf16[2,20,1536]{2,1,0:T(8,128)(2,1)S(1)} collective-permute-done((bf16[2,20,1536]{2,1,0:T(8,128)(2,1)S(1)}, bf16[2,20,1536]{2,1,0:T(8,128)(2,1)S(1)}, u32[]{:S(2)}, u32[]{:S(2)}) %collective-permute-start.28) | collective-permute-done | bytes 122912 | tf_op jit(solution)/shard_map/attention/ppermute | solution.py:25
  635.3 12.4 collective-permute-done.35
  652.6 16.0 %collective-permute-done.29 = bf16[2,148,1536]{2,0,1:T(2,128)(2,1)S(1)} collective-permute-done((bf16[2,148,1536]{2,0,1:T(2,128)(2,1)S(1)}, bf16[2,148,1536]{2,0,1:T(2,128)(2,1)S(1)}, u32[]{:S(2)}, u32[]{:S(2)}) %collective-permute-start.29) | collective-permute-done | bytes 909344 | tf_op jit(solution)/shard_map/mlp/ppermute | solution.py:25
  677.1 5.4 multiply_convert_fusion.5
  754.6 5.2 fusion.42
  759.8 6.5 fusion.196
  770.7 15.0 %collective-permute-done.32 = bf16[2,148,1536]{2,0,1:T(2,128)(2,1)S(1)} collective-permute-done((bf16[2,148,1536]{2,0,1:T(2,128)(2,1)S(1)}, bf16[2,148,1536]{2,0,1:T(2,128)(2,1)S(1)}, u32[]{:S(2)}, u32[]{:S(2)}) %collective-permute-start.32) | collective-permute-done | bytes 909344 | tf_op jit(solution)/shard_map/mlp/ppermute | solution.py:25
  801.5 6.2 fusion.233
  811.1 17.6 %collective-permute-done.41 = bf16[2,148,1536]{2,0,1:T(2,128)(2,1)S(1)} collective-permute-done((bf16[2,148,1536]{2,0,1:T(2,128)(2,1)S(1)}, bf16[2,148,1536]{2,0,1:T(2,128)(2,1)S(1)}, u32[]{:S(2)}, u32[]{:S(2)}) %collective-permute-start.41) | collective-permute-done | bytes 909344 | tf_op jit(solution)/shard_map/attention_grad/ppermute | solution.py:25
  837.0 27.6 %all_to_all.51 = bf16[8,148,384]{2,1,0:T(8,128)(2,1)} all-to-all(bf16[8,148,384]{2,1,0:T(8,128)(2,1)S(1)} %bitcast.1223), channel_id=1, replica_groups=mesh['dp'=8,'tensor'=4] {'dp'}, dimensions={0} | all-to-all | bytes 1818624 | tf_op jit(solution)/shard_map/attention_grad/all_to_all | solution.py:498
  868.8 29.1 %attention_grad.2 = (bf16[1184,384]{1,0:T(8,128)(2,1)S(1)}, bf16[1184,384]{1,0:T(8,128)(2,1)S(1)}, bf16[1184,384]{1,0:T(8,128)(2,1)S(1)}) custom-call(bf16[1184,1152]{1,0:T(8,128)(2,1)} %reshape.452.q_ref.k_ref.v_ref, bf16[1184,1152]{1,0:T(8,128)(2,1)} %reshape.452.q_ref.k_ref.v_ref, bf16[1184,1152]{1,0:T(8,128)(2,1)} %reshape.452.q_ref.k_ref.v_ref, ...), custom_call_target="tpu_custom_call" | custom-call | flops 10766254080 | bytes 6365184 | tf_op jit(solution)/shard_map/attention_grad/pallas_call | solution.py:217
  914.7 44.4 %all-to-all-done.6 = bf16[8,148,1152]{2,1,0:T(8,128)(2,1)} async-done(((bf16[8,148,1152]{2,1,0:T(8,128)(2,1)}), bf16[8,148,1152]{2,1,0:T(8,128)(2,1)}, u32[]{:S(2)}, u32[]{:S(2)}) %all-to-all-start.6) | async-done | bytes 2727968 | tf_op jit(solution)/shard_map/attention_grad/all_to_all | solution.py:506
  1002.9 15.5 %collective-permute-done.48 = bf16[2,20,1536]{2,1,0:T(8,128)(2,1)S(1)} collective-permute-done((bf16[2,20,1536]{2,1,0:T(8,128)(2,1)S(1)}, bf16[2,20,1536]{2,1,0:T(8,128)(2,1)S(1)}, u32[]{:S(2)}, u32[]{:S(2)}) %collective-permute-start.48) | collective-permute-done | bytes 122912 | tf_op jit(solution)/shard_map/attention_grad/ppermute | solution.py:25
  1042.0 10.4 collective-permute-done.49
  1117.0 6.1 multiply_reduce_fusion.4
  1129.2 14.5 collective-permute-done.55
  1152.3 5.9 all-to-all-start.7
  1164.6 18.2 %all-to-all-done.7 = bf16[8,148,384]{2,1,0:T(8,128)(2,1)} async-done(((bf16[8,148,384]{2,1,0:T(8,128)(2,1)}), bf16[8,148,384]{2,1,0:T(8,128)(2,1)}, u32[]{:S(2)}, u32[]{:S(2)}) %all-to-all-start.7) | async-done | bytes 909344 | tf_op jit(solution)/shard_map/attention_grad/all_to_all | solution.py:498
  1189.7 29.1 %attention_grad.3 = (bf16[1184,384]{1,0:T(8,128)(2,1)S(1)}, bf16[1184,384]{1,0:T(8,128)(2,1)S(1)}, bf16[1184,384]{1,0:T(8,128)(2,1)S(1)}) custom-call(bf16[1184,1152]{1,0:T(8,128)(2,1)} %reshape.446.q_ref.k_ref.v_ref, bf16[1184,1152]{1,0:T(8,128)(2,1)} %reshape.446.q_ref.k_ref.v_ref, bf16[1184,1152]{1,0:T(8,128)(2,1)} %reshape.446.q_ref.k_ref.v_ref, ...), custom_call_target="tpu_custom_call" | custom-call | flops 10766254080 | bytes 6365184 | tf_op jit(solution)/shard_map/attention_grad/pallas_call | solution.py:217
  1231.3 8.6 collective-permute-done.59
  1245.2 30.9 %all-to-all-done.8 = bf16[8,148,1152]{2,1,0:T(8,128)(2,1)} async-done(((bf16[8,148,1152]{2,1,0:T(8,128)(2,1)}), bf16[8,148,1152]{2,1,0:T(8,128)(2,1)}, u32[]{:S(2)}, u32[]{:S(2)}) %all-to-all-start.8) | async-done | bytes 2727968 | tf_op jit(solution)/shard_map/attention_grad/all_to_all | solution.py:506
  1300.6 6.3 reduce-scatter.9.cloned.1.call-done
  1339.9 14.4 collective-permute-done.70
  1361.1 12.3 collective-permute-done.61
  1389.0 25.6 %collective-permute-done.71 = bf16[192,3072]{1,0:T(8,128)(2,1)} collective-permute-done((bf16[192,3072]{1,0:T(8,128)(2,1)}, bf16[192,3072]{1,0:T(8,128)(2,1)}, u32[]{:S(2)}, u32[]{:S(2)}) %collective-permute-start.71) | collective-permute-done | bytes 1179680 | tf_op jit(solution)/shard_map/modulation_grad/ppermute | solution.py:25
  1432.8 7.4 collective-permute-done.65
  1441.7 13.1 collective-permute-done.69
  (1254 shorter events, 698.3 us)
Async XLA Ops:
  7.2 76.2 %all-gather.8.cloned.1.call-start = ((), (), s32[]{:S(2)}) async-start(), calls=%async_computation.14 | async-start | bytes 10616832 | tf_op jit(solution)/shard_map/all_gather | solution.py:553
  15.0 110.8 %all-gather.10.cloned.1.call-start = ((), (), s32[]{:S(2)}) async-start(), calls=%async_computation.15 | async-start | bytes 5308416 | tf_op jit(solution)/shard_map/all_gather | solution.py:553
  49.0 28.4 %collective-permute-start = (bf16[1,192,1536]{2,1,0:T(8,128)(2,1)}, bf16[1,192,1536]{2,1,0:T(8,128)(2,1)}, u32[]{:S(2)}, u32[]{:S(2)}) collective-permute-start(bf16[1,192,1536]{2,1,0:T(8,128)(2,1)} %get-tuple-element.98), channel_id=1, source_target_pairs={{0,2},{1,3},{2,0},{3,1},{4,6},{5,7},{6,4},{7,5},{8,10},{9,11},{10,... | collective-permute-start | bytes 1769480 | tf_op jit(solution)/shard_map/modulation/ppermute | solution.py:25
  83.5 184.5 %all-gather.12.cloned.1.call-start = ((), (), s32[]{:S(2)}) async-start(), calls=%async_computation.16 | async-start | bytes 21233664 | tf_op jit(solution)/shard_map/attention/all_gather | solution.py:553
  95.2 28.7 %collective-permute-start.4 = (bf16[2,148,1536]{2,0,1:T(2,128)(2,1)S(1)}, bf16[2,148,1536]{2,0,1:T(2,128)(2,1)S(1)}, u32[]{:S(2)}, u32[]{:S(2)}) collective-permute-start(bf16[2,148,1536]{2,0,1:T(2,128)(2,1)S(1)} %copy.89), channel_id=1, source_target_pairs={{0,1},{1,0},{2,3},{3,2},{4,5},{5,4},{6,7},{7,6},{8,9},{9,8},{10,11... | collective-permute-start | bytes 2727944 | tf_op jit(solution)/shard_map/attention/ppermute | solution.py:25
  157.2 51.0 %all-to-all-start.1 = ((bf16[8,148,1152]{2,1,0:T(8,128)(2,1)}), bf16[8,148,1152]{2,1,0:T(8,128)(2,1)}, u32[]{:S(2)}, u32[]{:S(2)}) async-start(bf16[8,148,1152]{2,1,0:T(8,128)(2,1)} %bitcast.1208), calls=%async_computation.1 | async-start | bytes 5603328 | tf_op jit(solution)/shard_map/attention/all_to_all | solution.py:348
  162.2 105.7 %collective-permute-start.8 = (bf16[2,192,1536]{2,1,0:T(8,128)(2,1)}, bf16[2,192,1536]{2,1,0:T(8,128)(2,1)}, u32[]{:S(2)}, u32[]{:S(2)}) collective-permute-start(bf16[2,192,1536]{2,1,0:T(8,128)(2,1)} %get-tuple-element.107), channel_id=1, source_target_pairs={{0,2},{1,3},{2,0},{3,1},{4,6},{5,7},{6,4},{7,5},{8,10},{9,11},{10,... | collective-permute-start | bytes 3538952 | tf_op jit(solution)/shard_map/attention/ppermute | solution.py:25
  234.1 33.8 %all-to-all-start.2 = ((bf16[8,148,384]{2,1,0:T(8,128)(2,1)}), bf16[8,148,384]{2,1,0:T(8,128)(2,1)}, u32[]{:S(2)}, u32[]{:S(2)}) async-start(bf16[8,148,384]{2,1,0:T(8,128)(2,1)} %reshape.447), calls=%async_computation.2 | async-start | bytes 1867776 | tf_op jit(solution)/shard_map/attention/all_to_all | solution.py:352
  238.4 105.2 %all-gather.14.cloned.1.call-start = ((), (), s32[]{:S(2)}) async-start(), calls=%async_computation.17 | async-start | bytes 10616832 | tf_op jit(solution)/shard_map/attention/all_gather | solution.py:553
  238.5 29.4 %collective-permute-start.9 = (bf16[1,192,1536]{2,1,0:T(8,128)(2,1)}, bf16[1,192,1536]{2,1,0:T(8,128)(2,1)}, u32[]{:S(2)}, u32[]{:S(2)}) collective-permute-start(bf16[1,192,1536]{2,1,0:T(8,128)(2,1)} %get-tuple-element.125), channel_id=1, source_target_pairs={{0,2},{1,3},{2,0},{3,1},{4,6},{5,7},{6,4},{7,5},{8,10},{9,11},{10,... | collective-permute-start | bytes 1769480 | tf_op jit(solution)/shard_map/attention/ppermute | solution.py:25
  268.0 165.0 %all-gather.16.cloned.1.call-start = ((), (), s32[]{:S(2)}) async-start(), calls=%async_computation.18 | async-start | bytes 15925248 | tf_op jit(solution)/shard_map/mlp/all_gather | solution.py:553
  346.4 226.3 %all-gather.18.cloned.1.call-start = ((), (), s32[]{:S(2)}) async-start(), calls=%async_computation.19 | async-start | bytes 21233664 | tf_op jit(solution)/shard_map/attention/all_gather | solution.py:553
  362.1 32.5 %collective-permute-start.19 = (bf16[2,20,1536]{2,1,0:T(8,128)(2,1)S(1)}, bf16[2,20,1536]{2,1,0:T(8,128)(2,1)S(1)}, u32[]{:S(2)}, u32[]{:S(2)}) collective-permute-start(bf16[2,20,1536]{2,1,0:T(8,128)(2,1)S(1)} %get-tuple-element.367), channel_id=1, source_target_pairs={{0,3},{1,2},{2,1},{3,0},{4,7},{5,6},{6,5},{7,4},{8,11},{9,10},{10,... | collective-permute-start | bytes 368648 | tf_op jit(solution)/shard_map/mlp/ppermute | solution.py:25
  364.0 30.7 %collective-permute-start.18 = (bf16[2,20,1536]{2,1,0:T(8,128)(2,1)S(1)}, bf16[2,20,1536]{2,1,0:T(8,128)(2,1)S(1)}, u32[]{:S(2)}, u32[]{:S(2)}) collective-permute-start(bf16[2,20,1536]{2,1,0:T(8,128)(2,1)S(1)} %get-tuple-element.368), channel_id=1, source_target_pairs={{0,2},{1,3},{2,0},{3,1},{4,6},{5,7},{6,4},{7,5},{8,10},{9,11},{10,... | collective-permute-start | bytes 368648 | tf_op jit(solution)/shard_map/mlp/ppermute | solution.py:25
  457.4 48.0 %all-to-all-start.3 = ((bf16[8,148,1152]{2,1,0:T(8,128)(2,1)}), bf16[8,148,1152]{2,1,0:T(8,128)(2,1)}, u32[]{:S(2)}, u32[]{:S(2)}) async-start(bf16[8,148,1152]{2,1,0:T(8,128)(2,1)} %bitcast.1209), calls=%async_computation.3 | async-start | bytes 5603328 | tf_op jit(solution)/shard_map/attention/all_to_all | solution.py:348
  461.8 74.9 %collective-permute-start.24 = (bf16[2,192,1536]{2,1,0:T(8,128)(2,1)}, bf16[2,192,1536]{2,1,0:T(8,128)(2,1)}, u32[]{:S(2)}, u32[]{:S(2)}) collective-permute-start(bf16[2,192,1536]{2,1,0:T(8,128)(2,1)} %get-tuple-element.131), channel_id=1, source_target_pairs={{0,2},{1,3},{2,0},{3,1},{4,6},{5,7},{6,4},{7,5},{8,10},{9,11},{10,... | collective-permute-start | bytes 3538952 | tf_op jit(solution)/shard_map/attention/ppermute | solution.py:25
  532.3 28.8 %all-to-all-start.4 = ((bf16[8,148,384]{2,1,0:T(8,128)(2,1)}), bf16[8,148,384]{2,1,0:T(8,128)(2,1)}, u32[]{:S(2)}, u32[]{:S(2)}) async-start(bf16[8,148,384]{2,1,0:T(8,128)(2,1)} %reshape.453), calls=%async_computation.4 | async-start | bytes 1867776 | tf_op jit(solution)/shard_map/attention/all_to_all | solution.py:352
  536.7 136.0 %all-gather.20.cloned.1.call-start = ((), (), s32[]{:S(2)}) async-start(), calls=%async_computation.20 | async-start | bytes 10616832 | tf_op jit(solution)/shard_map/attention/all_gather | solution.py:553
  572.8 417.1 %reduce-scatter.5.cloned.1.call-start = ((), (), s32[]{:S(2)}) async-start(), calls=%async_computation.21 | async-start | bytes 31850496 | tf_op jit(solution)/shard_map/mlp_grad/reduce_scatter | solution.py:408
  575.3 115.5 %collective-permute-start.37 = (bf16[2,20,1536]{2,1,0:T(8,128)(2,1)}, bf16[2,20,1536]{2,1,0:T(8,128)(2,1)}, u32[]{:S(2)}, u32[]{:S(2)}) collective-permute-start(bf16[2,20,1536]{2,1,0:T(8,128)(2,1)} %fusion.383), channel_id=1, source_target_pairs={{0,3},{1,2},{2,1},{3,0},{4,7},{5,6},{6,5},{7,4},{8,11},{9,10},{10,... | collective-permute-start | bytes 368648 | tf_op jit(solution)/shard_map/mlp_grad/ppermute | solution.py:25
  578.6 112.2 %collective-permute-start.36 = (bf16[2,20,1536]{2,1,0:T(8,128)(2,1)}, bf16[2,20,1536]{2,1,0:T(8,128)(2,1)}, u32[]{:S(2)}, u32[]{:S(2)}) collective-permute-start(bf16[2,20,1536]{2,1,0:T(8,128)(2,1)} %fusion.383), channel_id=1, source_target_pairs={{0,2},{1,3},{2,0},{3,1},{4,6},{5,7},{6,4},{7,5},{8,10},{9,11},{10,... | collective-permute-start | bytes 368648 | tf_op jit(solution)/shard_map/mlp_grad/ppermute | solution.py:25
  597.9 28.9 %collective-permute-start.26 = (bf16[2,148,1536]{2,0,1:T(2,128)(2,1)S(1)}, bf16[2,148,1536]{2,0,1:T(2,128)(2,1)S(1)}, u32[]{:S(2)}, u32[]{:S(2)}) collective-permute-start(bf16[2,148,1536]{2,0,1:T(2,128)(2,1)S(1)} %copy.116), channel_id=1, source_target_pairs={{0,1},{1,0},{2,3},{3,2},{4,5},{5,4},{6,7},{7,6},{8,9},{9,8},{10,11... | collective-permute-start | bytes 2727944 | tf_op jit(solution)/shard_map/attention/ppermute | solution.py:25
  632.8 35.8 %collective-permute-start.29 = (bf16[2,148,1536]{2,0,1:T(2,128)(2,1)S(1)}, bf16[2,148,1536]{2,0,1:T(2,128)(2,1)S(1)}, u32[]{:S(2)}, u32[]{:S(2)}) collective-permute-start(bf16[2,148,1536]{2,0,1:T(2,128)(2,1)S(1)} %copy.119), channel_id=1, source_target_pairs={{0,1},{1,0},{2,3},{3,2},{4,5},{5,4},{6,7},{7,6},{8,9},{9,8},{10,11... | collective-permute-start | bytes 2727944 | tf_op jit(solution)/shard_map/mlp/ppermute | solution.py:25
  697.4 49.0 %collective-permute-start.40 = (bf16[2,20,1536]{2,1,0:T(8,128)(2,1)}, bf16[2,20,1536]{2,1,0:T(8,128)(2,1)}, u32[]{:S(2)}, u32[]{:S(2)}) collective-permute-start(bf16[2,20,1536]{2,1,0:T(8,128)(2,1)} %get-tuple-element.358), channel_id=1, source_target_pairs={{0,3},{1,2},{2,1},{3,0},{4,7},{5,6},{6,5},{7,4},{8,11},{9,10},{10,... | collective-permute-start | bytes 368648 | tf_op jit(solution)/shard_map/mlp_grad/ppermute | solution.py:25
  700.9 45.4 %collective-permute-start.39 = (bf16[2,20,1536]{2,1,0:T(8,128)(2,1)}, bf16[2,20,1536]{2,1,0:T(8,128)(2,1)}, u32[]{:S(2)}, u32[]{:S(2)}) collective-permute-start(bf16[2,20,1536]{2,1,0:T(8,128)(2,1)} %get-tuple-element.359), channel_id=1, source_target_pairs={{0,2},{1,3},{2,0},{3,1},{4,6},{5,7},{6,4},{7,5},{8,10},{9,11},{10,... | collective-permute-start | bytes 368648 | tf_op jit(solution)/shard_map/mlp_grad/ppermute | solution.py:25
  714.8 31.6 %collective-permute-start.38 = (bf16[2,148,1536]{2,0,1:T(2,128)(2,1)}, bf16[2,148,1536]{2,0,1:T(2,128)(2,1)}, u32[]{:S(2)}, u32[]{:S(2)}) collective-permute-start(bf16[2,148,1536]{2,0,1:T(2,128)(2,1)} %copy.130), channel_id=1, source_target_pairs={{0,1},{1,0},{2,3},{3,2},{4,5},{5,4},{6,7},{7,6},{8,9},{9,8},{10,11... | collective-permute-start | bytes 2727944 | tf_op jit(solution)/shard_map/mlp_grad/ppermute | solution.py:25
  792.1 36.7 %collective-permute-start.42 = (bf16[2,20,1536]{2,1,0:T(8,128)(2,1)S(1)}, bf16[2,20,1536]{2,1,0:T(8,128)(2,1)S(1)}, u32[]{:S(2)}, u32[]{:S(2)}) collective-permute-start(bf16[2,20,1536]{2,1,0:T(8,128)(2,1)S(1)} %multiply_convert_fusion.15), channel_id=1, source_target_pairs={{0,2},{1,3},{2,0},{3,1},{4,6},{5,7},{6,4},{7,5},{8,10},{9,11},{10,... | collective-permute-start | bytes 368648 | tf_op jit(solution)/shard_map/attention_grad/ppermute | solution.py:25
  792.2 36.7 %collective-permute-start.43 = (bf16[2,20,1536]{2,1,0:T(8,128)(2,1)S(1)}, bf16[2,20,1536]{2,1,0:T(8,128)(2,1)S(1)}, u32[]{:S(2)}, u32[]{:S(2)}) collective-permute-start(bf16[2,20,1536]{2,1,0:T(8,128)(2,1)S(1)} %multiply_convert_fusion.15), channel_id=1, source_target_pairs={{0,3},{1,2},{2,1},{3,0},{4,7},{5,6},{6,5},{7,4},{8,11},{9,10},{10,... | collective-permute-start | bytes 368648 | tf_op jit(solution)/shard_map/attention_grad/ppermute | solution.py:25
  904.0 55.2 %all-to-all-start.6 = ((bf16[8,148,1152]{2,1,0:T(8,128)(2,1)}), bf16[8,148,1152]{2,1,0:T(8,128)(2,1)}, u32[]{:S(2)}, u32[]{:S(2)}) async-start(bf16[8,148,1152]{2,1,0:T(8,128)(2,1)} %reshape.461), calls=%async_computation.6 | async-start | bytes 5603328 | tf_op jit(solution)/shard_map/attention_grad/all_to_all | solution.py:506
  908.5 367.6 %reduce-scatter.7.cloned.1.call-start = ((), (), s32[]{:S(2)}) async-start(), calls=%async_computation.22 | async-start | bytes 15925248 | tf_op jit(solution)/shard_map/attention_grad/reduce_scatter | solution.py:408
  989.9 317.0 %reduce-scatter.9.cloned.1.call-start = ((), (), s32[]{:S(2)}) async-start(), calls=%async_computation.23 | async-start | bytes 31850496 | tf_op jit(solution)/shard_map/mlp_grad/reduce_scatter | solution.py:408
  1023.1 30.1 %collective-permute-start.50 = (bf16[2,20,1536]{2,1,0:T(8,128)(2,1)S(1)}, bf16[2,20,1536]{2,1,0:T(8,128)(2,1)S(1)}, u32[]{:S(2)}, u32[]{:S(2)}) collective-permute-start(bf16[2,20,1536]{2,1,0:T(8,128)(2,1)S(1)} %multiply_convert_fusion.14), channel_id=1, source_target_pairs={{0,2},{1,3},{2,0},{3,1},{4,6},{5,7},{6,4},{7,5},{8,10},{9,11},{10,... | collective-permute-start | bytes 368648 | tf_op jit(solution)/shard_map/mlp_grad/ppermute | solution.py:25
  1072.4 29.9 %collective-permute-start.54 = (bf16[2,20,1536]{2,1,0:T(8,128)(2,1)}, bf16[2,20,1536]{2,1,0:T(8,128)(2,1)}, u32[]{:S(2)}, u32[]{:S(2)}) collective-permute-start(bf16[2,20,1536]{2,1,0:T(8,128)(2,1)} %get-tuple-element.352), channel_id=1, source_target_pairs={{0,3},{1,2},{2,1},{3,0},{4,7},{5,6},{6,5},{7,4},{8,11},{9,10},{10,... | collective-permute-start | bytes 368648 | tf_op jit(solution)/shard_map/mlp_grad/ppermute | solution.py:25
  1073.7 28.6 %collective-permute-start.53 = (bf16[2,20,1536]{2,1,0:T(8,128)(2,1)}, bf16[2,20,1536]{2,1,0:T(8,128)(2,1)}, u32[]{:S(2)}, u32[]{:S(2)}) collective-permute-start(bf16[2,20,1536]{2,1,0:T(8,128)(2,1)} %get-tuple-element.353), channel_id=1, source_target_pairs={{0,2},{1,3},{2,0},{3,1},{4,6},{5,7},{6,4},{7,5},{8,10},{9,11},{10,... | collective-permute-start | bytes 368648 | tf_op jit(solution)/shard_map/mlp_grad/ppermute | solution.py:25
  1073.7 28.6 %collective-permute-start.52 = (bf16[2,148,1536]{2,0,1:T(2,128)(2,1)}, bf16[2,148,1536]{2,0,1:T(2,128)(2,1)}, u32[]{:S(2)}, u32[]{:S(2)}) collective-permute-start(bf16[2,148,1536]{2,0,1:T(2,128)(2,1)} %copy.151), channel_id=1, source_target_pairs={{0,1},{1,0},{2,3},{3,2},{4,5},{5,4},{6,7},{7,6},{8,9},{9,8},{10,11... | collective-permute-start | bytes 2727944 | tf_op jit(solution)/shard_map/mlp_grad/ppermute | solution.py:25
  1114.5 29.3 %collective-permute-start.56 = (bf16[2,20,1536]{2,1,0:T(8,128)(2,1)S(1)}, bf16[2,20,1536]{2,1,0:T(8,128)(2,1)S(1)}, u32[]{:S(2)}, u32[]{:S(2)}) collective-permute-start(bf16[2,20,1536]{2,1,0:T(8,128)(2,1)S(1)} %multiply_convert_fusion.13), channel_id=1, source_target_pairs={{0,2},{1,3},{2,0},{3,1},{4,6},{5,7},{6,4},{7,5},{8,10},{9,11},{10,... | collective-permute-start | bytes 368648 | tf_op jit(solution)/shard_map/attention_grad/ppermute | solution.py:25
  1114.6 29.2 %collective-permute-start.57 = (bf16[2,20,1536]{2,1,0:T(8,128)(2,1)S(1)}, bf16[2,20,1536]{2,1,0:T(8,128)(2,1)S(1)}, u32[]{:S(2)}, u32[]{:S(2)}) collective-permute-start(bf16[2,20,1536]{2,1,0:T(8,128)(2,1)S(1)} %multiply_convert_fusion.13), channel_id=1, source_target_pairs={{0,3},{1,2},{2,1},{3,0},{4,7},{5,6},{6,5},{7,4},{8,11},{9,10},{10,... | collective-permute-start | bytes 368648 | tf_op jit(solution)/shard_map/attention_grad/ppermute | solution.py:25
  1152.3 30.5 %all-to-all-start.7 = ((bf16[8,148,384]{2,1,0:T(8,128)(2,1)}), bf16[8,148,384]{2,1,0:T(8,128)(2,1)}, u32[]{:S(2)}, u32[]{:S(2)}) async-start(bf16[8,148,384]{2,1,0:T(8,128)(2,1)} %bitcast.1222), calls=%async_computation.8 | async-start | bytes 1867776 | tf_op jit(solution)/shard_map/attention_grad/all_to_all | solution.py:498
  1188.7 51.2 %collective-permute-start.59 = (bf16[192,3072]{1,0:T(8,128)(2,1)}, bf16[192,3072]{1,0:T(8,128)(2,1)}, u32[]{:S(2)}, u32[]{:S(2)}) collective-permute-start(bf16[192,3072]{1,0:T(8,128)(2,1)} %get-tuple-element.283), channel_id=1, source_target_pairs={{0,2},{1,3},{2,0},{3,1},{4,6},{5,7},{6,4},{7,5},{8,10},{9,11},{10,... | collective-permute-start | bytes 3538952 | tf_op jit(solution)/shard_map/attention_grad/ppermute | solution.py:25
  1224.8 51.3 %all-to-all-start.8 = ((bf16[8,148,1152]{2,1,0:T(8,128)(2,1)}), bf16[8,148,1152]{2,1,0:T(8,128)(2,1)}, u32[]{:S(2)}, u32[]{:S(2)}) async-start(bf16[8,148,1152]{2,1,0:T(8,128)(2,1)} %reshape.469), calls=%async_computation.10 | async-start | bytes 5603328 | tf_op jit(solution)/shard_map/attention_grad/all_to_all | solution.py:506
  1229.2 194.9 %reduce-scatter.11.cloned.1.call-start = ((), (), s32[]{:S(2)}) async-start(), calls=%async_computation.24 | async-start | bytes 15925248 | tf_op jit(solution)/shard_map/attention_grad/reduce_scatter | solution.py:408
  1318.1 36.2 %collective-permute-start.70 = (bf16[192,1536]{1,0:T(8,128)(2,1)S(1)}, bf16[192,1536]{1,0:T(8,128)(2,1)S(1)}, u32[]{:S(2)}, u32[]{:S(2)}) collective-permute-start(bf16[192,1536]{1,0:T(8,128)(2,1)S(1)} %get-tuple-element.315), channel_id=1, source_target_pairs={{0,2},{1,3},{2,0},{3,1},{4,6},{5,7},{6,4},{7,5},{8,10},{9,11},{10,... | collective-permute-start | bytes 1769480 | tf_op jit(solution)/shard_map/attention_grad/ppermute | solution.py:25
  1325.3 32.7 %collective-permute-start.63 = (bf16[2,20,1536]{2,1,0:T(8,128)(2,1)S(1)}, bf16[2,20,1536]{2,1,0:T(8,128)(2,1)S(1)}, u32[]{:S(2)}, u32[]{:S(2)}) collective-permute-start(bf16[2,20,1536]{2,1,0:T(8,128)(2,1)S(1)} %get-tuple-element.349), channel_id=1, source_target_pairs={{0,3},{1,2},{2,1},{3,0},{4,7},{5,6},{6,5},{7,4},{8,11},{9,10},{10,... | collective-permute-start | bytes 368648 | tf_op jit(solution)/shard_map/attention_grad/ppermute | solution.py:25
  1328.1 33.0 %collective-permute-start.62 = (bf16[2,20,1536]{2,1,0:T(8,128)(2,1)S(1)}, bf16[2,20,1536]{2,1,0:T(8,128)(2,1)S(1)}, u32[]{:S(2)}, u32[]{:S(2)}) collective-permute-start(bf16[2,20,1536]{2,1,0:T(8,128)(2,1)S(1)} %get-tuple-element.350), channel_id=1, source_target_pairs={{0,2},{1,3},{2,0},{3,1},{4,6},{5,7},{6,4},{7,5},{8,10},{9,11},{10,... | collective-permute-start | bytes 368648 | tf_op jit(solution)/shard_map/attention_grad/ppermute | solution.py:25
  1332.1 41.3 %collective-permute-start.61 = (bf16[2,148,1536]{2,0,1:T(2,128)(2,1)S(1)}, bf16[2,148,1536]{2,0,1:T(2,128)(2,1)S(1)}, u32[]{:S(2)}, u32[]{:S(2)}) collective-permute-start(bf16[2,148,1536]{2,0,1:T(2,128)(2,1)S(1)} %copy.166), channel_id=1, source_target_pairs={{0,1},{1,0},{2,3},{3,2},{4,5},{5,4},{6,7},{7,6},{8,9},{9,8},{10,11... | collective-permute-start | bytes 2727944 | tf_op jit(solution)/shard_map/attention_grad/ppermute | solution.py:25
  1336.9 77.6 %collective-permute-start.71 = (bf16[192,3072]{1,0:T(8,128)(2,1)}, bf16[192,3072]{1,0:T(8,128)(2,1)}, u32[]{:S(2)}, u32[]{:S(2)}) collective-permute-start(bf16[192,3072]{1,0:T(8,128)(2,1)} %get-tuple-element.281), channel_id=1, source_target_pairs={{0,2},{1,3},{2,0},{3,1},{4,6},{5,7},{6,4},{7,5},{8,10},{9,11},{10,... | collective-permute-start | bytes 3538952 | tf_op jit(solution)/shard_map/modulation_grad/ppermute | solution.py:25
  1379.5 44.5 %all-to-all-start.9 = ((f32[4,8,2304]{2,1,0:T(8,128)}), f32[4,8,2304]{2,1,0:T(8,128)}, u32[]{:S(2)}, u32[]{:S(2)}) async-start(f32[4,8,2304]{2,1,0:T(8,128)} %bitcast.1254), calls=%async_computation.13 | async-start | bytes 589824 | tf_op jit(solution)/shard_map/modulation_grad/all_to_all | solution.py:663
  1425.6 29.2 %collective-permute-start.69 = (bf16[192,1536]{1,0:T(8,128)(2,1)S(1)}, bf16[192,1536]{1,0:T(8,128)(2,1)S(1)}, u32[]{:S(2)}, u32[]{:S(2)}) collective-permute-start(bf16[192,1536]{1,0:T(8,128)(2,1)S(1)} %get-tuple-element.313), channel_id=1, source_target_pairs={{0,2},{1,3},{2,0},{3,1},{4,6},{5,7},{6,4},{7,5},{8,10},{9,11},{10,... | collective-permute-start | bytes 1769480 | tf_op jit(solution)/shard_map/modulation_grad/ppermute | solution.py:25
  (370 other events, 3707.9 us)
Sparse Core Ops, SparseCore 0:
  15.1 68.2 all-gather.7
  85.3 39.1 all-gather.9
  129.2 128.8 all-gather.11
  268.1 59.9 all-gather.13
  346.6 77.9 all-gather.15
  436.4 136.2 all-gather.17
  574.7 58.8 all-gather.19
  746.5 205.8 reduce-scatter.4
  990.0 97.9 reduce-scatter.6
  1102.5 204.3 reduce-scatter.8
  1310.5 100.6 reduce-scatter.10

commit v3 on v2

--- a/solution.py
+++ b/solution.py
@@ -44,6 +44,7 @@
 
 def rows_of_others(image, text):
     image_rows = image.shape[1]
+    image, text = tied(image, text)
     received = pair_swap(jnp.concatenate([image, text], axis=1))
     far = [tensor_swap(text, at) for at in range(2, lax.axis_size("tensor"))]
     return (image, received[:, :image_rows]), jnp.stack([text, received[:, image_rows:], *far])
@@ -325,17 +326,24 @@
     return image, text
 
 
-def forward_layer(streams, mods, attn_w, mlp_shards, next_shards):
+def mlp_result(image_act, text_act, down_w, middle, mods):
+    other = back_sum(image_act[1], down_w[0]).astype(BF16)
+    text_terms = back_dot(text_act, down_w[1][0])
+    own = back_sum(image_act[0], down_w[0])
+    (mlp,) = sum_over_others(own, other, text_terms)
+    return mlp, [middle[u] + mods[u][:, 5][:, None] * mlp[u] for u in range(2)]
+
+
+def forward_layer(streams, mods, attn_w, mlp_shards, next_shards, early):
     seqs, image_rows = streams[0].shape[:2]
     with jax.named_scope("attention"):
         normed = [modulate(streams[u], mods[u], 0) for u in range(2)]
         image_one, text_one = rows_of_others(*normed)
-        text_one, attn_w, mlp_shards, next_shards = tied(
-            text_one, attn_w, mlp_shards, next_shards
-        )
-        mlp_w = [gather_pages(jnp.concatenate(mlp_shards, axis=0))]
-        mlp_others = with_blocks(mlp_shards[0])[1:]
-        next_others = with_blocks(next_shards[0])[1:] if next_shards else []
+        image_shards = jnp.concatenate([mlp_shards[0], *next_shards[:1]], axis=0)
+        mlp_shards = jnp.concatenate(mlp_shards, axis=0)
+        text_one, mlp_shards, image_shards = tied(text_one, mlp_shards, image_shards)
+        mlp_w = [gather_pages(mlp_shards)]
+        others = with_blocks(image_shards)[1:]
         qkv_w, out_w = attention_pages(attn_w)
         blocks = len(qkv_w[0])
         text_heads = rows_dot(text_one, qkv_w[1][0]).astype(BF16)
@@ -345,14 +353,18 @@
         ]
         packed = to_attention(image_heads, text_heads)
         tokens, columns = packed.shape[1:]
+        if early:
+            early, packed = tied(early, packed)
+            early = rows_of_others(*early)
         packed = lax.all_to_all(packed, "dp", 0, 0, tiled=True)
         packed = packed.reshape(-1, columns)
         mixed, lse = attention_forward(packed)
         mixed = mixed.reshape(-1, tokens, columns // 3)
         mixed = lax.all_to_all(mixed, "dp", 0, 0, tiled=True)
-        mixed, mlp_others, next_others = tied(mixed, mlp_others, next_others)
-        mlp_others, mlp_w[0] = tied(mlp_others, mlp_w[0])
-        mlp_w.append(gather_pages(jnp.concatenate(mlp_others, axis=0)))
+        mixed, others, early = tied(mixed, others, early)
+        others, mlp_w[0] = tied(others, mlp_w[0])
+        mlp_w.append(gather_pages(jnp.concatenate([part[:2] for part in others], axis=0)))
+        next_others = [part[2:] for part in others]
         image_mixed, text_mixed = from_attention(mixed, blocks, image_rows)
         text_mixed = to_blocks(text_mixed, seqs)
         other = back_sum([part[seqs:] for part in image_mixed], out_w[0])
@@ -363,22 +375,20 @@
         middle = [streams[u] + mods[u][:, 2][:, None] * attn[u] for u in range(2)]
         normed_two = [modulate(middle[u], mods[u], 3) for u in range(2)]
         image_two, text_two = rows_of_others(*normed_two)
-        text_two, mlp_w, next_shards, next_others = tied(
-            text_two, mlp_w, next_shards, next_others
-        )
+        up_w, down_w = mlp_pages(mlp_w)
+        image_up = [[rows_dot(part, page) for page in up_w[0]] for part in image_two]
         next_attn = None
         if next_shards:
+            image_up[0][0], mlp_w[1], next_shards, next_others = tied(
+                image_up[0][0], mlp_w[1], next_shards, next_others
+            )
             next_attn = (gather_pages(jnp.concatenate([*next_shards, *next_others], axis=0)),)
-        up_w, down_w = mlp_pages(mlp_w)
-        image_up = [[rows_dot(part, page) for page in up_w[0]] for part in image_two]
         image_act = [[gelu_tanh(up).astype(BF16) for up in part] for part in image_up]
-        other = back_sum(image_act[1], down_w[0]).astype(BF16)
         text_up = rows_dot(text_two, up_w[1][0])
         text_act = gelu_tanh(text_up).astype(BF16)
-        text_terms = back_dot(text_act, down_w[1][0])
-        own = back_sum(image_act[0], down_w[0])
-        (mlp,) = sum_over_others(own, other, text_terms)
-        result = [middle[u] + mods[u][:, 5][:, None] * mlp[u] for u in range(2)]
+        mlp = result = None
+        if not early:
+            mlp, result = mlp_result(image_act, text_act, down_w, middle, mods)
     saved = dict(
         streams=streams,
         image_one=both(*image_one),
@@ -392,12 +402,12 @@
         image_two=both(*image_two),
         text_two=text_two,
         image_up=image_up,
-        image_act=[both(*parts) for parts in zip(*image_act)],
+        image_act=image_act,
         text_up=text_up,
         text_act=text_act,
         mlp=mlp,
     )
-    return result, saved, (attn_w, mlp_w), next_attn
+    return result, saved, (attn_w, mlp_w), next_attn, early
 
 
 def gelu_pull(up_values, d_active):
@@ -408,12 +418,18 @@
     return lax.psum_scatter(wide, "dp", scatter_dimension=0, tiled=True)
 
 
-def shard_rows(slab, width, blocks):
-    image = slab[:, :width].astype(F32)
-    for block in range(1, blocks):
-        part = slab[:, (block + 1) * width : (block + 2) * width]
-        image = image + hi_swap(part, block).astype(F32)
-    return image, slab[:, width : 2 * width].astype(F32)
+def send_blocks(slab, blocks):
+    width = slab.shape[1] // (blocks + 1)
+    parts = [slab[:, (block + 1) * width : (block + 2) * width] for block in range(1, blocks)]
+    return [slab[:, : 2 * width]] + [hi_swap(part, at + 1) for at, part in enumerate(parts)]
+
+
+def shard_rows(parts):
+    width = parts[0].shape[1] // 2
+    image = parts[0][:, :width].astype(F32)
+    for part in parts[1:]:
+        image = image + part.astype(F32)
+    return image, parts[0][:, width:].astype(F32)
 
 
 def page_list(image_first, image_second, text_first, text_second):
@@ -423,20 +439,18 @@
     return pages
 
 
-def mlp_shard(slab, blocks):
-    width = slab.shape[1] // (blocks + 1)
-    rows = shard_rows(slab, width, blocks)
-    half = width // 2
+def mlp_shard(parts):
+    rows = shard_rows(parts)
+    half = rows[0].shape[1] // 2
     return (
         jnp.stack([part[:, half:] for part in rows]),
         jnp.stack([part[:, :half].T for part in rows]),
     )
 
 
-def attention_shard(slab, blocks):
-    width = slab.shape[1] // (blocks + 1)
-    rows = shard_rows(slab, width, blocks)
-    columns = width // 4
+def attention_shard(parts):
+    rows = shard_rows(parts)
+    columns = rows[0].shape[1] // 4
     return (
         jnp.stack(
             [
@@ -448,16 +462,18 @@
     )
 
 
-def backward_layer(grads_out, mods, weights, saved, pending, final):
+def gated_rows(rows, mods, gate):
+    return [(mods[u][:, gate][:, None] * rows[u]).astype(BF16) for u in range(2)]
+
+
+def backward_layer(grads_out, mods, weights, saved, pending, final, dmlp):
     seqs, image_rows = grads_out[0].shape[:2]
     qkv_w, out_w = attention_pages(weights[0])
     up_w, down_w = mlp_pages(weights[1])
     blocks = len(qkv_w[0])
     middle, attn, mlp = saved["middle"], saved["attn"], saved["mlp"]
     with jax.named_scope("mlp_grad"):
-        gated = [(mods[u][:, 5][:, None] * grads_out[u]).astype(BF16) for u in range(2)]
-        image_dmlp, text_dmlp = rows_of_others(*gated)
-        d_gate_two = [jnp.sum(grads_out[u] * mlp[u], axis=1) for u in range(2)]
+        image_dmlp, text_dmlp = dmlp or rows_of_others(*gated_rows(grads_out, mods, 5))
         image_dup = [
             [
                 gelu_pull(saved["image_up"][at][block], rows_dot(image_dmlp[at], down_w[0][block]))
@@ -471,7 +487,7 @@
         own = back_sum(image_dup[0], up_w[0])
         dmlp_rows = both(*image_dmlp)
         grads = page_list(
-            [page_grad(dmlp_rows, act) for act in saved["image_act"]],
+            [page_grad(dmlp_rows, both(*parts)) for parts in zip(*saved["image_act"])],
             [page_grad(saved["image_two"], both(*parts)) for parts in zip(*image_dup)],
             page_grad(text_dmlp, saved["text_act"]),
             page_grad(saved["text_two"], text_dup),
@@ -486,8 +502,7 @@
             d_shift_two.append(d_shift)
             d_scale_two.append(d_scale)
     with jax.named_scope("attention_grad"):
-        gated = [(mods[u][:, 2][:, None] * d_middle[u]).astype(BF16) for u in range(2)]
-        image_dattn, text_dattn = rows_of_others(*gated)
+        image_dattn, text_dattn = rows_of_others(*gated_rows(d_middle, mods, 2))
         d_gate_one = [jnp.sum(d_middle[u] * attn[u], axis=1) for u in range(2)]
         text_dmixed = to_sequences(rows_dot(text_dattn, out_w[1][0]).astype(BF16), blocks)
         image_dmixed = [
@@ -495,18 +510,28 @@
         ]
         d_mixed = to_attention(image_dmixed, text_dmixed)
         tokens, columns = d_mixed.shape[1:]
+        result = None
+        if mlp is None:
+            late, d_mixed = tied((saved["image_act"], saved["text_act"]), d_mixed)
+            mlp, result = mlp_result(*late, down_w, middle, mods)
         d_mixed = lax.all_to_all(d_mixed, "dp", 0, 0, tiled=True)
         done = []
         if pending:
             mlp_before, d_mixed = tied(pending[0], d_mixed)
-            done.append(mlp_shard(mlp_before, blocks))
+            done.append(mlp_shard(send_blocks(mlp_before, blocks)))
         d_mixed = d_mixed.reshape(-1, columns)
         d_packed = attention_backward(saved["packed"], d_mixed, saved["lse"])
+        if pending:
+            attn_before, d_packed = tied(pending[1], d_packed)
+            attn_before = send_blocks(attn_before, blocks)
         d_packed = d_packed.reshape(-1, tokens, 3 * columns)
         d_packed = lax.all_to_all(d_packed, "dp", 0, 0, tiled=True)
         if pending:
-            done[0], attn_before, d_packed = tied(done[0], pending[1], d_packed)
-            done.append(attention_shard(attn_before, blocks))
+            done[0], attn_before, d_packed = tied(done[0], attn_before, d_packed)
+            done.append(attention_shard(attn_before))
+        if result:
+            mlp, result, d_packed = tied(mlp, result, d_packed)
+        d_gate_two = [jnp.sum(grads_out[u] * mlp[u], axis=1) for u in range(2)]
         image_dproj, text_dproj = from_attention(d_packed, blocks, image_rows)
         text_dproj = to_blocks(text_dproj, seqs)
         grad_rows = image_dproj
@@ -541,7 +566,7 @@
                     axis=1,
                 )
             )
-    return d_inputs, jnp.concatenate(d_mods), (mlp_slab, attn_slab), done
+    return d_inputs, jnp.concatenate(d_mods), (mlp_slab, attn_slab), done, result
 
 
 def with_blocks(pages):
@@ -636,36 +661,45 @@
         return values.reshape(micro_count, own_rows, values.shape[1], model_width)
 
     streams = [rows_in(image_in), rows_in(text_in)]
+    grads_now = [rows_in(cot_image), rows_in(cot_text)]
     saved, weights = [], []
     for layer_at in range(layer_count):
-        streams, kept, gathered, attn_w = forward_layer(
+        last = layer_at + 1 == layer_count
+        streams, kept, gathered, attn_w, dmlp = forward_layer(
             streams,
             mods[layer_at],
             attn_w,
             all_mlp_shards[layer_at],
-            attn_shards[layer_at + 1] if layer_at + 1 < layer_count else [],
+            [] if last else attn_shards[layer_at + 1],
+            gated_rows(grads_now, mods[layer_at], 5) if last else (),
         )
         weights.append(gathered)
         saved.append(kept)
-    grads_now = [rows_in(cot_image), rows_in(cot_text)]
     shards = [None] * layer_count
     d_mods = [None] * layer_count
     pending = None
     for layer_at in reversed(range(layer_count)):
-        grads_now, d_mods[layer_at], slabs, done = backward_layer(
-            grads_now, mods[layer_at], weights[layer_at], saved[layer_at], pending, layer_at == 0
-        )
+        grads_now, d_mods[layer_at], slabs, done, result = backward_layer(
+            grads_now,
+            mods[layer_at],
+            weights[layer_at],
+            saved[layer_at],
+            pending,
+            layer_at == 0,
+            dmlp,
+        )
+        dmlp = None
+        streams = result or streams
         if pending:
             shards[layer_at + 1] = done
         pending = slabs
     with jax.named_scope("modulation_grad"):
         d_mods = jnp.concatenate(d_mods).reshape(layer_count * 2 * seqs, n_tensor, column_count)
         d_mods = lax.all_to_all(d_mods.transpose(1, 0, 2), "tensor", 0, 0, tiled=True)
-        attn_slab, d_mods = tied(pending[1], d_mods)
-        shards[0] = (
-            mlp_shard(pending[0], n_tensor // 2),
-            attention_shard(attn_slab, n_tensor // 2),
-        )
+        blocks = n_tensor // 2
+        mlp_parts = send_blocks(pending[0], blocks)
+        mlp_parts, attn_slab = tied(mlp_parts, pending[1])
+        attn_parts = send_blocks(attn_slab, blocks)
         d_mods = axis_sum(d_mods, "dp")
         d_mods = d_mods.reshape(n_tensor, layer_count, 2, micro_count, own_rows, column_count)
         d_columns = d_mods.transpose(1, 2, 3, 0, 4, 5)
@@ -690,10 +724,13 @@
             jnp.dot(onehot.T, d_cond, precision=HIGHEST, preferred_element_type=F32), "tensor"
         )
     with jax.named_scope("weight_grads"):
-        stacked = [
-            jnp.stack([layer[part][at] for layer in shards])
-            for part, at in ((1, 0), (1, 1), (0, 0), (0, 1))
-        ]
+        mlp_done = [mlp_shard(mlp_parts)] + [layer[0] for layer in shards[1:]]
+        grad_up, grad_down = [jnp.stack(parts) for parts in zip(*mlp_done)]
+        attn_parts, grad_up, grad_down, grad_w_mod, grad_cond = tied(
+            attn_parts, grad_up, grad_down, grad_w_mod, grad_cond
+        )
+        attn_done = [attention_shard(attn_parts)] + [layer[1] for layer in shards[1:]]
+        grad_qkv, grad_out = [jnp.stack(parts) for parts in zip(*attn_done)]
     return (
         rows_out(streams[0].astype(BF16)),
         rows_out(streams[1].astype(BF16)),
@@ -701,7 +738,10 @@
         rows_out(grads_now[1]),
         grad_cond,
         grad_w_mod,
-        *stacked,
+        grad_qkv,
+        grad_out,
+        grad_up,
+        grad_down,
     )
 
 

time: 1490 us -> 1410 us (0.946)
  waiting for transfers between devices: 614 us -> 553 us
  blocking collectives: 43.3 us -> 15.7 us
  matrix products: 320 us -> 304 us
    all_to_all x2, waiting for transfers between devices: 75.3 us -> 10.2 us  [backward_layer(): d_packed = lax.all_to_all(d_packed, 'dp', 0, 0, tiled=True)]
    all_to_all x1 -> x0, blocking collectives: 27.6 us -> none  [backward_layer(): d_mixed = lax.all_to_all(d_mixed, 'dp', 0, 0, tiled=True)]
    ppermute x8, waiting for transfers between devices: 30.3 us -> 48.2 us  [axis_sum(): lax.ppermute(values, axis, [(i, i ^ step) for i in range(count)])]
    dot_general x81, matrix products: 224 us -> 208 us  [dot32(): return jnp.einsum(pattern, left, right, preferred_element_type=F32)]
    ppermute x64 -> x63, waiting for transfers between devices: 353 us -> 338 us  [tensor_swap(): lax.ppermute(values, 'tensor', [(i, i ^ distance) for i in range(count)])]
    unnamed x717 -> x811, local copies, waits for them, and re-layouts: 58 us -> 45.7 us
    all_to_all x1 -> x2, waiting for transfers between devices: 18.2 us -> 30.1 us  [backward_layer(): d_mixed = lax.all_to_all(d_mixed, 'dp', 0, 0, tiled=True)]
    ppermute x64 -> x63, starting transfers between devices: 84.1 us -> 83.8 us  [tensor_swap(): lax.ppermute(values, 'tensor', [(i, i ^ distance) for i in range(count)])]
  transfers between devices with their start and end apart: 91 -> 91, of which waited for: 49 -> 57; matrix products, arithmetic and copies ran while one was open for 35% -> 38% of each run, Pallas kernels for 6% -> 6%
where the time goes in v3:
time: 1410 us; the launch traced here: 1400 us
  waiting for transfers between devices  553 us (39%)
  matrix products  304 us (22%)
  local copies, waits for them, and re-layouts  173 us (12%)
  starting transfers between devices  137 us (10%)
  other arithmetic  110 us (8%)
  Pallas kernels  90.6 us (6%)
  between operations  19.9 us (1%)
  blocking collectives  15.7 us (1%)
    ppermute x63, waiting for transfers between devices, tensor_swap(): lax.ppermute(values, 'tensor', [(i, i ^ distance) for i in range(count)])  338 us
    dot_general x81, matrix products, dot32(): return jnp.einsum(pattern, left, right, preferred_element_type=F32)  208 us
    all_to_all x2, waiting for transfers between devices, forward_layer(): packed = lax.all_to_all(packed, 'dp', 0, 0, tiled=True)  91.3 us
    dot_general x24, matrix products, page_grad(): lax.dot_general(flat(left), flat(right), (((0,), (0,)), ((), ())), prefer...  86.1 us
    ppermute x63, starting transfers between devices, tensor_swap(): lax.ppermute(values, 'tensor', [(i, i ^ distance) for i in range(count)])  83.8 us
    pallas_call x2, Pallas kernels, attention_backward(): pl.pallas_call(attn_bwd_kernel, grid=(pairs, tiles), in_specs=[pl.BlockSp...  58.3 us
    ppermute x8, waiting for transfers between devices, axis_sum(): lax.ppermute(values, axis, [(i, i ^ step) for i in range(count)])  48.2 us
    unnamed x811, local copies, waits for them, and re-layouts  45.7 us
  transfers between devices with their start and end apart: 91, of which 57 were waited for; matrix products, arithmetic and copies ran while one was open for 38% of the time, Pallas kernels for 6%

profile of v3, /device:TPU:0, one launch (start us, length us, event | category | flops | bytes accessed | tf_op | source)
XLA Modules:
  0.0 1403.3 jit_solution(15251690313305705083)
XLA Ops:
  20.6 15.7 %all_to_all.50 = f32[4,8,2304]{2,1,0:T(8,128)S(1)} all-to-all(f32[4,8,2304]{2,1,0:T(8,128)S(1)} %copy.202), channel_id=1, replica_groups=mesh['dp'=8,'tensor'=4] {'tensor'}, dimensions={0} | all-to-all | bytes 589824 | tf_op jit(solution)/shard_map/modulation/all_to_all | solution.py:647
  39.4 7.9 collective-permute-done.2
  51.3 10.9 collective-permute-done.3
  64.9 12.3 collective-permute-done
  77.3 6.0 all-gather.8.cloned.1.call-done
  106.9 14.7 %collective-permute-done.4 = bf16[2,148,1536]{2,0,1:T(2,128)(2,1)} collective-permute-done((bf16[2,148,1536]{2,0,1:T(2,128)(2,1)}, bf16[2,148,1536]{2,0,1:T(2,128)(2,1)}, u32[]{:S(2)}, u32[]{:S(2)}) %collective-permute-start.4) | collective-permute-done | bytes 909344 | tf_op jit(solution)/shard_map/attention/ppermute | solution.py:25
  127.8 6.7 slice_bitcast_fusion.7
  161.7 45.7 %all-to-all-done.1 = bf16[8,148,1152]{2,1,0:T(8,128)(2,1)} async-done(((bf16[8,148,1152]{2,1,0:T(8,128)(2,1)}), bf16[8,148,1152]{2,1,0:T(8,128)(2,1)}, u32[]{:S(2)}, u32[]{:S(2)}) %all-to-all-start.1) | async-done | bytes 2727968 | tf_op jit(solution)/shard_map/attention/all_to_all | solution.py:359
  213.5 16.1 %attention.2 = (bf16[1184,384]{1,0:T(8,128)(2,1)S(1)}, f32[3,2,8,592]{3,2,1,0:T(8,128)S(1)}) custom-call(bf16[1184,1152]{1,0:T(8,128)(2,1)S(1)} %copy-done.1, bf16[1184,1152]{1,0:T(8,128)(2,1)S(1)} %copy-done.1, bf16[1184,1152]{1,0:T(8,128)(2,1)S(1)} %copy-done.1), custom_call_target="tpu_custom_call" | custom-call | flops 4306501632 | bytes 3637248 | tf_op jit(solution)/shard_map/attention/pallas_call | solution.py:183
  240.4 15.8 %all-to-all-done.2 = bf16[8,148,384]{2,1,0:T(8,128)(2,1)} async-done(((bf16[8,148,384]{2,1,0:T(8,128)(2,1)}), bf16[8,148,384]{2,1,0:T(8,128)(2,1)}, u32[]{:S(2)}, u32[]{:S(2)}) %all-to-all-start.2) | async-done | bytes 909344 | tf_op jit(solution)/shard_map/attention/all_to_all | solution.py:363
  276.7 17.4 %collective-permute-done.11 = bf16[2,20,1536]{2,1,0:T(8,128)(2,1)S(1)} collective-permute-done((bf16[2,20,1536]{2,1,0:T(8,128)(2,1)S(1)}, bf16[2,20,1536]{2,1,0:T(8,128)(2,1)S(1)}, u32[]{:S(2)}, u32[]{:S(2)}) %collective-permute-start.11) | collective-permute-done | bytes 122912 | tf_op jit(solution)/shard_map/attention/ppermute | solution.py:25
  311.0 8.5 all-gather.14.cloned.1.call-done
  330.6 19.6 %collective-permute-done.13 = bf16[2,148,1536]{2,0,1:T(2,128)(2,1)S(1)} collective-permute-done((bf16[2,148,1536]{2,0,1:T(2,128)(2,1)S(1)}, bf16[2,148,1536]{2,0,1:T(2,128)(2,1)S(1)}, u32[]{:S(2)}, u32[]{:S(2)}) %collective-permute-start.13) | collective-permute-done | bytes 909344 | tf_op jit(solution)/shard_map/mlp/ppermute | solution.py:25
  359.4 5.2 fusion.426
  366.5 5.1 multiply_convert_fusion.8
  390.9 12.1 collective-permute-done.16
  418.5 17.1 %collective-permute-done.19 = bf16[2,148,1536]{2,0,1:T(2,128)(2,1)} collective-permute-done((bf16[2,148,1536]{2,0,1:T(2,128)(2,1)}, bf16[2,148,1536]{2,0,1:T(2,128)(2,1)}, u32[]{:S(2)}, u32[]{:S(2)}) %collective-permute-start.19) | collective-permute-done | bytes 909344 | tf_op jit(solution)/shard_map/attention/ppermute | solution.py:25
  447.6 6.6 slice_bitcast_fusion.2
  462.7 5.2 collective-permute-done.22
  479.2 45.5 %all-to-all-done.3 = bf16[8,148,1152]{2,1,0:T(8,128)(2,1)} async-done(((bf16[8,148,1152]{2,1,0:T(8,128)(2,1)}), bf16[8,148,1152]{2,1,0:T(8,128)(2,1)}, u32[]{:S(2)}, u32[]{:S(2)}) %all-to-all-start.3) | async-done | bytes 2727968 | tf_op jit(solution)/shard_map/attention/all_to_all | solution.py:359
  530.8 16.1 %attention.3 = (bf16[1184,384]{1,0:T(8,128)(2,1)S(1)}, f32[3,2,8,592]{3,2,1,0:T(8,128)S(1)}) custom-call(bf16[1184,1152]{1,0:T(8,128)(2,1)S(1)} %copy-done.2, bf16[1184,1152]{1,0:T(8,128)(2,1)S(1)} %copy-done.2, bf16[1184,1152]{1,0:T(8,128)(2,1)S(1)} %copy-done.2), custom_call_target="tpu_custom_call" | custom-call | flops 4306501632 | bytes 3637248 | tf_op jit(solution)/shard_map/attention/pallas_call | solution.py:183
  558.9 7.1 collective-permute-done.25
  586.3 17.1 %collective-permute-done.29 = bf16[2,20,1536]{2,1,0:T(8,128)(2,1)S(1)} collective-permute-done((bf16[2,20,1536]{2,1,0:T(8,128)(2,1)S(1)}, bf16[2,20,1536]{2,1,0:T(8,128)(2,1)S(1)}, u32[]{:S(2)}, u32[]{:S(2)}) %collective-permute-start.29) | collective-permute-done | bytes 122912 | tf_op jit(solution)/shard_map/attention/ppermute | solution.py:25
  618.4 19.2 %collective-permute-done.31 = bf16[2,148,1536]{2,0,1:T(2,128)(2,1)S(1)} collective-permute-done((bf16[2,148,1536]{2,0,1:T(2,128)(2,1)S(1)}, bf16[2,148,1536]{2,0,1:T(2,128)(2,1)S(1)}, u32[]{:S(2)}, u32[]{:S(2)}) %collective-permute-start.31) | collective-permute-done | bytes 909344 | tf_op jit(solution)/shard_map/mlp/ppermute | solution.py:25
  716.2 6.4 multiply_reduce_fusion
  734.3 15.8 %collective-permute-done.37 = bf16[2,148,1536]{2,0,1:T(2,128)(2,1)S(1)} collective-permute-done((bf16[2,148,1536]{2,0,1:T(2,128)(2,1)S(1)}, bf16[2,148,1536]{2,0,1:T(2,128)(2,1)S(1)}, u32[]{:S(2)}, u32[]{:S(2)}) %collective-permute-start.37) | collective-permute-done | bytes 909344 | tf_op jit(solution)/shard_map/attention_grad/ppermute | solution.py:25
  766.6 5.4 fusion.429
  779.2 11.8 all-to-all-done.5
  795.4 29.2 %attention_grad.2 = (bf16[1184,384]{1,0:T(8,128)(2,1)S(1)}, bf16[1184,384]{1,0:T(8,128)(2,1)S(1)}, bf16[1184,384]{1,0:T(8,128)(2,1)S(1)}) custom-call(bf16[1184,1152]{1,0:T(8,128)(2,1)} %reshape.405.q_ref.k_ref.v_ref, bf16[1184,1152]{1,0:T(8,128)(2,1)} %reshape.405.q_ref.k_ref.v_ref, bf16[1184,1152]{1,0:T(8,128)(2,1)} %reshape.405.q_ref.k_ref.v_ref, ...), custom_call_target="tpu_custom_call" | custom-call | flops 10766254080 | bytes 6365184 | tf_op jit(solution)/shard_map/attention_grad/pallas_call | solution.py:218
  849.3 11.8 collective-permute-done.42
  861.2 5.7 collective-permute-done.43
  868.8 5.3 multiply_add_fusion.2
  874.2 6.3 all-to-all-done.6
  925.8 16.0 %collective-permute-done.46 = bf16[2,20,1536]{2,1,0:T(8,128)(2,1)S(1)} collective-permute-done((bf16[2,20,1536]{2,1,0:T(8,128)(2,1)S(1)}, bf16[2,20,1536]{2,1,0:T(8,128)(2,1)S(1)}, u32[]{:S(2)}, u32[]{:S(2)}) %collective-permute-start.46) | collective-permute-done | bytes 122912 | tf_op jit(solution)/shard_map/attention_grad/ppermute | solution.py:25
  941.8 5.1 collective-permute-done.47
  959.6 6.0 fusion.187
  969.1 13.1 collective-permute-done.48
  1037.8 6.0 multiply_reduce_fusion.4
  1056.1 17.2 %collective-permute-done.54 = bf16[2,148,1536]{2,0,1:T(2,128)(2,1)S(1)} collective-permute-done((bf16[2,148,1536]{2,0,1:T(2,128)(2,1)S(1)}, bf16[2,148,1536]{2,0,1:T(2,128)(2,1)S(1)}, u32[]{:S(2)}, u32[]{:S(2)}) %collective-permute-start.54) | collective-permute-done | bytes 909344 | tf_op jit(solution)/shard_map/attention_grad/ppermute | solution.py:25
  1084.2 9.0 all-to-all-start.7
  1099.5 18.2 %all-to-all-done.7 = bf16[8,148,384]{2,1,0:T(8,128)(2,1)} async-done(((bf16[8,148,384]{2,1,0:T(8,128)(2,1)}), bf16[8,148,384]{2,1,0:T(8,128)(2,1)}, u32[]{:S(2)}, u32[]{:S(2)}) %all-to-all-start.7) | async-done | bytes 909344 | tf_op jit(solution)/shard_map/attention_grad/all_to_all | solution.py:517
  1123.7 29.2 %attention_grad.3 = (bf16[1184,384]{1,0:T(8,128)(2,1)S(1)}, bf16[1184,384]{1,0:T(8,128)(2,1)S(1)}, bf16[1184,384]{1,0:T(8,128)(2,1)S(1)}) custom-call(bf16[1184,1152]{1,0:T(8,128)(2,1)} %reshape.398.q_ref.k_ref.v_ref, bf16[1184,1152]{1,0:T(8,128)(2,1)} %reshape.398.q_ref.k_ref.v_ref, bf16[1184,1152]{1,0:T(8,128)(2,1)} %reshape.398.q_ref.k_ref.v_ref, ...), custom_call_target="tpu_custom_call" | custom-call | flops 10766254080 | bytes 6365184 | tf_op jit(solution)/shard_map/attention_grad/pallas_call | solution.py:218
  1165.7 8.9 collective-permute-done.58
  1182.3 23.5 %collective-permute-done.59 = bf16[192,1536]{1,0:T(8,128)(2,1)} collective-permute-done((bf16[192,1536]{1,0:T(8,128)(2,1)S(1)}, bf16[192,1536]{1,0:T(8,128)(2,1)}, u32[]{:S(2)}, u32[]{:S(2)}) %collective-permute-start.59) | collective-permute-done | bytes 589856 | tf_op jit(solution)/shard_map/attention_grad/ppermute | solution.py:25
  1261.6 18.0 %collective-permute-done.62 = bf16[2,20,1536]{2,1,0:T(8,128)(2,1)S(1)} collective-permute-done((bf16[2,20,1536]{2,1,0:T(8,128)(2,1)S(1)}, bf16[2,20,1536]{2,1,0:T(8,128)(2,1)S(1)}, u32[]{:S(2)}, u32[]{:S(2)}) %collective-permute-start.62) | collective-permute-done | bytes 122912 | tf_op jit(solution)/shard_map/attention_grad/ppermute | solution.py:25
  1320.6 11.9 collective-permute-done.68
  1345.5 11.6 collective-permute-done.69
  1378.9 11.5 collective-permute-done.65
  (1358 shorter events, 726.8 us)
Async XLA Ops:
  7.2 76.1 %all-gather.8.cloned.1.call-start = ((), (), s32[]{:S(2)}) async-start(), calls=%async_computation.14 | async-start | bytes 10616832 | tf_op jit(solution)/shard_map/all_gather | solution.py:578
  14.8 130.3 %all-gather.10.cloned.1.call-start = ((), (), s32[]{:S(2)}) async-start(), calls=%async_computation.15 | async-start | bytes 5308416 | tf_op jit(solution)/shard_map/all_gather | solution.py:578
  48.9 28.4 %collective-permute-start = (bf16[1,192,1536]{2,1,0:T(8,128)(2,1)}, bf16[1,192,1536]{2,1,0:T(8,128)(2,1)}, u32[]{:S(2)}, u32[]{:S(2)}) collective-permute-start(bf16[1,192,1536]{2,1,0:T(8,128)(2,1)} %get-tuple-element.131), channel_id=1, source_target_pairs={{0,2},{1,3},{2,0},{3,1},{4,6},{5,7},{6,4},{7,5},{8,10},{9,11},{10,... | collective-permute-start | bytes 1769480 | tf_op jit(solution)/shard_map/modulation/ppermute | solution.py:25
  83.3 172.9 %all-gather.12.cloned.1.call-start = ((), (), s32[]{:S(2)}) async-start(), calls=%async_computation.16 | async-start | bytes 21233664 | tf_op jit(solution)/shard_map/attention/all_gather | solution.py:578
  95.8 25.8 %collective-permute-start.4 = (bf16[2,148,1536]{2,0,1:T(2,128)(2,1)}, bf16[2,148,1536]{2,0,1:T(2,128)(2,1)}, u32[]{:S(2)}, u32[]{:S(2)}) collective-permute-start(bf16[2,148,1536]{2,0,1:T(2,128)(2,1)} %copy.89), channel_id=1, source_target_pairs={{0,1},{1,0},{2,3},{3,2},{4,5},{5,4},{6,7},{7,6},{8,9},{9,8},{10,11... | collective-permute-start | bytes 2727944 | tf_op jit(solution)/shard_map/attention/ppermute | solution.py:25
  155.6 51.9 %all-to-all-start.1 = ((bf16[8,148,1152]{2,1,0:T(8,128)(2,1)}), bf16[8,148,1152]{2,1,0:T(8,128)(2,1)}, u32[]{:S(2)}, u32[]{:S(2)}) async-start(bf16[8,148,1152]{2,1,0:T(8,128)(2,1)} %bitcast.1172), calls=%async_computation.1 | async-start | bytes 5603328 | tf_op jit(solution)/shard_map/attention/all_to_all | solution.py:359
  160.6 79.8 %collective-permute-start.8 = (bf16[3,192,1536]{2,1,0:T(8,128)(2,1)}, bf16[3,192,1536]{2,1,0:T(8,128)(2,1)}, u32[]{:S(2)}, u32[]{:S(2)}) collective-permute-start(bf16[3,192,1536]{2,1,0:T(8,128)(2,1)} %pad_maximum_fusion.11), channel_id=1, source_target_pairs={{0,2},{1,3},{2,0},{3,1},{4,6},{5,7},{6,4},{7,5},{8,10},{9,11},{10,... | collective-permute-start | bytes 5308424 | tf_op jit(solution)/shard_map/attention/ppermute | solution.py:25
  237.7 81.9 %all-gather.14.cloned.1.call-start = ((), (), s32[]{:S(2)}) async-start(), calls=%async_computation.17 | async-start | bytes 10616832 | tf_op jit(solution)/shard_map/attention/all_gather | solution.py:578
  258.5 189.1 %all-gather.16.cloned.1.call-start = ((), (), s32[]{:S(2)}) async-start(), calls=%async_computation.18 | async-start | bytes 15925248 | tf_op jit(solution)/shard_map/mlp/all_gather | solution.py:578
  269.1 29.1 %collective-permute-start.10 = (bf16[2,148,1536]{2,0,1:T(2,128)(2,1)S(1)}, bf16[2,148,1536]{2,0,1:T(2,128)(2,1)S(1)}, u32[]{:S(2)}, u32[]{:S(2)}) collective-permute-start(bf16[2,148,1536]{2,0,1:T(2,128)(2,1)S(1)} %copy.98), channel_id=1, source_target_pairs={{0,1},{1,0},{2,3},{3,2},{4,5},{5,4},{6,7},{7,6},{8,9},{9,8},{10,11... | collective-permute-start | bytes 2727944 | tf_op jit(solution)/shard_map/attention/ppermute | solution.py:25
  273.8 24.4 %collective-permute-start.12 = (bf16[2,20,1536]{2,1,0:T(8,128)(2,1)S(1)}, bf16[2,20,1536]{2,1,0:T(8,128)(2,1)S(1)}, u32[]{:S(2)}, u32[]{:S(2)}) collective-permute-start(bf16[2,20,1536]{2,1,0:T(8,128)(2,1)S(1)} %get-tuple-element.430), channel_id=1, source_target_pairs={{0,3},{1,2},{2,1},{3,0},{4,7},{5,6},{6,5},{7,4},{8,11},{9,10},{10,... | collective-permute-start | bytes 368648 | tf_op jit(solution)/shard_map/attention/ppermute | solution.py:25
  322.4 246.9 %all-gather.18.cloned.1.call-start = ((), (), s32[]{:S(2)}) async-start(), calls=%async_computation.19 | async-start | bytes 21233664 | tf_op jit(solution)/shard_map/attention/all_gather | solution.py:578
  324.7 25.6 %collective-permute-start.13 = (bf16[2,148,1536]{2,0,1:T(2,128)(2,1)S(1)}, bf16[2,148,1536]{2,0,1:T(2,128)(2,1)S(1)}, u32[]{:S(2)}, u32[]{:S(2)}) collective-permute-start(bf16[2,148,1536]{2,0,1:T(2,128)(2,1)S(1)} %copy.102), channel_id=1, source_target_pairs={{0,1},{1,0},{2,3},{3,2},{4,5},{5,4},{6,7},{7,6},{8,9},{9,8},{10,11... | collective-permute-start | bytes 2727944 | tf_op jit(solution)/shard_map/mlp/ppermute | solution.py:25
  326.9 24.0 %collective-permute-start.14 = (bf16[2,20,1536]{2,1,0:T(8,128)(2,1)S(1)}, bf16[2,20,1536]{2,1,0:T(8,128)(2,1)S(1)}, u32[]{:S(2)}, u32[]{:S(2)}) collective-permute-start(bf16[2,20,1536]{2,1,0:T(8,128)(2,1)S(1)} %copy-done.142), channel_id=1, source_target_pairs={{0,2},{1,3},{2,0},{3,1},{4,6},{5,7},{6,4},{7,5},{8,10},{9,11},{10,... | collective-permute-start | bytes 368648 | tf_op jit(solution)/shard_map/mlp/ppermute | solution.py:25
  329.3 25.9 %collective-permute-start.15 = (bf16[2,20,1536]{2,1,0:T(8,128)(2,1)S(1)}, bf16[2,20,1536]{2,1,0:T(8,128)(2,1)S(1)}, u32[]{:S(2)}, u32[]{:S(2)}) collective-permute-start(bf16[2,20,1536]{2,1,0:T(8,128)(2,1)S(1)} %copy-done.142), channel_id=1, source_target_pairs={{0,3},{1,2},{2,1},{3,0},{4,7},{5,6},{6,5},{7,4},{8,11},{9,10},{10,... | collective-permute-start | bytes 368648 | tf_op jit(solution)/shard_map/mlp/ppermute | solution.py:25
  364.7 25.8 %collective-permute-start.17 = (bf16[2,20,1536]{2,1,0:T(8,128)(2,1)S(1)}, bf16[2,20,1536]{2,1,0:T(8,128)(2,1)S(1)}, u32[]{:S(2)}, u32[]{:S(2)}) collective-permute-start(bf16[2,20,1536]{2,1,0:T(8,128)(2,1)S(1)} %get-tuple-element.424), channel_id=1, source_target_pairs={{0,2},{1,3},{2,0},{3,1},{4,6},{5,7},{6,4},{7,5},{8,10},{9,11},{10,... | collective-permute-start | bytes 368648 | tf_op jit(solution)/shard_map/mlp/ppermute | solution.py:25
  364.8 26.1 %collective-permute-start.18 = (bf16[2,20,1536]{2,1,0:T(8,128)(2,1)S(1)}, bf16[2,20,1536]{2,1,0:T(8,128)(2,1)S(1)}, u32[]{:S(2)}, u32[]{:S(2)}) collective-permute-start(bf16[2,20,1536]{2,1,0:T(8,128)(2,1)S(1)} %get-tuple-element.423), channel_id=1, source_target_pairs={{0,3},{1,2},{2,1},{3,0},{4,7},{5,6},{6,5},{7,4},{8,11},{9,10},{10,... | collective-permute-start | bytes 368648 | tf_op jit(solution)/shard_map/mlp/ppermute | solution.py:25
  410.1 25.6 %collective-permute-start.19 = (bf16[2,148,1536]{2,0,1:T(2,128)(2,1)}, bf16[2,148,1536]{2,0,1:T(2,128)(2,1)}, u32[]{:S(2)}, u32[]{:S(2)}) collective-permute-start(bf16[2,148,1536]{2,0,1:T(2,128)(2,1)} %copy.110), channel_id=1, source_target_pairs={{0,1},{1,0},{2,3},{3,2},{4,5},{5,4},{6,7},{7,6},{8,9},{9,8},{10,11... | collective-permute-start | bytes 2727944 | tf_op jit(solution)/shard_map/attention/ppermute | solution.py:25
  470.1 54.7 %all-to-all-start.3 = ((bf16[8,148,1152]{2,1,0:T(8,128)(2,1)}), bf16[8,148,1152]{2,1,0:T(8,128)(2,1)}, u32[]{:S(2)}, u32[]{:S(2)}) async-start(bf16[8,148,1152]{2,1,0:T(8,128)(2,1)} %bitcast.1171), calls=%async_computation.3 | async-start | bytes 5603328 | tf_op jit(solution)/shard_map/attention/all_to_all | solution.py:359
  474.5 92.5 %collective-permute-start.23 = (bf16[2,192,1536]{2,1,0:T(8,128)(2,1)}, bf16[2,192,1536]{2,1,0:T(8,128)(2,1)}, u32[]{:S(2)}, u32[]{:S(2)}) collective-permute-start(bf16[2,192,1536]{2,1,0:T(8,128)(2,1)} %pad_maximum_fusion.17), channel_id=1, source_target_pairs={{0,2},{1,3},{2,0},{3,1},{4,6},{5,7},{6,4},{7,5},{8,10},{9,11},{10,... | collective-permute-start | bytes 3538952 | tf_op jit(solution)/shard_map/attention/ppermute | solution.py:25
  477.5 77.7 %collective-permute-start.24 = (bf16[2,148,1536]{2,0,1:T(2,128)(2,1)}, bf16[2,148,1536]{2,0,1:T(2,128)(2,1)}, u32[]{:S(2)}, u32[]{:S(2)}) collective-permute-start(bf16[2,148,1536]{2,0,1:T(2,128)(2,1)} %copy.114), channel_id=1, source_target_pairs={{0,1},{1,0},{2,3},{3,2},{4,5},{5,4},{6,7},{7,6},{8,9},{9,8},{10,11... | collective-permute-start | bytes 2727944 | tf_op jit(solution)/shard_map/attention/ppermute | solution.py:25
  554.9 121.9 %all-gather.20.cloned.1.call-start = ((), (), s32[]{:S(2)}) async-start(), calls=%async_computation.20 | async-start | bytes 10616832 | tf_op jit(solution)/shard_map/attention/all_gather | solution.py:578
  569.3 344.0 %reduce-scatter.5.cloned.1.call-start = ((), (), s32[]{:S(2)}) async-start(), calls=%async_computation.21 | async-start | bytes 31850496 | tf_op jit(solution)/shard_map/mlp_grad/reduce_scatter | solution.py:418
  579.6 27.6 %collective-permute-start.28 = (bf16[2,148,1536]{2,0,1:T(2,128)(2,1)S(1)}, bf16[2,148,1536]{2,0,1:T(2,128)(2,1)S(1)}, u32[]{:S(2)}, u32[]{:S(2)}) collective-permute-start(bf16[2,148,1536]{2,0,1:T(2,128)(2,1)S(1)} %copy.121), channel_id=1, source_target_pairs={{0,1},{1,0},{2,3},{3,2},{4,5},{5,4},{6,7},{7,6},{8,9},{9,8},{10,11... | collective-permute-start | bytes 2727944 | tf_op jit(solution)/shard_map/attention/ppermute | solution.py:25
  582.4 24.4 %collective-permute-start.30 = (bf16[2,20,1536]{2,1,0:T(8,128)(2,1)S(1)}, bf16[2,20,1536]{2,1,0:T(8,128)(2,1)S(1)}, u32[]{:S(2)}, u32[]{:S(2)}) collective-permute-start(bf16[2,20,1536]{2,1,0:T(8,128)(2,1)S(1)} %get-tuple-element.420), channel_id=1, source_target_pairs={{0,3},{1,2},{2,1},{3,0},{4,7},{5,6},{6,5},{7,4},{8,11},{9,10},{10,... | collective-permute-start | bytes 368648 | tf_op jit(solution)/shard_map/attention/ppermute | solution.py:25
  647.4 54.7 %collective-permute-start.35 = (bf16[2,20,1536]{2,1,0:T(8,128)(2,1)}, bf16[2,20,1536]{2,1,0:T(8,128)(2,1)}, u32[]{:S(2)}, u32[]{:S(2)}) collective-permute-start(bf16[2,20,1536]{2,1,0:T(8,128)(2,1)} %get-tuple-element.418), channel_id=1, source_target_pairs={{0,2},{1,3},{2,0},{3,1},{4,6},{5,7},{6,4},{7,5},{8,10},{9,11},{10,... | collective-permute-start | bytes 368648 | tf_op jit(solution)/shard_map/mlp_grad/ppermute | solution.py:25
  648.2 53.9 %collective-permute-start.36 = (bf16[2,20,1536]{2,1,0:T(8,128)(2,1)}, bf16[2,20,1536]{2,1,0:T(8,128)(2,1)}, u32[]{:S(2)}, u32[]{:S(2)}) collective-permute-start(bf16[2,20,1536]{2,1,0:T(8,128)(2,1)} %get-tuple-element.417), channel_id=1, source_target_pairs={{0,3},{1,2},{2,1},{3,0},{4,7},{5,6},{6,5},{7,4},{8,11},{9,10},{10,... | collective-permute-start | bytes 368648 | tf_op jit(solution)/shard_map/mlp_grad/ppermute | solution.py:25
  762.2 28.9 %all-to-all-start.5 = ((bf16[8,148,384]{2,1,0:T(8,128)(2,1)}), bf16[8,148,384]{2,1,0:T(8,128)(2,1)}, u32[]{:S(2)}, u32[]{:S(2)}) async-start(bf16[8,148,384]{2,1,0:T(8,128)(2,1)} %bitcast.1187), calls=%async_computation.5 | async-start | bytes 1867776 | tf_op jit(solution)/shard_map/attention_grad/all_to_all | solution.py:517
  830.5 50.0 %all-to-all-start.6 = ((bf16[8,148,1152]{2,1,0:T(8,128)(2,1)}), bf16[8,148,1152]{2,1,0:T(8,128)(2,1)}, u32[]{:S(2)}, u32[]{:S(2)}) async-start(bf16[8,148,1152]{2,1,0:T(8,128)(2,1)} %reshape.412), calls=%async_computation.6 | async-start | bytes 5603328 | tf_op jit(solution)/shard_map/attention_grad/all_to_all | solution.py:528
  835.0 319.6 %reduce-scatter.7.cloned.1.call-start = ((), (), s32[]{:S(2)}) async-start(), calls=%async_computation.22 | async-start | bytes 15925248 | tf_op jit(solution)/shard_map/attention_grad/reduce_scatter | solution.py:418
  837.4 29.4 %collective-permute-start.41 = (bf16[2,148,1536]{2,0,1:T(2,128)(2,1)S(1)}, bf16[2,148,1536]{2,0,1:T(2,128)(2,1)S(1)}, u32[]{:S(2)}, u32[]{:S(2)}) collective-permute-start(bf16[2,148,1536]{2,0,1:T(2,128)(2,1)S(1)} %copy.138), channel_id=1, source_target_pairs={{0,1},{1,0},{2,3},{3,2},{4,5},{5,4},{6,7},{7,6},{8,9},{9,8},{10,11... | collective-permute-start | bytes 2727944 | tf_op jit(solution)/shard_map/attention_grad/ppermute | solution.py:25
  913.4 323.8 %reduce-scatter.9.cloned.1.call-start = ((), (), s32[]{:S(2)}) async-start(), calls=%async_computation.23 | async-start | bytes 31850496 | tf_op jit(solution)/shard_map/mlp_grad/reduce_scatter | solution.py:418
  918.1 28.9 %collective-permute-start.45 = (bf16[2,148,1536]{2,0,1:T(2,128)(2,1)S(1)}, bf16[2,148,1536]{2,0,1:T(2,128)(2,1)S(1)}, u32[]{:S(2)}, u32[]{:S(2)}) collective-permute-start(bf16[2,148,1536]{2,0,1:T(2,128)(2,1)S(1)} %copy.145), channel_id=1, source_target_pairs={{0,1},{1,0},{2,3},{3,2},{4,5},{5,4},{6,7},{7,6},{8,9},{9,8},{10,11... | collective-permute-start | bytes 2727944 | tf_op jit(solution)/shard_map/attention_grad/ppermute | solution.py:25
  922.5 24.5 %collective-permute-start.47 = (bf16[2,20,1536]{2,1,0:T(8,128)(2,1)S(1)}, bf16[2,20,1536]{2,1,0:T(8,128)(2,1)S(1)}, u32[]{:S(2)}, u32[]{:S(2)}) collective-permute-start(bf16[2,20,1536]{2,1,0:T(8,128)(2,1)S(1)} %get-tuple-element.411), channel_id=1, source_target_pairs={{0,3},{1,2},{2,1},{3,0},{4,7},{5,6},{6,5},{7,4},{8,11},{9,10},{10,... | collective-permute-start | bytes 368648 | tf_op jit(solution)/shard_map/attention_grad/ppermute | solution.py:25
  955.1 27.7 %collective-permute-start.49 = (bf16[2,20,1536]{2,1,0:T(8,128)(2,1)S(1)}, bf16[2,20,1536]{2,1,0:T(8,128)(2,1)}, u32[]{:S(2)}, u32[]{:S(2)}) collective-permute-start(bf16[2,20,1536]{2,1,0:T(8,128)(2,1)S(1)} %multiply_convert_fusion.14), channel_id=1, source_target_pairs={{0,2},{1,3},{2,0},{3,1},{4,6},{5,7},{6,4},{7,5},{8,10},{9,11},{10,... | collective-permute-start | bytes 368648 | tf_op jit(solution)/shard_map/mlp_grad/ppermute | solution.py:25
  955.2 27.7 %collective-permute-start.50 = (bf16[2,20,1536]{2,1,0:T(8,128)(2,1)S(1)}, bf16[2,20,1536]{2,1,0:T(8,128)(2,1)}, u32[]{:S(2)}, u32[]{:S(2)}) collective-permute-start(bf16[2,20,1536]{2,1,0:T(8,128)(2,1)S(1)} %multiply_convert_fusion.14), channel_id=1, source_target_pairs={{0,3},{1,2},{2,1},{3,0},{4,7},{5,6},{6,5},{7,4},{8,11},{9,10},{10,... | collective-permute-start | bytes 368648 | tf_op jit(solution)/shard_map/mlp_grad/ppermute | solution.py:25
  957.8 24.4 %collective-permute-start.48 = (bf16[2,148,1536]{2,0,1:T(2,128)(2,1)S(1)}, bf16[2,148,1536]{2,0,1:T(2,128)(2,1)S(1)}, u32[]{:S(2)}, u32[]{:S(2)}) collective-permute-start(bf16[2,148,1536]{2,0,1:T(2,128)(2,1)S(1)} %copy.148), channel_id=1, source_target_pairs={{0,1},{1,0},{2,3},{3,2},{4,5},{5,4},{6,7},{7,6},{8,9},{9,8},{10,11... | collective-permute-start | bytes 2727944 | tf_op jit(solution)/shard_map/mlp_grad/ppermute | solution.py:25
  999.1 31.0 %collective-permute-start.51 = (bf16[2,148,1536]{2,0,1:T(2,128)(2,1)}, bf16[2,148,1536]{2,0,1:T(2,128)(2,1)}, u32[]{:S(2)}, u32[]{:S(2)}) collective-permute-start(bf16[2,148,1536]{2,0,1:T(2,128)(2,1)} %copy.151), channel_id=1, source_target_pairs={{0,1},{1,0},{2,3},{3,2},{4,5},{5,4},{6,7},{7,6},{8,9},{9,8},{10,11... | collective-permute-start | bytes 2727944 | tf_op jit(solution)/shard_map/mlp_grad/ppermute | solution.py:25
  999.1 31.0 %collective-permute-start.52 = (bf16[2,20,1536]{2,1,0:T(8,128)(2,1)}, bf16[2,20,1536]{2,1,0:T(8,128)(2,1)}, u32[]{:S(2)}, u32[]{:S(2)}) collective-permute-start(bf16[2,20,1536]{2,1,0:T(8,128)(2,1)} %get-tuple-element.409), channel_id=1, source_target_pairs={{0,2},{1,3},{2,0},{3,1},{4,6},{5,7},{6,4},{7,5},{8,10},{9,11},{10,... | collective-permute-start | bytes 368648 | tf_op jit(solution)/shard_map/mlp_grad/ppermute | solution.py:25
  1002.0 28.0 %collective-permute-start.53 = (bf16[2,20,1536]{2,1,0:T(8,128)(2,1)}, bf16[2,20,1536]{2,1,0:T(8,128)(2,1)}, u32[]{:S(2)}, u32[]{:S(2)}) collective-permute-start(bf16[2,20,1536]{2,1,0:T(8,128)(2,1)} %get-tuple-element.408), channel_id=1, source_target_pairs={{0,3},{1,2},{2,1},{3,0},{4,7},{5,6},{6,5},{7,4},{8,11},{9,10},{10,... | collective-permute-start | bytes 368648 | tf_op jit(solution)/shard_map/mlp_grad/ppermute | solution.py:25
  1084.2 33.5 %all-to-all-start.7 = ((bf16[8,148,384]{2,1,0:T(8,128)(2,1)}), bf16[8,148,384]{2,1,0:T(8,128)(2,1)}, u32[]{:S(2)}, u32[]{:S(2)}) async-start(bf16[8,148,384]{2,1,0:T(8,128)(2,1)} %bitcast.1188), calls=%async_computation.8 | async-start | bytes 1867776 | tf_op jit(solution)/shard_map/attention_grad/all_to_all | solution.py:517
  1123.6 50.9 %collective-permute-start.58 = (bf16[192,3072]{1,0:T(8,128)(2,1)}, bf16[192,3072]{1,0:T(8,128)(2,1)}, u32[]{:S(2)}, u32[]{:S(2)}) collective-permute-start(bf16[192,3072]{1,0:T(8,128)(2,1)} %get-tuple-element.349), channel_id=1, source_target_pairs={{0,2},{1,3},{2,0},{3,1},{4,6},{5,7},{6,4},{7,5},{8,10},{9,11},{10,... | collective-permute-start | bytes 3538952 | tf_op jit(solution)/shard_map/attention_grad/ppermute | solution.py:25
  1158.9 50.8 %all-to-all-start.8 = ((bf16[8,148,1152]{2,1,0:T(8,128)(2,1)}), bf16[8,148,1152]{2,1,0:T(8,128)(2,1)}, u32[]{:S(2)}, u32[]{:S(2)}) async-start(bf16[8,148,1152]{2,1,0:T(8,128)(2,1)} %reshape.422), calls=%async_computation.10 | async-start | bytes 5603328 | tf_op jit(solution)/shard_map/attention_grad/all_to_all | solution.py:528
  1163.3 199.4 %reduce-scatter.11.cloned.1.call-start = ((), (), s32[]{:S(2)}) async-start(), calls=%async_computation.24 | async-start | bytes 15925248 | tf_op jit(solution)/shard_map/attention_grad/reduce_scatter | solution.py:418
  1178.0 27.8 %collective-permute-start.59 = (bf16[192,1536]{1,0:T(8,128)(2,1)S(1)}, bf16[192,1536]{1,0:T(8,128)(2,1)}, u32[]{:S(2)}, u32[]{:S(2)}) collective-permute-start(bf16[192,1536]{1,0:T(8,128)(2,1)S(1)} %slice.960), channel_id=1, source_target_pairs={{0,2},{1,3},{2,0},{3,1},{4,6},{5,7},{6,4},{7,5},{8,10},{9,11},{10,... | collective-permute-start | bytes 1769480 | tf_op jit(solution)/shard_map/attention_grad/ppermute | solution.py:25
  1253.8 30.4 %collective-permute-start.61 = (bf16[2,148,1536]{2,0,1:T(2,128)(2,1)S(1)}, bf16[2,148,1536]{2,0,1:T(2,128)(2,1)S(1)}, u32[]{:S(2)}, u32[]{:S(2)}) collective-permute-start(bf16[2,148,1536]{2,0,1:T(2,128)(2,1)S(1)} %copy.166), channel_id=1, source_target_pairs={{0,1},{1,0},{2,3},{3,2},{4,5},{5,4},{6,7},{7,6},{8,9},{9,8},{10,11... | collective-permute-start | bytes 2727944 | tf_op jit(solution)/shard_map/attention_grad/ppermute | solution.py:25
  1259.8 24.4 %collective-permute-start.63 = (bf16[2,20,1536]{2,1,0:T(8,128)(2,1)S(1)}, bf16[2,20,1536]{2,1,0:T(8,128)(2,1)S(1)}, u32[]{:S(2)}, u32[]{:S(2)}) collective-permute-start(bf16[2,20,1536]{2,1,0:T(8,128)(2,1)S(1)} %get-tuple-element.405), channel_id=1, source_target_pairs={{0,3},{1,2},{2,1},{3,0},{4,7},{5,6},{6,5},{7,4},{8,11},{9,10},{10,... | collective-permute-start | bytes 368648 | tf_op jit(solution)/shard_map/attention_grad/ppermute | solution.py:25
  1303.3 59.5 %collective-permute-start.64 = (bf16[192,3072]{1,0:T(8,128)(2,1)}, bf16[192,3072]{1,0:T(8,128)(2,1)}, u32[]{:S(2)}, u32[]{:S(2)}) collective-permute-start(bf16[192,3072]{1,0:T(8,128)(2,1)} %slice.978), channel_id=1, source_target_pairs={{0,2},{1,3},{2,0},{3,1},{4,6},{5,7},{6,4},{7,5},{8,10},{9,11},{10,... | collective-permute-start | bytes 3538952 | tf_op jit(solution)/shard_map/modulation_grad/ppermute | solution.py:25
  (417 other events, 3815.6 us)
Sparse Core Ops, SparseCore 0:
  15.0 68.2 all-gather.7
  85.2 39.1 all-gather.9
  127.9 127.5 all-gather.11
  258.7 60.7 all-gather.13
  322.5 78.7 all-gather.15
  439.3 121.6 all-gather.17
  569.4 58.2 all-gather.19
  707.3 203.1 reduce-scatter.4
  914.1 100.7 reduce-scatter.6
  1030.2 206.8 reduce-scatter.8
  1240.7 106.3 reduce-scatter.10

commit v4 on v3

--- a/solution.py
+++ b/solution.py
@@ -153,10 +153,6 @@
         dv_ref[...] = dv_acc[...].astype(BF16)
 
 
-def query_rows(length):
-    return length // 2 if length % 32 == 0 else length
-
-
 def padded_columns(columns):
     return -(-columns // LANES) * LANES
 
@@ -177,8 +173,7 @@
     columns = packed.shape[1] // 3
     wide = padded_columns(columns)
     pairs = wide // LANES
-    rows = query_rows(length)
-    tiles = length // rows
+    rows, tiles = length, 1
     packed = pad_heads(packed, 3)
     mixed, lse = pl.pallas_call(
         attn_fwd_kernel,
@@ -211,8 +206,7 @@
     columns = packed.shape[1] // 3
     wide = padded_columns(columns)
     pairs = wide // LANES
-    rows = query_rows(length)
-    tiles = length // rows
+    rows, tiles = length, 1
     packed = pad_heads(packed, 3)
     d_mixed = pad_heads(d_mixed, 1)
     grads = pl.pallas_call(
@@ -362,14 +356,14 @@
         mixed = mixed.reshape(-1, tokens, columns // 3)
         mixed = lax.all_to_all(mixed, "dp", 0, 0, tiled=True)
         mixed, others, early = tied(mixed, others, early)
-        others, mlp_w[0] = tied(others, mlp_w[0])
-        mlp_w.append(gather_pages(jnp.concatenate([part[:2] for part in others], axis=0)))
-        next_others = [part[2:] for part in others]
         image_mixed, text_mixed = from_attention(mixed, blocks, image_rows)
         text_mixed = to_blocks(text_mixed, seqs)
         other = back_sum([part[seqs:] for part in image_mixed], out_w[0])
         text_terms = back_dot(text_mixed, out_w[1][0])
         own = back_sum([part[:seqs] for part in image_mixed], out_w[0])
+        others, mlp_w[0], own = tied(others, mlp_w[0], own)
+        mlp_w.append(gather_pages(jnp.concatenate([part[:2] for part in others], axis=0)))
+        next_others = [part[2:] for part in others]
         (attn,) = sum_over_others(own, other, text_terms)
     with jax.named_scope("mlp"):
         middle = [streams[u] + mods[u][:, 2][:, None] * attn[u] for u in range(2)]
@@ -379,8 +373,8 @@
         image_up = [[rows_dot(part, page) for page in up_w[0]] for part in image_two]
         next_attn = None
         if next_shards:
-            image_up[0][0], mlp_w[1], next_shards, next_others = tied(
-                image_up[0][0], mlp_w[1], next_shards, next_others
+            image_up[1][0], mlp_w[1], next_shards, next_others = tied(
+                image_up[1][0], mlp_w[1], next_shards, next_others
             )
             next_attn = (gather_pages(jnp.concatenate([*next_shards, *next_others], axis=0)),)
         image_act = [[gelu_tanh(up).astype(BF16) for up in part] for part in image_up]

time: 1410 us -> 1400 us (level)
  waiting for transfers between devices: 553 us -> 531 us
    unnamed x811 -> x807, local copies, waits for them, and re-layouts: 45.7 us -> 52.4 us
  transfers between devices with their start and end apart: 91 -> 91, of which waited for: 57 -> 52; matrix products, arithmetic and copies ran while one was open for 38% -> 38% of each run, Pallas kernels for 6% -> 6%
where the time goes in v4:
time: 1400 us
  waiting for transfers between devices  531 us (38%)
  matrix products  304 us (22%)
  local copies, waits for them, and re-layouts  179 us (13%)
  starting transfers between devices  150 us (11%)
  other arithmetic  112 us (8%)
  Pallas kernels  83.2 us (6%)
  between operations  19.8 us (1%)
  blocking collectives  15.7 us (1%)
    ppermute x63, waiting for transfers between devices, tensor_swap(): lax.ppermute(values, 'tensor', [(i, i ^ distance) for i in range(count)])  329 us
    dot_general x81, matrix products, dot32(): return jnp.einsum(pattern, left, right, preferred_element_type=F32)  209 us
    all_to_all x2, waiting for transfers between devices, forward_layer(): packed = lax.all_to_all(packed, 'dp', 0, 0, tiled=True)  86.2 us
    ppermute x63, starting transfers between devices, tensor_swap(): lax.ppermute(values, 'tensor', [(i, i ^ distance) for i in range(count)])  85.7 us
    dot_general x24, matrix products, page_grad(): lax.dot_general(flat(left), flat(right), (((0,), (0,)), ((), ())), prefer...  85.2 us
    pallas_call x2, Pallas kernels, attention_backward(): pl.pallas_call(attn_bwd_kernel, grid=(pairs, tiles), in_specs=[pl.BlockSp...  56.3 us
    unnamed x807, local copies, waits for them, and re-layouts  52.4 us
    ppermute x8, waiting for transfers between devices, axis_sum(): lax.ppermute(values, axis, [(i, i ^ step) for i in range(count)])  43.4 us
  transfers between devices with their start and end apart: 91, of which 52 were waited for; matrix products, arithmetic and copies ran while one was open for 38% of the time, Pallas kernels for 6%

profile of v4, /device:TPU:0, one launch (start us, length us, event | category | flops | bytes accessed | tf_op | source)
XLA Modules:
  0.0 1395.4 jit_solution(7375959556037393609)
XLA Ops:
  20.6 15.7 %all_to_all.50 = f32[4,8,2304]{2,1,0:T(8,128)S(1)} all-to-all(f32[4,8,2304]{2,1,0:T(8,128)S(1)} %copy.202), channel_id=1, replica_groups=mesh['dp'=8,'tensor'=4] {'tensor'}, dimensions={0} | all-to-all | bytes 589824 | tf_op jit(solution)/shard_map/modulation/all_to_all | solution.py:641
  39.4 7.9 collective-permute-done.2
  51.3 10.9 collective-permute-done.3
  64.9 12.3 collective-permute-done
  77.3 6.0 all-gather.8.cloned.1.call-done
  106.9 14.7 %collective-permute-done.4 = bf16[2,148,1536]{2,0,1:T(2,128)(2,1)} collective-permute-done((bf16[2,148,1536]{2,0,1:T(2,128)(2,1)}, bf16[2,148,1536]{2,0,1:T(2,128)(2,1)}, u32[]{:S(2)}, u32[]{:S(2)}) %collective-permute-start.4) | collective-permute-done | bytes 909344 | tf_op jit(solution)/shard_map/attention/ppermute | solution.py:25
  127.7 6.7 slice_bitcast_fusion.8
  161.7 45.7 %all-to-all-done.1 = bf16[8,148,1152]{2,1,0:T(8,128)(2,1)} async-done(((bf16[8,148,1152]{2,1,0:T(8,128)(2,1)}), bf16[8,148,1152]{2,1,0:T(8,128)(2,1)}, u32[]{:S(2)}, u32[]{:S(2)}) %all-to-all-start.1) | async-done | bytes 2727968 | tf_op jit(solution)/shard_map/attention/all_to_all | solution.py:353
  213.4 13.5 attention.2
  234.9 5.4 collective-permute-done.8
  240.3 15.8 %all-to-all-done.2 = bf16[8,148,384]{2,1,0:T(8,128)(2,1)} async-done(((bf16[8,148,384]{2,1,0:T(8,128)(2,1)}), bf16[8,148,384]{2,1,0:T(8,128)(2,1)}, u32[]{:S(2)}, u32[]{:S(2)}) %all-to-all-start.2) | async-done | bytes 909344 | tf_op jit(solution)/shard_map/attention/all_to_all | solution.py:357
  279.0 18.1 %collective-permute-done.11 = bf16[2,20,1536]{2,1,0:T(8,128)(2,1)S(1)} collective-permute-done((bf16[2,20,1536]{2,1,0:T(8,128)(2,1)S(1)}, bf16[2,20,1536]{2,1,0:T(8,128)(2,1)S(1)}, u32[]{:S(2)}, u32[]{:S(2)}) %collective-permute-start.11) | collective-permute-done | bytes 122912 | tf_op jit(solution)/shard_map/attention/ppermute | solution.py:25
  307.6 14.9 %collective-permute-done.13 = bf16[2,148,1536]{2,0,1:T(2,128)(2,1)S(1)} collective-permute-done((bf16[2,148,1536]{2,0,1:T(2,128)(2,1)S(1)}, bf16[2,148,1536]{2,0,1:T(2,128)(2,1)S(1)}, u32[]{:S(2)}, u32[]{:S(2)}) %collective-permute-start.13) | collective-permute-done | bytes 909344 | tf_op jit(solution)/shard_map/mlp/ppermute | solution.py:25
  340.7 6.1 multiply_convert_fusion.10
  377.6 12.0 collective-permute-done.17
  410.3 16.2 %collective-permute-done.19 = bf16[2,148,1536]{2,0,1:T(2,128)(2,1)} collective-permute-done((bf16[2,148,1536]{2,0,1:T(2,128)(2,1)}, bf16[2,148,1536]{2,0,1:T(2,128)(2,1)}, u32[]{:S(2)}, u32[]{:S(2)}) %collective-permute-start.19) | collective-permute-done | bytes 909344 | tf_op jit(solution)/shard_map/attention/ppermute | solution.py:25
  436.9 6.7 slice_bitcast_fusion.4
  455.7 12.1 all-to-all-start.3
  473.4 40.5 %all-to-all-done.3 = bf16[8,148,1152]{2,1,0:T(8,128)(2,1)} async-done(((bf16[8,148,1152]{2,1,0:T(8,128)(2,1)}), bf16[8,148,1152]{2,1,0:T(8,128)(2,1)}, u32[]{:S(2)}, u32[]{:S(2)}) %all-to-all-start.3) | async-done | bytes 2727968 | tf_op jit(solution)/shard_map/attention/all_to_all | solution.py:353
  519.9 13.5 attention.3
  549.0 6.6 collective-permute-done.25
  556.5 6.6 all-to-all-done.4
  584.5 17.9 %collective-permute-done.29 = bf16[2,20,1536]{2,1,0:T(8,128)(2,1)S(1)} collective-permute-done((bf16[2,20,1536]{2,1,0:T(8,128)(2,1)S(1)}, bf16[2,20,1536]{2,1,0:T(8,128)(2,1)S(1)}, u32[]{:S(2)}, u32[]{:S(2)}) %collective-permute-start.29) | collective-permute-done | bytes 122912 | tf_op jit(solution)/shard_map/attention/ppermute | solution.py:25
  622.0 12.6 collective-permute-done.31
  705.4 5.5 multiply_reduce_fusion
  722.4 16.2 %collective-permute-done.37 = bf16[2,148,1536]{2,0,1:T(2,128)(2,1)S(1)} collective-permute-done((bf16[2,148,1536]{2,0,1:T(2,128)(2,1)S(1)}, bf16[2,148,1536]{2,0,1:T(2,128)(2,1)S(1)}, u32[]{:S(2)}, u32[]{:S(2)}) %collective-permute-start.37) | collective-permute-done | bytes 909344 | tf_op jit(solution)/shard_map/attention_grad/ppermute | solution.py:25
  750.7 8.0 all-to-all-start.5
  758.8 5.4 fusion.427
  771.4 11.8 all-to-all-done.5
  787.5 28.2 %attention_grad.2 = (bf16[1184,384]{1,0:T(8,128)(2,1)S(1)}, bf16[1184,384]{1,0:T(8,128)(2,1)S(1)}, bf16[1184,384]{1,0:T(8,128)(2,1)S(1)}) custom-call(bf16[1184,1152]{1,0:T(8,128)(2,1)} %reshape.405.q_ref.k_ref.v_ref, bf16[1184,1152]{1,0:T(8,128)(2,1)} %reshape.405.q_ref.k_ref.v_ref, bf16[1184,1152]{1,0:T(8,128)(2,1)} %reshape.405.q_ref.k_ref.v_ref, ...), custom_call_target="tpu_custom_call" | custom-call | flops 10766254080 | bytes 6365184 | tf_op jit(solution)/shard_map/attention_grad/pallas_call | solution.py:212
  840.3 11.8 collective-permute-done.42
  859.2 5.3 multiply_add_fusion.2
  864.5 7.4 all-to-all-done.6
  916.1 17.3 %collective-permute-done.46 = bf16[2,20,1536]{2,1,0:T(8,128)(2,1)S(1)} collective-permute-done((bf16[2,20,1536]{2,1,0:T(8,128)(2,1)S(1)}, bf16[2,20,1536]{2,1,0:T(8,128)(2,1)S(1)}, u32[]{:S(2)}, u32[]{:S(2)}) %collective-permute-start.46) | collective-permute-done | bytes 122912 | tf_op jit(solution)/shard_map/attention_grad/ppermute | solution.py:25
  950.7 5.5 fusion.185
  956.3 5.2 fusion.192
  961.5 13.6 collective-permute-done.48
  1029.8 5.7 multiply_reduce_fusion.4
  1048.1 18.9 %collective-permute-done.54 = bf16[2,148,1536]{2,0,1:T(2,128)(2,1)S(1)} collective-permute-done((bf16[2,148,1536]{2,0,1:T(2,128)(2,1)S(1)}, bf16[2,148,1536]{2,0,1:T(2,128)(2,1)S(1)}, u32[]{:S(2)}, u32[]{:S(2)}) %collective-permute-start.54) | collective-permute-done | bytes 909344 | tf_op jit(solution)/shard_map/attention_grad/ppermute | solution.py:25
  1076.2 8.9 all-to-all-start.7
  1091.5 18.2 %all-to-all-done.7 = bf16[8,148,384]{2,1,0:T(8,128)(2,1)} async-done(((bf16[8,148,384]{2,1,0:T(8,128)(2,1)}), bf16[8,148,384]{2,1,0:T(8,128)(2,1)}, u32[]{:S(2)}, u32[]{:S(2)}) %all-to-all-start.7) | async-done | bytes 909344 | tf_op jit(solution)/shard_map/attention_grad/all_to_all | solution.py:511
  1115.8 28.1 %attention_grad.3 = (bf16[1184,384]{1,0:T(8,128)(2,1)S(1)}, bf16[1184,384]{1,0:T(8,128)(2,1)S(1)}, bf16[1184,384]{1,0:T(8,128)(2,1)S(1)}) custom-call(bf16[1184,1152]{1,0:T(8,128)(2,1)} %reshape.398.q_ref.k_ref.v_ref, bf16[1184,1152]{1,0:T(8,128)(2,1)} %reshape.398.q_ref.k_ref.v_ref, bf16[1184,1152]{1,0:T(8,128)(2,1)} %reshape.398.q_ref.k_ref.v_ref, ...), custom_call_target="tpu_custom_call" | custom-call | flops 10766254080 | bytes 6365184 | tf_op jit(solution)/shard_map/attention_grad/pallas_call | solution.py:212
  1156.4 9.9 collective-permute-done.58
  1174.1 23.6 %collective-permute-done.59 = bf16[192,1536]{1,0:T(8,128)(2,1)} collective-permute-done((bf16[192,1536]{1,0:T(8,128)(2,1)S(1)}, bf16[192,1536]{1,0:T(8,128)(2,1)}, u32[]{:S(2)}, u32[]{:S(2)}) %collective-permute-start.59) | collective-permute-done | bytes 589856 | tf_op jit(solution)/shard_map/attention_grad/ppermute | solution.py:25
  1253.5 17.3 %collective-permute-done.62 = bf16[2,20,1536]{2,1,0:T(8,128)(2,1)S(1)} collective-permute-done((bf16[2,20,1536]{2,1,0:T(8,128)(2,1)S(1)}, bf16[2,20,1536]{2,1,0:T(8,128)(2,1)S(1)}, u32[]{:S(2)}, u32[]{:S(2)}) %collective-permute-start.62) | collective-permute-done | bytes 122912 | tf_op jit(solution)/shard_map/attention_grad/ppermute | solution.py:25
  1270.8 5.3 collective-permute-done.63
  1312.5 12.0 collective-permute-done.68
  1363.2 19.3 %collective-permute-done.65 = bf16[192,1536]{1,0:T(8,128)(2,1)S(1)} collective-permute-done((bf16[192,1536]{1,0:T(8,128)(2,1)S(1)}, bf16[192,1536]{1,0:T(8,128)(2,1)S(1)}, u32[]{:S(2)}, u32[]{:S(2)}) %collective-permute-start.65) | collective-permute-done | bytes 589856 | tf_op jit(solution)/shard_map/modulation_grad/ppermute | solution.py:25
  (1356 shorter events, 728.8 us)
Async XLA Ops:
  7.2 76.1 %all-gather.8.cloned.1.call-start = ((), (), s32[]{:S(2)}) async-start(), calls=%async_computation.14 | async-start | bytes 10616832 | tf_op jit(solution)/shard_map/all_gather | solution.py:572
  14.8 130.3 %all-gather.10.cloned.1.call-start = ((), (), s32[]{:S(2)}) async-start(), calls=%async_computation.15 | async-start | bytes 5308416 | tf_op jit(solution)/shard_map/all_gather | solution.py:572
  48.9 28.4 %collective-permute-start = (bf16[1,192,1536]{2,1,0:T(8,128)(2,1)}, bf16[1,192,1536]{2,1,0:T(8,128)(2,1)}, u32[]{:S(2)}, u32[]{:S(2)}) collective-permute-start(bf16[1,192,1536]{2,1,0:T(8,128)(2,1)} %get-tuple-element.133), channel_id=1, source_target_pairs={{0,2},{1,3},{2,0},{3,1},{4,6},{5,7},{6,4},{7,5},{8,10},{9,11},{10,... | collective-permute-start | bytes 1769480 | tf_op jit(solution)/shard_map/modulation/ppermute | solution.py:25
  83.3 178.0 %all-gather.12.cloned.1.call-start = ((), (), s32[]{:S(2)}) async-start(), calls=%async_computation.16 | async-start | bytes 21233664 | tf_op jit(solution)/shard_map/attention/all_gather | solution.py:572
  95.8 25.8 %collective-permute-start.4 = (bf16[2,148,1536]{2,0,1:T(2,128)(2,1)}, bf16[2,148,1536]{2,0,1:T(2,128)(2,1)}, u32[]{:S(2)}, u32[]{:S(2)}) collective-permute-start(bf16[2,148,1536]{2,0,1:T(2,128)(2,1)} %copy.89), channel_id=1, source_target_pairs={{0,1},{1,0},{2,3},{3,2},{4,5},{5,4},{6,7},{7,6},{8,9},{9,8},{10,11... | collective-permute-start | bytes 2727944 | tf_op jit(solution)/shard_map/attention/ppermute | solution.py:25
  155.6 51.8 %all-to-all-start.1 = ((bf16[8,148,1152]{2,1,0:T(8,128)(2,1)}), bf16[8,148,1152]{2,1,0:T(8,128)(2,1)}, u32[]{:S(2)}, u32[]{:S(2)}) async-start(bf16[8,148,1152]{2,1,0:T(8,128)(2,1)} %bitcast.1164), calls=%async_computation.1 | async-start | bytes 5603328 | tf_op jit(solution)/shard_map/attention/all_to_all | solution.py:353
  160.5 79.8 %collective-permute-start.8 = (bf16[3,192,1536]{2,1,0:T(8,128)(2,1)}, bf16[3,192,1536]{2,1,0:T(8,128)(2,1)}, u32[]{:S(2)}, u32[]{:S(2)}) collective-permute-start(bf16[3,192,1536]{2,1,0:T(8,128)(2,1)} %pad_maximum_fusion.11), channel_id=1, source_target_pairs={{0,2},{1,3},{2,0},{3,1},{4,6},{5,7},{6,4},{7,5},{8,10},{9,11},{10,... | collective-permute-start | bytes 5308424 | tf_op jit(solution)/shard_map/attention/ppermute | solution.py:25
  230.6 25.5 %all-to-all-start.2 = ((bf16[8,148,384]{2,1,0:T(8,128)(2,1)}), bf16[8,148,384]{2,1,0:T(8,128)(2,1)}, u32[]{:S(2)}, u32[]{:S(2)}) async-start(bf16[8,148,384]{2,1,0:T(8,128)(2,1)} %reshape.399), calls=%async_computation.2 | async-start | bytes 1867776 | tf_op jit(solution)/shard_map/attention/all_to_all | solution.py:357
  234.8 94.9 %all-gather.14.cloned.1.call-start = ((), (), s32[]{:S(2)}) async-start(), calls=%async_computation.17 | async-start | bytes 10616832 | tf_op jit(solution)/shard_map/attention/all_gather | solution.py:572
  263.7 173.2 %all-gather.16.cloned.1.call-start = ((), (), s32[]{:S(2)}) async-start(), calls=%async_computation.18 | async-start | bytes 15925248 | tf_op jit(solution)/shard_map/mlp/all_gather | solution.py:572
  274.3 25.7 %collective-permute-start.10 = (bf16[2,148,1536]{2,0,1:T(2,128)(2,1)S(1)}, bf16[2,148,1536]{2,0,1:T(2,128)(2,1)S(1)}, u32[]{:S(2)}, u32[]{:S(2)}) collective-permute-start(bf16[2,148,1536]{2,0,1:T(2,128)(2,1)S(1)} %copy.98), channel_id=1, source_target_pairs={{0,1},{1,0},{2,3},{3,2},{4,5},{5,4},{6,7},{7,6},{8,9},{9,8},{10,11... | collective-permute-start | bytes 2727944 | tf_op jit(solution)/shard_map/attention/ppermute | solution.py:25
  332.6 235.7 %all-gather.18.cloned.1.call-start = ((), (), s32[]{:S(2)}) async-start(), calls=%async_computation.19 | async-start | bytes 21233664 | tf_op jit(solution)/shard_map/attention/all_gather | solution.py:572
  366.1 28.4 %collective-permute-start.16 = (bf16[2,148,1536]{2,0,1:T(2,128)(2,1)S(1)}, bf16[2,148,1536]{2,0,1:T(2,128)(2,1)S(1)}, u32[]{:S(2)}, u32[]{:S(2)}) collective-permute-start(bf16[2,148,1536]{2,0,1:T(2,128)(2,1)S(1)} %copy.105), channel_id=1, source_target_pairs={{0,1},{1,0},{2,3},{3,2},{4,5},{5,4},{6,7},{7,6},{8,9},{9,8},{10,11... | collective-permute-start | bytes 2727944 | tf_op jit(solution)/shard_map/mlp/ppermute | solution.py:25
  401.9 24.7 %collective-permute-start.19 = (bf16[2,148,1536]{2,0,1:T(2,128)(2,1)}, bf16[2,148,1536]{2,0,1:T(2,128)(2,1)}, u32[]{:S(2)}, u32[]{:S(2)}) collective-permute-start(bf16[2,148,1536]{2,0,1:T(2,128)(2,1)} %copy.110), channel_id=1, source_target_pairs={{0,1},{1,0},{2,3},{3,2},{4,5},{5,4},{6,7},{7,6},{8,9},{9,8},{10,11... | collective-permute-start | bytes 2727944 | tf_op jit(solution)/shard_map/attention/ppermute | solution.py:25
  455.7 58.2 %all-to-all-start.3 = ((bf16[8,148,1152]{2,1,0:T(8,128)(2,1)}), bf16[8,148,1152]{2,1,0:T(8,128)(2,1)}, u32[]{:S(2)}, u32[]{:S(2)}) async-start(bf16[8,148,1152]{2,1,0:T(8,128)(2,1)} %bitcast.1163), calls=%async_computation.3 | async-start | bytes 5603328 | tf_op jit(solution)/shard_map/attention/all_to_all | solution.py:353
  467.8 88.7 %collective-permute-start.23 = (bf16[2,192,1536]{2,1,0:T(8,128)(2,1)}, bf16[2,192,1536]{2,1,0:T(8,128)(2,1)}, u32[]{:S(2)}, u32[]{:S(2)}) collective-permute-start(bf16[2,192,1536]{2,1,0:T(8,128)(2,1)} %pad_maximum_fusion.17), channel_id=1, source_target_pairs={{0,2},{1,3},{2,0},{3,1},{4,6},{5,7},{6,4},{7,5},{8,10},{9,11},{10,... | collective-permute-start | bytes 3538952 | tf_op jit(solution)/shard_map/attention/ppermute | solution.py:25
  470.8 74.5 %collective-permute-start.24 = (bf16[2,148,1536]{2,0,1:T(2,128)(2,1)}, bf16[2,148,1536]{2,0,1:T(2,128)(2,1)}, u32[]{:S(2)}, u32[]{:S(2)}) collective-permute-start(bf16[2,148,1536]{2,0,1:T(2,128)(2,1)} %copy.114), channel_id=1, source_target_pairs={{0,1},{1,0},{2,3},{3,2},{4,5},{5,4},{6,7},{7,6},{8,9},{9,8},{10,11... | collective-permute-start | bytes 2727944 | tf_op jit(solution)/shard_map/attention/ppermute | solution.py:25
  537.1 26.0 %all-to-all-start.4 = ((bf16[8,148,384]{2,1,0:T(8,128)(2,1)}), bf16[8,148,384]{2,1,0:T(8,128)(2,1)}, u32[]{:S(2)}, u32[]{:S(2)}) async-start(bf16[8,148,384]{2,1,0:T(8,128)(2,1)} %reshape.406), calls=%async_computation.4 | async-start | bytes 1867776 | tf_op jit(solution)/shard_map/attention/all_to_all | solution.py:357
  541.4 125.0 %all-gather.20.cloned.1.call-start = ((), (), s32[]{:S(2)}) async-start(), calls=%async_computation.20 | async-start | bytes 10616832 | tf_op jit(solution)/shard_map/attention/all_gather | solution.py:572
  568.3 335.8 %reduce-scatter.5.cloned.1.call-start = ((), (), s32[]{:S(2)}) async-start(), calls=%async_computation.21 | async-start | bytes 31850496 | tf_op jit(solution)/shard_map/mlp_grad/reduce_scatter | solution.py:412
  579.6 25.5 %collective-permute-start.28 = (bf16[2,148,1536]{2,0,1:T(2,128)(2,1)S(1)}, bf16[2,148,1536]{2,0,1:T(2,128)(2,1)S(1)}, u32[]{:S(2)}, u32[]{:S(2)}) collective-permute-start(bf16[2,148,1536]{2,0,1:T(2,128)(2,1)S(1)} %copy.121), channel_id=1, source_target_pairs={{0,1},{1,0},{2,3},{3,2},{4,5},{5,4},{6,7},{7,6},{8,9},{9,8},{10,11... | collective-permute-start | bytes 2727944 | tf_op jit(solution)/shard_map/attention/ppermute | solution.py:25
  608.1 26.6 %collective-permute-start.32 = (bf16[2,20,1536]{2,1,0:T(8,128)(2,1)S(1)}, bf16[2,20,1536]{2,1,0:T(8,128)(2,1)S(1)}, u32[]{:S(2)}, u32[]{:S(2)}) collective-permute-start(bf16[2,20,1536]{2,1,0:T(8,128)(2,1)S(1)} %add_convert_fusion.3), channel_id=1, source_target_pairs={{0,2},{1,3},{2,0},{3,1},{4,6},{5,7},{6,4},{7,5},{8,10},{9,11},{10,... | collective-permute-start | bytes 368648 | tf_op jit(solution)/shard_map/mlp/ppermute | solution.py:25
  608.8 25.9 %collective-permute-start.33 = (bf16[2,20,1536]{2,1,0:T(8,128)(2,1)S(1)}, bf16[2,20,1536]{2,1,0:T(8,128)(2,1)S(1)}, u32[]{:S(2)}, u32[]{:S(2)}) collective-permute-start(bf16[2,20,1536]{2,1,0:T(8,128)(2,1)S(1)} %add_convert_fusion.3), channel_id=1, source_target_pairs={{0,3},{1,2},{2,1},{3,0},{4,7},{5,6},{6,5},{7,4},{8,11},{9,10},{10,... | collective-permute-start | bytes 368648 | tf_op jit(solution)/shard_map/mlp/ppermute | solution.py:25
  641.1 51.1 %collective-permute-start.35 = (bf16[2,20,1536]{2,1,0:T(8,128)(2,1)}, bf16[2,20,1536]{2,1,0:T(8,128)(2,1)}, u32[]{:S(2)}, u32[]{:S(2)}) collective-permute-start(bf16[2,20,1536]{2,1,0:T(8,128)(2,1)} %get-tuple-element.422), channel_id=1, source_target_pairs={{0,2},{1,3},{2,0},{3,1},{4,6},{5,7},{6,4},{7,5},{8,10},{9,11},{10,... | collective-permute-start | bytes 368648 | tf_op jit(solution)/shard_map/mlp_grad/ppermute | solution.py:25
  641.1 51.1 %collective-permute-start.36 = (bf16[2,20,1536]{2,1,0:T(8,128)(2,1)}, bf16[2,20,1536]{2,1,0:T(8,128)(2,1)}, u32[]{:S(2)}, u32[]{:S(2)}) collective-permute-start(bf16[2,20,1536]{2,1,0:T(8,128)(2,1)} %get-tuple-element.421), channel_id=1, source_target_pairs={{0,3},{1,2},{2,1},{3,0},{4,7},{5,6},{6,5},{7,4},{8,11},{9,10},{10,... | collective-permute-start | bytes 368648 | tf_op jit(solution)/shard_map/mlp_grad/ppermute | solution.py:25
  750.7 32.6 %all-to-all-start.5 = ((bf16[8,148,384]{2,1,0:T(8,128)(2,1)}), bf16[8,148,384]{2,1,0:T(8,128)(2,1)}, u32[]{:S(2)}, u32[]{:S(2)}) async-start(bf16[8,148,384]{2,1,0:T(8,128)(2,1)} %bitcast.1179), calls=%async_computation.5 | async-start | bytes 1867776 | tf_op jit(solution)/shard_map/attention_grad/all_to_all | solution.py:511
  821.7 50.1 %all-to-all-start.6 = ((bf16[8,148,1152]{2,1,0:T(8,128)(2,1)}), bf16[8,148,1152]{2,1,0:T(8,128)(2,1)}, u32[]{:S(2)}, u32[]{:S(2)}) async-start(bf16[8,148,1152]{2,1,0:T(8,128)(2,1)} %reshape.412), calls=%async_computation.6 | async-start | bytes 5603328 | tf_op jit(solution)/shard_map/attention_grad/all_to_all | solution.py:522
  826.1 319.5 %reduce-scatter.7.cloned.1.call-start = ((), (), s32[]{:S(2)}) async-start(), calls=%async_computation.22 | async-start | bytes 15925248 | tf_op jit(solution)/shard_map/attention_grad/reduce_scatter | solution.py:412
  828.4 28.8 %collective-permute-start.41 = (bf16[2,148,1536]{2,0,1:T(2,128)(2,1)S(1)}, bf16[2,148,1536]{2,0,1:T(2,128)(2,1)S(1)}, u32[]{:S(2)}, u32[]{:S(2)}) collective-permute-start(bf16[2,148,1536]{2,0,1:T(2,128)(2,1)S(1)} %copy.138), channel_id=1, source_target_pairs={{0,1},{1,0},{2,3},{3,2},{4,5},{5,4},{6,7},{7,6},{8,9},{9,8},{10,11... | collective-permute-start | bytes 2727944 | tf_op jit(solution)/shard_map/attention_grad/ppermute | solution.py:25
  904.1 324.7 %reduce-scatter.9.cloned.1.call-start = ((), (), s32[]{:S(2)}) async-start(), calls=%async_computation.23 | async-start | bytes 31850496 | tf_op jit(solution)/shard_map/mlp_grad/reduce_scatter | solution.py:412
  908.8 29.3 %collective-permute-start.45 = (bf16[2,148,1536]{2,0,1:T(2,128)(2,1)S(1)}, bf16[2,148,1536]{2,0,1:T(2,128)(2,1)S(1)}, u32[]{:S(2)}, u32[]{:S(2)}) collective-permute-start(bf16[2,148,1536]{2,0,1:T(2,128)(2,1)S(1)} %copy.145), channel_id=1, source_target_pairs={{0,1},{1,0},{2,3},{3,2},{4,5},{5,4},{6,7},{7,6},{8,9},{9,8},{10,11... | collective-permute-start | bytes 2727944 | tf_op jit(solution)/shard_map/attention_grad/ppermute | solution.py:25
  913.2 24.9 %collective-permute-start.47 = (bf16[2,20,1536]{2,1,0:T(8,128)(2,1)S(1)}, bf16[2,20,1536]{2,1,0:T(8,128)(2,1)S(1)}, u32[]{:S(2)}, u32[]{:S(2)}) collective-permute-start(bf16[2,20,1536]{2,1,0:T(8,128)(2,1)S(1)} %get-tuple-element.415), channel_id=1, source_target_pairs={{0,3},{1,2},{2,1},{3,0},{4,7},{5,6},{6,5},{7,4},{8,11},{9,10},{10,... | collective-permute-start | bytes 368648 | tf_op jit(solution)/shard_map/attention_grad/ppermute | solution.py:25
  946.3 29.5 %collective-permute-start.49 = (bf16[2,20,1536]{2,1,0:T(8,128)(2,1)S(1)}, bf16[2,20,1536]{2,1,0:T(8,128)(2,1)S(1)}, u32[]{:S(2)}, u32[]{:S(2)}) collective-permute-start(bf16[2,20,1536]{2,1,0:T(8,128)(2,1)S(1)} %multiply_convert_fusion.14), channel_id=1, source_target_pairs={{0,2},{1,3},{2,0},{3,1},{4,6},{5,7},{6,4},{7,5},{8,10},{9,11},{10,... | collective-permute-start | bytes 368648 | tf_op jit(solution)/shard_map/mlp_grad/ppermute | solution.py:25
  946.3 29.4 %collective-permute-start.50 = (bf16[2,20,1536]{2,1,0:T(8,128)(2,1)S(1)}, bf16[2,20,1536]{2,1,0:T(8,128)(2,1)S(1)}, u32[]{:S(2)}, u32[]{:S(2)}) collective-permute-start(bf16[2,20,1536]{2,1,0:T(8,128)(2,1)S(1)} %multiply_convert_fusion.14), channel_id=1, source_target_pairs={{0,3},{1,2},{2,1},{3,0},{4,7},{5,6},{6,5},{7,4},{8,11},{9,10},{10,... | collective-permute-start | bytes 368648 | tf_op jit(solution)/shard_map/mlp_grad/ppermute | solution.py:25
  948.9 26.2 %collective-permute-start.48 = (bf16[2,148,1536]{2,0,1:T(2,128)(2,1)S(1)}, bf16[2,148,1536]{2,0,1:T(2,128)(2,1)S(1)}, u32[]{:S(2)}, u32[]{:S(2)}) collective-permute-start(bf16[2,148,1536]{2,0,1:T(2,128)(2,1)S(1)} %copy.148), channel_id=1, source_target_pairs={{0,1},{1,0},{2,3},{3,2},{4,5},{5,4},{6,7},{7,6},{8,9},{9,8},{10,11... | collective-permute-start | bytes 2727944 | tf_op jit(solution)/shard_map/mlp_grad/ppermute | solution.py:25
  992.2 29.9 %collective-permute-start.51 = (bf16[2,148,1536]{2,0,1:T(2,128)(2,1)}, bf16[2,148,1536]{2,0,1:T(2,128)(2,1)}, u32[]{:S(2)}, u32[]{:S(2)}) collective-permute-start(bf16[2,148,1536]{2,0,1:T(2,128)(2,1)} %copy.151), channel_id=1, source_target_pairs={{0,1},{1,0},{2,3},{3,2},{4,5},{5,4},{6,7},{7,6},{8,9},{9,8},{10,11... | collective-permute-start | bytes 2727944 | tf_op jit(solution)/shard_map/mlp_grad/ppermute | solution.py:25
  992.2 29.9 %collective-permute-start.52 = (bf16[2,20,1536]{2,1,0:T(8,128)(2,1)}, bf16[2,20,1536]{2,1,0:T(8,128)(2,1)}, u32[]{:S(2)}, u32[]{:S(2)}) collective-permute-start(bf16[2,20,1536]{2,1,0:T(8,128)(2,1)} %get-tuple-element.413), channel_id=1, source_target_pairs={{0,2},{1,3},{2,0},{3,1},{4,6},{5,7},{6,4},{7,5},{8,10},{9,11},{10,... | collective-permute-start | bytes 368648 | tf_op jit(solution)/shard_map/mlp_grad/ppermute | solution.py:25
  994.3 27.7 %collective-permute-start.53 = (bf16[2,20,1536]{2,1,0:T(8,128)(2,1)}, bf16[2,20,1536]{2,1,0:T(8,128)(2,1)}, u32[]{:S(2)}, u32[]{:S(2)}) collective-permute-start(bf16[2,20,1536]{2,1,0:T(8,128)(2,1)} %get-tuple-element.412), channel_id=1, source_target_pairs={{0,3},{1,2},{2,1},{3,0},{4,7},{5,6},{6,5},{7,4},{8,11},{9,10},{10,... | collective-permute-start | bytes 368648 | tf_op jit(solution)/shard_map/mlp_grad/ppermute | solution.py:25
  1041.4 25.5 %collective-permute-start.54 = (bf16[2,148,1536]{2,0,1:T(2,128)(2,1)S(1)}, bf16[2,148,1536]{2,0,1:T(2,128)(2,1)S(1)}, u32[]{:S(2)}, u32[]{:S(2)}) collective-permute-start(bf16[2,148,1536]{2,0,1:T(2,128)(2,1)S(1)} %copy.160), channel_id=1, source_target_pairs={{0,1},{1,0},{2,3},{3,2},{4,5},{5,4},{6,7},{7,6},{8,9},{9,8},{10,11... | collective-permute-start | bytes 2727944 | tf_op jit(solution)/shard_map/attention_grad/ppermute | solution.py:25
  1076.2 33.5 %all-to-all-start.7 = ((bf16[8,148,384]{2,1,0:T(8,128)(2,1)}), bf16[8,148,384]{2,1,0:T(8,128)(2,1)}, u32[]{:S(2)}, u32[]{:S(2)}) async-start(bf16[8,148,384]{2,1,0:T(8,128)(2,1)} %bitcast.1180), calls=%async_computation.8 | async-start | bytes 1867776 | tf_op jit(solution)/shard_map/attention_grad/all_to_all | solution.py:511
  1115.7 50.6 %collective-permute-start.58 = (bf16[192,3072]{1,0:T(8,128)(2,1)}, bf16[192,3072]{1,0:T(8,128)(2,1)}, u32[]{:S(2)}, u32[]{:S(2)}) collective-permute-start(bf16[192,3072]{1,0:T(8,128)(2,1)} %get-tuple-element.353), channel_id=1, source_target_pairs={{0,2},{1,3},{2,0},{3,1},{4,6},{5,7},{6,4},{7,5},{8,10},{9,11},{10,... | collective-permute-start | bytes 3538952 | tf_op jit(solution)/shard_map/attention_grad/ppermute | solution.py:25
  1149.9 50.6 %all-to-all-start.8 = ((bf16[8,148,1152]{2,1,0:T(8,128)(2,1)}), bf16[8,148,1152]{2,1,0:T(8,128)(2,1)}, u32[]{:S(2)}, u32[]{:S(2)}) async-start(bf16[8,148,1152]{2,1,0:T(8,128)(2,1)} %reshape.422), calls=%async_computation.10 | async-start | bytes 5603328 | tf_op jit(solution)/shard_map/attention_grad/all_to_all | solution.py:522
  1154.3 195.6 %reduce-scatter.11.cloned.1.call-start = ((), (), s32[]{:S(2)}) async-start(), calls=%async_computation.24 | async-start | bytes 15925248 | tf_op jit(solution)/shard_map/attention_grad/reduce_scatter | solution.py:412
  1169.7 28.0 %collective-permute-start.59 = (bf16[192,1536]{1,0:T(8,128)(2,1)S(1)}, bf16[192,1536]{1,0:T(8,128)(2,1)}, u32[]{:S(2)}, u32[]{:S(2)}) collective-permute-start(bf16[192,1536]{1,0:T(8,128)(2,1)S(1)} %slice.960), channel_id=1, source_target_pairs={{0,2},{1,3},{2,0},{3,1},{4,6},{5,7},{6,4},{7,5},{8,10},{9,11},{10,... | collective-permute-start | bytes 1769480 | tf_op jit(solution)/shard_map/attention_grad/ppermute | solution.py:25
  1245.7 30.4 %collective-permute-start.61 = (bf16[2,148,1536]{2,0,1:T(2,128)(2,1)S(1)}, bf16[2,148,1536]{2,0,1:T(2,128)(2,1)S(1)}, u32[]{:S(2)}, u32[]{:S(2)}) collective-permute-start(bf16[2,148,1536]{2,0,1:T(2,128)(2,1)S(1)} %copy.166), channel_id=1, source_target_pairs={{0,1},{1,0},{2,3},{3,2},{4,5},{5,4},{6,7},{7,6},{8,9},{9,8},{10,11... | collective-permute-start | bytes 2727944 | tf_op jit(solution)/shard_map/attention_grad/ppermute | solution.py:25
  1251.7 24.5 %collective-permute-start.63 = (bf16[2,20,1536]{2,1,0:T(8,128)(2,1)S(1)}, bf16[2,20,1536]{2,1,0:T(8,128)(2,1)S(1)}, u32[]{:S(2)}, u32[]{:S(2)}) collective-permute-start(bf16[2,20,1536]{2,1,0:T(8,128)(2,1)S(1)} %get-tuple-element.409), channel_id=1, source_target_pairs={{0,3},{1,2},{2,1},{3,0},{4,7},{5,6},{6,5},{7,4},{8,11},{9,10},{10,... | collective-permute-start | bytes 368648 | tf_op jit(solution)/shard_map/attention_grad/ppermute | solution.py:25
  1295.2 54.7 %collective-permute-start.64 = (bf16[192,3072]{1,0:T(8,128)(2,1)}, bf16[192,3072]{1,0:T(8,128)(2,1)}, u32[]{:S(2)}, u32[]{:S(2)}) collective-permute-start(bf16[192,3072]{1,0:T(8,128)(2,1)} %slice.978), channel_id=1, source_target_pairs={{0,2},{1,3},{2,0},{3,1},{4,6},{5,7},{6,4},{7,5},{8,10},{9,11},{10,... | collective-permute-start | bytes 3538952 | tf_op jit(solution)/shard_map/modulation_grad/ppermute | solution.py:25
  1354.8 27.8 %collective-permute-start.65 = (bf16[192,1536]{1,0:T(8,128)(2,1)S(1)}, bf16[192,1536]{1,0:T(8,128)(2,1)S(1)}, u32[]{:S(2)}, u32[]{:S(2)}) collective-permute-start(bf16[192,1536]{1,0:T(8,128)(2,1)S(1)} %slice.980), channel_id=1, source_target_pairs={{0,2},{1,3},{2,0},{3,1},{4,6},{5,7},{6,4},{7,5},{8,10},{9,11},{10,... | collective-permute-start | bytes 1769480 | tf_op jit(solution)/shard_map/modulation_grad/ppermute | solution.py:25
  (416 other events, 3489.1 us)
Sparse Core Ops, SparseCore 0:
  15.0 68.2 all-gather.7
  85.2 39.1 all-gather.9
  127.8 127.9 all-gather.11
  263.8 57.9 all-gather.13
  332.7 80.8 all-gather.15
  428.6 134.1 all-gather.17
  568.4 57.9 all-gather.19
  696.7 206.4 reduce-scatter.4
  906.7 100.7 reduce-scatter.6
  1022.2 206.5 reduce-scatter.8
  1232.4 106.6 reduce-scatter.10

commit v5 on v4

--- a/solution.py
+++ b/solution.py
@@ -720,9 +720,7 @@
     with jax.named_scope("weight_grads"):
         mlp_done = [mlp_shard(mlp_parts)] + [layer[0] for layer in shards[1:]]
         grad_up, grad_down = [jnp.stack(parts) for parts in zip(*mlp_done)]
-        attn_parts, grad_up, grad_down, grad_w_mod, grad_cond = tied(
-            attn_parts, grad_up, grad_down, grad_w_mod, grad_cond
-        )
+        attn_parts, grad_up, grad_down = tied(attn_parts, grad_up, grad_down)
         attn_done = [attention_shard(attn_parts)] + [layer[1] for layer in shards[1:]]
         grad_qkv, grad_out = [jnp.stack(parts) for parts in zip(*attn_done)]
     return (

time: 1400 us -> 1400 us (level)
  no operation moved by 1% of the time
where the time goes in v5:
time: 1400 us
  waiting for transfers between devices  531 us (38%)
  matrix products  304 us (22%)
  local copies, waits for them, and re-layouts  179 us (13%)
  starting transfers between devices  150 us (11%)
  other arithmetic  112 us (8%)
  Pallas kernels  83.2 us (6%)
  between operations  19.8 us (1%)
  blocking collectives  15.7 us (1%)
    ppermute x63, waiting for transfers between devices, tensor_swap(): lax.ppermute(values, 'tensor', [(i, i ^ distance) for i in range(count)])  329 us
    dot_general x81, matrix products, dot32(): return jnp.einsum(pattern, left, right, preferred_element_type=F32)  209 us
    all_to_all x2, waiting for transfers between devices, forward_layer(): packed = lax.all_to_all(packed, 'dp', 0, 0, tiled=True)  86.2 us
    ppermute x63, starting transfers between devices, tensor_swap(): lax.ppermute(values, 'tensor', [(i, i ^ distance) for i in range(count)])  85.7 us
    dot_general x24, matrix products, page_grad(): lax.dot_general(flat(left), flat(right), (((0,), (0,)), ((), ())), prefer...  85.2 us
    pallas_call x2, Pallas kernels, attention_backward(): pl.pallas_call(attn_bwd_kernel, grid=(pairs, tiles), in_specs=[pl.BlockSp...  56.3 us
    unnamed x807, local copies, waits for them, and re-layouts  52.4 us
    ppermute x8, waiting for transfers between devices, axis_sum(): lax.ppermute(values, axis, [(i, i ^ step) for i in range(count)])  43.4 us
  transfers between devices with their start and end apart: 91, of which 52 were waited for; matrix products, arithmetic and copies ran while one was open for 38% of the time, Pallas kernels for 6%

profile of v5, /device:TPU:0, one launch (start us, length us, event | category | flops | bytes accessed | tf_op | source)
XLA Modules:
  0.0 1395.4 jit_solution(1051758614463204005)
XLA Ops:
  20.6 15.7 %all_to_all.50 = f32[4,8,2304]{2,1,0:T(8,128)S(1)} all-to-all(f32[4,8,2304]{2,1,0:T(8,128)S(1)} %copy.202), channel_id=1, replica_groups=mesh['dp'=8,'tensor'=4] {'tensor'}, dimensions={0} | all-to-all | bytes 589824 | tf_op jit(solution)/shard_map/modulation/all_to_all | solution.py:641
  39.4 7.9 collective-permute-done.2
  51.3 10.9 collective-permute-done.3
  64.9 12.3 collective-permute-done
  77.3 6.0 all-gather.8.cloned.1.call-done
  106.9 14.7 %collective-permute-done.4 = bf16[2,148,1536]{2,0,1:T(2,128)(2,1)} collective-permute-done((bf16[2,148,1536]{2,0,1:T(2,128)(2,1)}, bf16[2,148,1536]{2,0,1:T(2,128)(2,1)}, u32[]{:S(2)}, u32[]{:S(2)}) %collective-permute-start.4) | collective-permute-done | bytes 909344 | tf_op jit(solution)/shard_map/attention/ppermute | solution.py:25
  127.7 6.7 slice_bitcast_fusion.8
  161.7 45.7 %all-to-all-done.1 = bf16[8,148,1152]{2,1,0:T(8,128)(2,1)} async-done(((bf16[8,148,1152]{2,1,0:T(8,128)(2,1)}), bf16[8,148,1152]{2,1,0:T(8,128)(2,1)}, u32[]{:S(2)}, u32[]{:S(2)}) %all-to-all-start.1) | async-done | bytes 2727968 | tf_op jit(solution)/shard_map/attention/all_to_all | solution.py:353
  213.4 13.5 attention.2
  234.9 5.4 collective-permute-done.8
  240.3 15.8 %all-to-all-done.2 = bf16[8,148,384]{2,1,0:T(8,128)(2,1)} async-done(((bf16[8,148,384]{2,1,0:T(8,128)(2,1)}), bf16[8,148,384]{2,1,0:T(8,128)(2,1)}, u32[]{:S(2)}, u32[]{:S(2)}) %all-to-all-start.2) | async-done | bytes 909344 | tf_op jit(solution)/shard_map/attention/all_to_all | solution.py:357
  279.0 18.1 %collective-permute-done.11 = bf16[2,20,1536]{2,1,0:T(8,128)(2,1)S(1)} collective-permute-done((bf16[2,20,1536]{2,1,0:T(8,128)(2,1)S(1)}, bf16[2,20,1536]{2,1,0:T(8,128)(2,1)S(1)}, u32[]{:S(2)}, u32[]{:S(2)}) %collective-permute-start.11) | collective-permute-done | bytes 122912 | tf_op jit(solution)/shard_map/attention/ppermute | solution.py:25
  307.6 14.9 %collective-permute-done.13 = bf16[2,148,1536]{2,0,1:T(2,128)(2,1)S(1)} collective-permute-done((bf16[2,148,1536]{2,0,1:T(2,128)(2,1)S(1)}, bf16[2,148,1536]{2,0,1:T(2,128)(2,1)S(1)}, u32[]{:S(2)}, u32[]{:S(2)}) %collective-permute-start.13) | collective-permute-done | bytes 909344 | tf_op jit(solution)/shard_map/mlp/ppermute | solution.py:25
  340.7 6.1 multiply_convert_fusion.10
  377.6 12.0 collective-permute-done.17
  410.3 16.2 %collective-permute-done.19 = bf16[2,148,1536]{2,0,1:T(2,128)(2,1)} collective-permute-done((bf16[2,148,1536]{2,0,1:T(2,128)(2,1)}, bf16[2,148,1536]{2,0,1:T(2,128)(2,1)}, u32[]{:S(2)}, u32[]{:S(2)}) %collective-permute-start.19) | collective-permute-done | bytes 909344 | tf_op jit(solution)/shard_map/attention/ppermute | solution.py:25
  436.9 6.7 slice_bitcast_fusion.4
  455.7 12.1 all-to-all-start.3
  473.4 40.5 %all-to-all-done.3 = bf16[8,148,1152]{2,1,0:T(8,128)(2,1)} async-done(((bf16[8,148,1152]{2,1,0:T(8,128)(2,1)}), bf16[8,148,1152]{2,1,0:T(8,128)(2,1)}, u32[]{:S(2)}, u32[]{:S(2)}) %all-to-all-start.3) | async-done | bytes 2727968 | tf_op jit(solution)/shard_map/attention/all_to_all | solution.py:353
  519.9 13.5 attention.3
  549.0 6.6 collective-permute-done.25
  556.5 6.6 all-to-all-done.4
  584.5 17.9 %collective-permute-done.29 = bf16[2,20,1536]{2,1,0:T(8,128)(2,1)S(1)} collective-permute-done((bf16[2,20,1536]{2,1,0:T(8,128)(2,1)S(1)}, bf16[2,20,1536]{2,1,0:T(8,128)(2,1)S(1)}, u32[]{:S(2)}, u32[]{:S(2)}) %collective-permute-start.29) | collective-permute-done | bytes 122912 | tf_op jit(solution)/shard_map/attention/ppermute | solution.py:25
  622.0 12.6 collective-permute-done.31
  705.4 5.5 multiply_reduce_fusion
  722.4 16.2 %collective-permute-done.37 = bf16[2,148,1536]{2,0,1:T(2,128)(2,1)S(1)} collective-permute-done((bf16[2,148,1536]{2,0,1:T(2,128)(2,1)S(1)}, bf16[2,148,1536]{2,0,1:T(2,128)(2,1)S(1)}, u32[]{:S(2)}, u32[]{:S(2)}) %collective-permute-start.37) | collective-permute-done | bytes 909344 | tf_op jit(solution)/shard_map/attention_grad/ppermute | solution.py:25
  750.7 8.0 all-to-all-start.5
  758.8 5.4 fusion.427
  771.4 11.8 all-to-all-done.5
  787.5 28.2 %attention_grad.2 = (bf16[1184,384]{1,0:T(8,128)(2,1)S(1)}, bf16[1184,384]{1,0:T(8,128)(2,1)S(1)}, bf16[1184,384]{1,0:T(8,128)(2,1)S(1)}) custom-call(bf16[1184,1152]{1,0:T(8,128)(2,1)} %reshape.405.q_ref.k_ref.v_ref, bf16[1184,1152]{1,0:T(8,128)(2,1)} %reshape.405.q_ref.k_ref.v_ref, bf16[1184,1152]{1,0:T(8,128)(2,1)} %reshape.405.q_ref.k_ref.v_ref, ...), custom_call_target="tpu_custom_call" | custom-call | flops 10766254080 | bytes 6365184 | tf_op jit(solution)/shard_map/attention_grad/pallas_call | solution.py:212
  840.3 11.8 collective-permute-done.42
  859.2 5.3 multiply_add_fusion.2
  864.5 7.4 all-to-all-done.6
  916.1 17.3 %collective-permute-done.46 = bf16[2,20,1536]{2,1,0:T(8,128)(2,1)S(1)} collective-permute-done((bf16[2,20,1536]{2,1,0:T(8,128)(2,1)S(1)}, bf16[2,20,1536]{2,1,0:T(8,128)(2,1)S(1)}, u32[]{:S(2)}, u32[]{:S(2)}) %collective-permute-start.46) | collective-permute-done | bytes 122912 | tf_op jit(solution)/shard_map/attention_grad/ppermute | solution.py:25
  950.7 5.5 fusion.185
  956.3 5.2 fusion.192
  961.5 13.6 collective-permute-done.48
  1029.8 5.7 multiply_reduce_fusion.4
  1048.1 18.9 %collective-permute-done.54 = bf16[2,148,1536]{2,0,1:T(2,128)(2,1)S(1)} collective-permute-done((bf16[2,148,1536]{2,0,1:T(2,128)(2,1)S(1)}, bf16[2,148,1536]{2,0,1:T(2,128)(2,1)S(1)}, u32[]{:S(2)}, u32[]{:S(2)}) %collective-permute-start.54) | collective-permute-done | bytes 909344 | tf_op jit(solution)/shard_map/attention_grad/ppermute | solution.py:25
  1076.2 8.9 all-to-all-start.7
  1091.5 18.2 %all-to-all-done.7 = bf16[8,148,384]{2,1,0:T(8,128)(2,1)} async-done(((bf16[8,148,384]{2,1,0:T(8,128)(2,1)}), bf16[8,148,384]{2,1,0:T(8,128)(2,1)}, u32[]{:S(2)}, u32[]{:S(2)}) %all-to-all-start.7) | async-done | bytes 909344 | tf_op jit(solution)/shard_map/attention_grad/all_to_all | solution.py:511
  1115.8 28.1 %attention_grad.3 = (bf16[1184,384]{1,0:T(8,128)(2,1)S(1)}, bf16[1184,384]{1,0:T(8,128)(2,1)S(1)}, bf16[1184,384]{1,0:T(8,128)(2,1)S(1)}) custom-call(bf16[1184,1152]{1,0:T(8,128)(2,1)} %reshape.398.q_ref.k_ref.v_ref, bf16[1184,1152]{1,0:T(8,128)(2,1)} %reshape.398.q_ref.k_ref.v_ref, bf16[1184,1152]{1,0:T(8,128)(2,1)} %reshape.398.q_ref.k_ref.v_ref, ...), custom_call_target="tpu_custom_call" | custom-call | flops 10766254080 | bytes 6365184 | tf_op jit(solution)/shard_map/attention_grad/pallas_call | solution.py:212
  1156.4 9.9 collective-permute-done.58
  1174.1 23.6 %collective-permute-done.59 = bf16[192,1536]{1,0:T(8,128)(2,1)} collective-permute-done((bf16[192,1536]{1,0:T(8,128)(2,1)S(1)}, bf16[192,1536]{1,0:T(8,128)(2,1)}, u32[]{:S(2)}, u32[]{:S(2)}) %collective-permute-start.59) | collective-permute-done | bytes 589856 | tf_op jit(solution)/shard_map/attention_grad/ppermute | solution.py:25
  1253.5 17.3 %collective-permute-done.62 = bf16[2,20,1536]{2,1,0:T(8,128)(2,1)S(1)} collective-permute-done((bf16[2,20,1536]{2,1,0:T(8,128)(2,1)S(1)}, bf16[2,20,1536]{2,1,0:T(8,128)(2,1)S(1)}, u32[]{:S(2)}, u32[]{:S(2)}) %collective-permute-start.62) | collective-permute-done | bytes 122912 | tf_op jit(solution)/shard_map/attention_grad/ppermute | solution.py:25
  1270.8 5.3 collective-permute-done.63
  1312.5 12.0 collective-permute-done.66
  1363.2 19.3 %collective-permute-done.70 = bf16[192,1536]{1,0:T(8,128)(2,1)S(1)} collective-permute-done((bf16[192,1536]{1,0:T(8,128)(2,1)S(1)}, bf16[192,1536]{1,0:T(8,128)(2,1)S(1)}, u32[]{:S(2)}, u32[]{:S(2)}) %collective-permute-start.70) | collective-permute-done | bytes 589856 | tf_op jit(solution)/shard_map/modulation_grad/ppermute | solution.py:25
  (1356 shorter events, 728.8 us)
Async XLA Ops:
  7.2 76.1 %all-gather.8.cloned.1.call-start = ((), (), s32[]{:S(2)}) async-start(), calls=%async_computation.14 | async-start | bytes 10616832 | tf_op jit(solution)/shard_map/all_gather | solution.py:572
  14.8 130.3 %all-gather.10.cloned.1.call-start = ((), (), s32[]{:S(2)}) async-start(), calls=%async_computation.15 | async-start | bytes 5308416 | tf_op jit(solution)/shard_map/all_gather | solution.py:572
  48.9 28.4 %collective-permute-start = (bf16[1,192,1536]{2,1,0:T(8,128)(2,1)}, bf16[1,192,1536]{2,1,0:T(8,128)(2,1)}, u32[]{:S(2)}, u32[]{:S(2)}) collective-permute-start(bf16[1,192,1536]{2,1,0:T(8,128)(2,1)} %get-tuple-element.131), channel_id=1, source_target_pairs={{0,2},{1,3},{2,0},{3,1},{4,6},{5,7},{6,4},{7,5},{8,10},{9,11},{10,... | collective-permute-start | bytes 1769480 | tf_op jit(solution)/shard_map/modulation/ppermute | solution.py:25
  83.3 178.0 %all-gather.12.cloned.1.call-start = ((), (), s32[]{:S(2)}) async-start(), calls=%async_computation.16 | async-start | bytes 21233664 | tf_op jit(solution)/shard_map/attention/all_gather | solution.py:572
  95.8 25.8 %collective-permute-start.4 = (bf16[2,148,1536]{2,0,1:T(2,128)(2,1)}, bf16[2,148,1536]{2,0,1:T(2,128)(2,1)}, u32[]{:S(2)}, u32[]{:S(2)}) collective-permute-start(bf16[2,148,1536]{2,0,1:T(2,128)(2,1)} %copy.89), channel_id=1, source_target_pairs={{0,1},{1,0},{2,3},{3,2},{4,5},{5,4},{6,7},{7,6},{8,9},{9,8},{10,11... | collective-permute-start | bytes 2727944 | tf_op jit(solution)/shard_map/attention/ppermute | solution.py:25
  155.6 51.8 %all-to-all-start.1 = ((bf16[8,148,1152]{2,1,0:T(8,128)(2,1)}), bf16[8,148,1152]{2,1,0:T(8,128)(2,1)}, u32[]{:S(2)}, u32[]{:S(2)}) async-start(bf16[8,148,1152]{2,1,0:T(8,128)(2,1)} %bitcast.1164), calls=%async_computation.1 | async-start | bytes 5603328 | tf_op jit(solution)/shard_map/attention/all_to_all | solution.py:353
  160.5 79.8 %collective-permute-start.8 = (bf16[3,192,1536]{2,1,0:T(8,128)(2,1)}, bf16[3,192,1536]{2,1,0:T(8,128)(2,1)}, u32[]{:S(2)}, u32[]{:S(2)}) collective-permute-start(bf16[3,192,1536]{2,1,0:T(8,128)(2,1)} %pad_maximum_fusion.11), channel_id=1, source_target_pairs={{0,2},{1,3},{2,0},{3,1},{4,6},{5,7},{6,4},{7,5},{8,10},{9,11},{10,... | collective-permute-start | bytes 5308424 | tf_op jit(solution)/shard_map/attention/ppermute | solution.py:25
  230.6 25.5 %all-to-all-start.2 = ((bf16[8,148,384]{2,1,0:T(8,128)(2,1)}), bf16[8,148,384]{2,1,0:T(8,128)(2,1)}, u32[]{:S(2)}, u32[]{:S(2)}) async-start(bf16[8,148,384]{2,1,0:T(8,128)(2,1)} %reshape.399), calls=%async_computation.2 | async-start | bytes 1867776 | tf_op jit(solution)/shard_map/attention/all_to_all | solution.py:357
  234.8 94.9 %all-gather.14.cloned.1.call-start = ((), (), s32[]{:S(2)}) async-start(), calls=%async_computation.17 | async-start | bytes 10616832 | tf_op jit(solution)/shard_map/attention/all_gather | solution.py:572
  263.7 173.2 %all-gather.16.cloned.1.call-start = ((), (), s32[]{:S(2)}) async-start(), calls=%async_computation.18 | async-start | bytes 15925248 | tf_op jit(solution)/shard_map/mlp/all_gather | solution.py:572
  274.3 25.7 %collective-permute-start.10 = (bf16[2,148,1536]{2,0,1:T(2,128)(2,1)S(1)}, bf16[2,148,1536]{2,0,1:T(2,128)(2,1)S(1)}, u32[]{:S(2)}, u32[]{:S(2)}) collective-permute-start(bf16[2,148,1536]{2,0,1:T(2,128)(2,1)S(1)} %copy.98), channel_id=1, source_target_pairs={{0,1},{1,0},{2,3},{3,2},{4,5},{5,4},{6,7},{7,6},{8,9},{9,8},{10,11... | collective-permute-start | bytes 2727944 | tf_op jit(solution)/shard_map/attention/ppermute | solution.py:25
  332.6 235.7 %all-gather.18.cloned.1.call-start = ((), (), s32[]{:S(2)}) async-start(), calls=%async_computation.19 | async-start | bytes 21233664 | tf_op jit(solution)/shard_map/attention/all_gather | solution.py:572
  366.1 28.4 %collective-permute-start.16 = (bf16[2,148,1536]{2,0,1:T(2,128)(2,1)S(1)}, bf16[2,148,1536]{2,0,1:T(2,128)(2,1)S(1)}, u32[]{:S(2)}, u32[]{:S(2)}) collective-permute-start(bf16[2,148,1536]{2,0,1:T(2,128)(2,1)S(1)} %copy.105), channel_id=1, source_target_pairs={{0,1},{1,0},{2,3},{3,2},{4,5},{5,4},{6,7},{7,6},{8,9},{9,8},{10,11... | collective-permute-start | bytes 2727944 | tf_op jit(solution)/shard_map/mlp/ppermute | solution.py:25
  401.9 24.7 %collective-permute-start.19 = (bf16[2,148,1536]{2,0,1:T(2,128)(2,1)}, bf16[2,148,1536]{2,0,1:T(2,128)(2,1)}, u32[]{:S(2)}, u32[]{:S(2)}) collective-permute-start(bf16[2,148,1536]{2,0,1:T(2,128)(2,1)} %copy.110), channel_id=1, source_target_pairs={{0,1},{1,0},{2,3},{3,2},{4,5},{5,4},{6,7},{7,6},{8,9},{9,8},{10,11... | collective-permute-start | bytes 2727944 | tf_op jit(solution)/shard_map/attention/ppermute | solution.py:25
  455.7 58.2 %all-to-all-start.3 = ((bf16[8,148,1152]{2,1,0:T(8,128)(2,1)}), bf16[8,148,1152]{2,1,0:T(8,128)(2,1)}, u32[]{:S(2)}, u32[]{:S(2)}) async-start(bf16[8,148,1152]{2,1,0:T(8,128)(2,1)} %bitcast.1163), calls=%async_computation.3 | async-start | bytes 5603328 | tf_op jit(solution)/shard_map/attention/all_to_all | solution.py:353
  467.8 88.7 %collective-permute-start.23 = (bf16[2,192,1536]{2,1,0:T(8,128)(2,1)}, bf16[2,192,1536]{2,1,0:T(8,128)(2,1)}, u32[]{:S(2)}, u32[]{:S(2)}) collective-permute-start(bf16[2,192,1536]{2,1,0:T(8,128)(2,1)} %pad_maximum_fusion.17), channel_id=1, source_target_pairs={{0,2},{1,3},{2,0},{3,1},{4,6},{5,7},{6,4},{7,5},{8,10},{9,11},{10,... | collective-permute-start | bytes 3538952 | tf_op jit(solution)/shard_map/attention/ppermute | solution.py:25
  470.8 74.5 %collective-permute-start.24 = (bf16[2,148,1536]{2,0,1:T(2,128)(2,1)}, bf16[2,148,1536]{2,0,1:T(2,128)(2,1)}, u32[]{:S(2)}, u32[]{:S(2)}) collective-permute-start(bf16[2,148,1536]{2,0,1:T(2,128)(2,1)} %copy.114), channel_id=1, source_target_pairs={{0,1},{1,0},{2,3},{3,2},{4,5},{5,4},{6,7},{7,6},{8,9},{9,8},{10,11... | collective-permute-start | bytes 2727944 | tf_op jit(solution)/shard_map/attention/ppermute | solution.py:25
  537.1 26.0 %all-to-all-start.4 = ((bf16[8,148,384]{2,1,0:T(8,128)(2,1)}), bf16[8,148,384]{2,1,0:T(8,128)(2,1)}, u32[]{:S(2)}, u32[]{:S(2)}) async-start(bf16[8,148,384]{2,1,0:T(8,128)(2,1)} %reshape.406), calls=%async_computation.4 | async-start | bytes 1867776 | tf_op jit(solution)/shard_map/attention/all_to_all | solution.py:357
  541.4 125.0 %all-gather.20.cloned.1.call-start = ((), (), s32[]{:S(2)}) async-start(), calls=%async_computation.20 | async-start | bytes 10616832 | tf_op jit(solution)/shard_map/attention/all_gather | solution.py:572
  568.3 335.8 %reduce-scatter.5.cloned.1.call-start = ((), (), s32[]{:S(2)}) async-start(), calls=%async_computation.21 | async-start | bytes 31850496 | tf_op jit(solution)/shard_map/mlp_grad/reduce_scatter | solution.py:412
  579.6 25.5 %collective-permute-start.28 = (bf16[2,148,1536]{2,0,1:T(2,128)(2,1)S(1)}, bf16[2,148,1536]{2,0,1:T(2,128)(2,1)S(1)}, u32[]{:S(2)}, u32[]{:S(2)}) collective-permute-start(bf16[2,148,1536]{2,0,1:T(2,128)(2,1)S(1)} %copy.121), channel_id=1, source_target_pairs={{0,1},{1,0},{2,3},{3,2},{4,5},{5,4},{6,7},{7,6},{8,9},{9,8},{10,11... | collective-permute-start | bytes 2727944 | tf_op jit(solution)/shard_map/attention/ppermute | solution.py:25
  608.1 26.6 %collective-permute-start.32 = (bf16[2,20,1536]{2,1,0:T(8,128)(2,1)S(1)}, bf16[2,20,1536]{2,1,0:T(8,128)(2,1)S(1)}, u32[]{:S(2)}, u32[]{:S(2)}) collective-permute-start(bf16[2,20,1536]{2,1,0:T(8,128)(2,1)S(1)} %add_convert_fusion.3), channel_id=1, source_target_pairs={{0,2},{1,3},{2,0},{3,1},{4,6},{5,7},{6,4},{7,5},{8,10},{9,11},{10,... | collective-permute-start | bytes 368648 | tf_op jit(solution)/shard_map/mlp/ppermute | solution.py:25
  608.8 25.9 %collective-permute-start.33 = (bf16[2,20,1536]{2,1,0:T(8,128)(2,1)S(1)}, bf16[2,20,1536]{2,1,0:T(8,128)(2,1)S(1)}, u32[]{:S(2)}, u32[]{:S(2)}) collective-permute-start(bf16[2,20,1536]{2,1,0:T(8,128)(2,1)S(1)} %add_convert_fusion.3), channel_id=1, source_target_pairs={{0,3},{1,2},{2,1},{3,0},{4,7},{5,6},{6,5},{7,4},{8,11},{9,10},{10,... | collective-permute-start | bytes 368648 | tf_op jit(solution)/shard_map/mlp/ppermute | solution.py:25
  641.1 51.1 %collective-permute-start.35 = (bf16[2,20,1536]{2,1,0:T(8,128)(2,1)}, bf16[2,20,1536]{2,1,0:T(8,128)(2,1)}, u32[]{:S(2)}, u32[]{:S(2)}) collective-permute-start(bf16[2,20,1536]{2,1,0:T(8,128)(2,1)} %get-tuple-element.418), channel_id=1, source_target_pairs={{0,2},{1,3},{2,0},{3,1},{4,6},{5,7},{6,4},{7,5},{8,10},{9,11},{10,... | collective-permute-start | bytes 368648 | tf_op jit(solution)/shard_map/mlp_grad/ppermute | solution.py:25
  641.1 51.1 %collective-permute-start.36 = (bf16[2,20,1536]{2,1,0:T(8,128)(2,1)}, bf16[2,20,1536]{2,1,0:T(8,128)(2,1)}, u32[]{:S(2)}, u32[]{:S(2)}) collective-permute-start(bf16[2,20,1536]{2,1,0:T(8,128)(2,1)} %get-tuple-element.417), channel_id=1, source_target_pairs={{0,3},{1,2},{2,1},{3,0},{4,7},{5,6},{6,5},{7,4},{8,11},{9,10},{10,... | collective-permute-start | bytes 368648 | tf_op jit(solution)/shard_map/mlp_grad/ppermute | solution.py:25
  750.7 32.6 %all-to-all-start.5 = ((bf16[8,148,384]{2,1,0:T(8,128)(2,1)}), bf16[8,148,384]{2,1,0:T(8,128)(2,1)}, u32[]{:S(2)}, u32[]{:S(2)}) async-start(bf16[8,148,384]{2,1,0:T(8,128)(2,1)} %bitcast.1179), calls=%async_computation.5 | async-start | bytes 1867776 | tf_op jit(solution)/shard_map/attention_grad/all_to_all | solution.py:511
  821.7 50.1 %all-to-all-start.6 = ((bf16[8,148,1152]{2,1,0:T(8,128)(2,1)}), bf16[8,148,1152]{2,1,0:T(8,128)(2,1)}, u32[]{:S(2)}, u32[]{:S(2)}) async-start(bf16[8,148,1152]{2,1,0:T(8,128)(2,1)} %reshape.412), calls=%async_computation.6 | async-start | bytes 5603328 | tf_op jit(solution)/shard_map/attention_grad/all_to_all | solution.py:522
  826.1 319.5 %reduce-scatter.7.cloned.1.call-start = ((), (), s32[]{:S(2)}) async-start(), calls=%async_computation.22 | async-start | bytes 15925248 | tf_op jit(solution)/shard_map/attention_grad/reduce_scatter | solution.py:412
  828.4 28.8 %collective-permute-start.41 = (bf16[2,148,1536]{2,0,1:T(2,128)(2,1)S(1)}, bf16[2,148,1536]{2,0,1:T(2,128)(2,1)S(1)}, u32[]{:S(2)}, u32[]{:S(2)}) collective-permute-start(bf16[2,148,1536]{2,0,1:T(2,128)(2,1)S(1)} %copy.138), channel_id=1, source_target_pairs={{0,1},{1,0},{2,3},{3,2},{4,5},{5,4},{6,7},{7,6},{8,9},{9,8},{10,11... | collective-permute-start | bytes 2727944 | tf_op jit(solution)/shard_map/attention_grad/ppermute | solution.py:25
  904.1 324.7 %reduce-scatter.9.cloned.1.call-start = ((), (), s32[]{:S(2)}) async-start(), calls=%async_computation.23 | async-start | bytes 31850496 | tf_op jit(solution)/shard_map/mlp_grad/reduce_scatter | solution.py:412
  908.8 29.3 %collective-permute-start.45 = (bf16[2,148,1536]{2,0,1:T(2,128)(2,1)S(1)}, bf16[2,148,1536]{2,0,1:T(2,128)(2,1)S(1)}, u32[]{:S(2)}, u32[]{:S(2)}) collective-permute-start(bf16[2,148,1536]{2,0,1:T(2,128)(2,1)S(1)} %copy.145), channel_id=1, source_target_pairs={{0,1},{1,0},{2,3},{3,2},{4,5},{5,4},{6,7},{7,6},{8,9},{9,8},{10,11... | collective-permute-start | bytes 2727944 | tf_op jit(solution)/shard_map/attention_grad/ppermute | solution.py:25
  913.2 24.9 %collective-permute-start.47 = (bf16[2,20,1536]{2,1,0:T(8,128)(2,1)S(1)}, bf16[2,20,1536]{2,1,0:T(8,128)(2,1)S(1)}, u32[]{:S(2)}, u32[]{:S(2)}) collective-permute-start(bf16[2,20,1536]{2,1,0:T(8,128)(2,1)S(1)} %get-tuple-element.411), channel_id=1, source_target_pairs={{0,3},{1,2},{2,1},{3,0},{4,7},{5,6},{6,5},{7,4},{8,11},{9,10},{10,... | collective-permute-start | bytes 368648 | tf_op jit(solution)/shard_map/attention_grad/ppermute | solution.py:25
  946.3 29.5 %collective-permute-start.49 = (bf16[2,20,1536]{2,1,0:T(8,128)(2,1)S(1)}, bf16[2,20,1536]{2,1,0:T(8,128)(2,1)S(1)}, u32[]{:S(2)}, u32[]{:S(2)}) collective-permute-start(bf16[2,20,1536]{2,1,0:T(8,128)(2,1)S(1)} %multiply_convert_fusion.14), channel_id=1, source_target_pairs={{0,2},{1,3},{2,0},{3,1},{4,6},{5,7},{6,4},{7,5},{8,10},{9,11},{10,... | collective-permute-start | bytes 368648 | tf_op jit(solution)/shard_map/mlp_grad/ppermute | solution.py:25
  946.3 29.4 %collective-permute-start.50 = (bf16[2,20,1536]{2,1,0:T(8,128)(2,1)S(1)}, bf16[2,20,1536]{2,1,0:T(8,128)(2,1)S(1)}, u32[]{:S(2)}, u32[]{:S(2)}) collective-permute-start(bf16[2,20,1536]{2,1,0:T(8,128)(2,1)S(1)} %multiply_convert_fusion.14), channel_id=1, source_target_pairs={{0,3},{1,2},{2,1},{3,0},{4,7},{5,6},{6,5},{7,4},{8,11},{9,10},{10,... | collective-permute-start | bytes 368648 | tf_op jit(solution)/shard_map/mlp_grad/ppermute | solution.py:25
  948.9 26.2 %collective-permute-start.48 = (bf16[2,148,1536]{2,0,1:T(2,128)(2,1)S(1)}, bf16[2,148,1536]{2,0,1:T(2,128)(2,1)S(1)}, u32[]{:S(2)}, u32[]{:S(2)}) collective-permute-start(bf16[2,148,1536]{2,0,1:T(2,128)(2,1)S(1)} %copy.148), channel_id=1, source_target_pairs={{0,1},{1,0},{2,3},{3,2},{4,5},{5,4},{6,7},{7,6},{8,9},{9,8},{10,11... | collective-permute-start | bytes 2727944 | tf_op jit(solution)/shard_map/mlp_grad/ppermute | solution.py:25
  992.2 29.9 %collective-permute-start.51 = (bf16[2,148,1536]{2,0,1:T(2,128)(2,1)}, bf16[2,148,1536]{2,0,1:T(2,128)(2,1)}, u32[]{:S(2)}, u32[]{:S(2)}) collective-permute-start(bf16[2,148,1536]{2,0,1:T(2,128)(2,1)} %copy.151), channel_id=1, source_target_pairs={{0,1},{1,0},{2,3},{3,2},{4,5},{5,4},{6,7},{7,6},{8,9},{9,8},{10,11... | collective-permute-start | bytes 2727944 | tf_op jit(solution)/shard_map/mlp_grad/ppermute | solution.py:25
  992.2 29.9 %collective-permute-start.52 = (bf16[2,20,1536]{2,1,0:T(8,128)(2,1)}, bf16[2,20,1536]{2,1,0:T(8,128)(2,1)}, u32[]{:S(2)}, u32[]{:S(2)}) collective-permute-start(bf16[2,20,1536]{2,1,0:T(8,128)(2,1)} %get-tuple-element.409), channel_id=1, source_target_pairs={{0,2},{1,3},{2,0},{3,1},{4,6},{5,7},{6,4},{7,5},{8,10},{9,11},{10,... | collective-permute-start | bytes 368648 | tf_op jit(solution)/shard_map/mlp_grad/ppermute | solution.py:25
  994.3 27.7 %collective-permute-start.53 = (bf16[2,20,1536]{2,1,0:T(8,128)(2,1)}, bf16[2,20,1536]{2,1,0:T(8,128)(2,1)}, u32[]{:S(2)}, u32[]{:S(2)}) collective-permute-start(bf16[2,20,1536]{2,1,0:T(8,128)(2,1)} %get-tuple-element.408), channel_id=1, source_target_pairs={{0,3},{1,2},{2,1},{3,0},{4,7},{5,6},{6,5},{7,4},{8,11},{9,10},{10,... | collective-permute-start | bytes 368648 | tf_op jit(solution)/shard_map/mlp_grad/ppermute | solution.py:25
  1041.4 25.5 %collective-permute-start.54 = (bf16[2,148,1536]{2,0,1:T(2,128)(2,1)S(1)}, bf16[2,148,1536]{2,0,1:T(2,128)(2,1)S(1)}, u32[]{:S(2)}, u32[]{:S(2)}) collective-permute-start(bf16[2,148,1536]{2,0,1:T(2,128)(2,1)S(1)} %copy.160), channel_id=1, source_target_pairs={{0,1},{1,0},{2,3},{3,2},{4,5},{5,4},{6,7},{7,6},{8,9},{9,8},{10,11... | collective-permute-start | bytes 2727944 | tf_op jit(solution)/shard_map/attention_grad/ppermute | solution.py:25
  1076.2 33.5 %all-to-all-start.7 = ((bf16[8,148,384]{2,1,0:T(8,128)(2,1)}), bf16[8,148,384]{2,1,0:T(8,128)(2,1)}, u32[]{:S(2)}, u32[]{:S(2)}) async-start(bf16[8,148,384]{2,1,0:T(8,128)(2,1)} %bitcast.1180), calls=%async_computation.8 | async-start | bytes 1867776 | tf_op jit(solution)/shard_map/attention_grad/all_to_all | solution.py:511
  1115.7 50.6 %collective-permute-start.58 = (bf16[192,3072]{1,0:T(8,128)(2,1)}, bf16[192,3072]{1,0:T(8,128)(2,1)}, u32[]{:S(2)}, u32[]{:S(2)}) collective-permute-start(bf16[192,3072]{1,0:T(8,128)(2,1)} %get-tuple-element.349), channel_id=1, source_target_pairs={{0,2},{1,3},{2,0},{3,1},{4,6},{5,7},{6,4},{7,5},{8,10},{9,11},{10,... | collective-permute-start | bytes 3538952 | tf_op jit(solution)/shard_map/attention_grad/ppermute | solution.py:25
  1149.9 50.6 %all-to-all-start.8 = ((bf16[8,148,1152]{2,1,0:T(8,128)(2,1)}), bf16[8,148,1152]{2,1,0:T(8,128)(2,1)}, u32[]{:S(2)}, u32[]{:S(2)}) async-start(bf16[8,148,1152]{2,1,0:T(8,128)(2,1)} %reshape.422), calls=%async_computation.10 | async-start | bytes 5603328 | tf_op jit(solution)/shard_map/attention_grad/all_to_all | solution.py:522
  1154.3 195.6 %reduce-scatter.11.cloned.1.call-start = ((), (), s32[]{:S(2)}) async-start(), calls=%async_computation.24 | async-start | bytes 15925248 | tf_op jit(solution)/shard_map/attention_grad/reduce_scatter | solution.py:412
  1169.7 28.0 %collective-permute-start.59 = (bf16[192,1536]{1,0:T(8,128)(2,1)S(1)}, bf16[192,1536]{1,0:T(8,128)(2,1)}, u32[]{:S(2)}, u32[]{:S(2)}) collective-permute-start(bf16[192,1536]{1,0:T(8,128)(2,1)S(1)} %slice.960), channel_id=1, source_target_pairs={{0,2},{1,3},{2,0},{3,1},{4,6},{5,7},{6,4},{7,5},{8,10},{9,11},{10,... | collective-permute-start | bytes 1769480 | tf_op jit(solution)/shard_map/attention_grad/ppermute | solution.py:25
  1245.7 30.4 %collective-permute-start.61 = (bf16[2,148,1536]{2,0,1:T(2,128)(2,1)S(1)}, bf16[2,148,1536]{2,0,1:T(2,128)(2,1)S(1)}, u32[]{:S(2)}, u32[]{:S(2)}) collective-permute-start(bf16[2,148,1536]{2,0,1:T(2,128)(2,1)S(1)} %copy.166), channel_id=1, source_target_pairs={{0,1},{1,0},{2,3},{3,2},{4,5},{5,4},{6,7},{7,6},{8,9},{9,8},{10,11... | collective-permute-start | bytes 2727944 | tf_op jit(solution)/shard_map/attention_grad/ppermute | solution.py:25
  1251.7 24.5 %collective-permute-start.63 = (bf16[2,20,1536]{2,1,0:T(8,128)(2,1)S(1)}, bf16[2,20,1536]{2,1,0:T(8,128)(2,1)S(1)}, u32[]{:S(2)}, u32[]{:S(2)}) collective-permute-start(bf16[2,20,1536]{2,1,0:T(8,128)(2,1)S(1)} %get-tuple-element.405), channel_id=1, source_target_pairs={{0,3},{1,2},{2,1},{3,0},{4,7},{5,6},{6,5},{7,4},{8,11},{9,10},{10,... | collective-permute-start | bytes 368648 | tf_op jit(solution)/shard_map/attention_grad/ppermute | solution.py:25
  1295.2 54.7 %collective-permute-start.69 = (bf16[192,3072]{1,0:T(8,128)(2,1)}, bf16[192,3072]{1,0:T(8,128)(2,1)}, u32[]{:S(2)}, u32[]{:S(2)}) collective-permute-start(bf16[192,3072]{1,0:T(8,128)(2,1)} %slice.978), channel_id=1, source_target_pairs={{0,2},{1,3},{2,0},{3,1},{4,6},{5,7},{6,4},{7,5},{8,10},{9,11},{10,... | collective-permute-start | bytes 3538952 | tf_op jit(solution)/shard_map/modulation_grad/ppermute | solution.py:25
  1354.8 27.8 %collective-permute-start.70 = (bf16[192,1536]{1,0:T(8,128)(2,1)S(1)}, bf16[192,1536]{1,0:T(8,128)(2,1)S(1)}, u32[]{:S(2)}, u32[]{:S(2)}) collective-permute-start(bf16[192,1536]{1,0:T(8,128)(2,1)S(1)} %slice.980), channel_id=1, source_target_pairs={{0,2},{1,3},{2,0},{3,1},{4,6},{5,7},{6,4},{7,5},{8,10},{9,11},{10,... | collective-permute-start | bytes 1769480 | tf_op jit(solution)/shard_map/modulation_grad/ppermute | solution.py:25
  (416 other events, 3489.1 us)
Sparse Core Ops, SparseCore 0:
  15.0 68.2 all-gather.7
  85.2 39.1 all-gather.9
  127.8 127.9 all-gather.11
  263.8 57.9 all-gather.13
  332.7 80.8 all-gather.15
  428.6 134.1 all-gather.17
  568.4 57.9 all-gather.19
  696.7 206.4 reduce-scatter.4
  906.7 100.7 reduce-scatter.6
  1022.2 206.5 reduce-scatter.8
  1232.4 106.6 reduce-scatter.10
